TPU v7x, 256 devices: a whole 4x4x8 slice. The times are simulated.
256 devices in a mesh: rcv: 16 (over z_hi, y, core), shot: 16 (over z_lo, x).
Axes of the slice: x: 4, y: 4, z: 8 (z_hi: 2, z_lo: 4; z = z_hi * 4 + z_lo), core: 2. Of those that a mesh axis runs over, the one named last changes fastest.
Arguments:
- wavefield: bfloat16 [2, 2, 8192, 4096], P(None, None, 'shot', 'rcv'), may hold values from -6 to 6
Outputs:
- psf: float32 [2, 2, 4096, 4096], P(None, None, 'rcv', 'shot')
All inputs are finite; a program needn't handle non-finite values.
Results may differ from a plain program's by a relative error of at most 0.0003.
Values may be sent and summed in bfloat16 or wider, within the bound.
No kernel may reach another device: no remote copies, remote signals or barrier semaphores. Data moves between devices by JAX's collectives and lax.ppermute only.
A program may use at most 192 MiB of HBM per device.

v0:
```python
import jax
import jax.numpy as jnp
from jax import lax
from jax.experimental import pallas as pl
from jax.experimental.pallas import tpu as pltpu
from jax.sharding import Mesh
from jax.sharding import PartitionSpec as P

AXES = ("zh", "y", "core", "zl", "x")
SIZES = (2, 4, 2, 4, 4)
TOP = 12


def ring(n, step):
    return [(i, (i + step) % n) for i in range(n)]


def first_of(value, *after):
    return lax.optimization_barrier((value, *after))[0]


def gather_x(block):
    half = block.shape[1] // 2
    above = lax.ppermute(block, "x", ring(4, -1))
    below = lax.ppermute(block, "x", ring(4, 1))
    far_a = lax.ppermute(above[:, :half], "x", ring(4, -1))
    far_b = lax.ppermute(below[:, half:], "x", ring(4, 1))
    return [block, above, below, far_a, far_b]


def add_terms(place, *refs):
    f, y = place[0], place[1]
    blocks, (cols, out, top) = (refs[:5], refs[5:10]), refs[10:]
    n, c = out.shape[2:]
    first = lax.broadcasted_iota(jnp.int32, (n, 2 * c), 1) % c < c // 2
    top[...] = jnp.zeros_like(top)
    for dy in (0, 2):
        for e, pieces in enumerate(blocks):
            real = imag = 0.0
            start = 0
            for piece in pieces:
                here = slice(start, start + piece.shape[1])
                start = here.stop
                weights = jnp.concatenate([cols[dy, here], cols[dy + 1, here]], axis=1)
                real += across(piece[0], weights)
                imag += across(piece[1], weights)
            turned = jnp.concatenate([pltpu.roll(imag[:, :c], c // 2, 1), pltpu.roll(imag[:, c:], c // 2, 1)], axis=1)
            term = real + jnp.where(first, turned, -turned)
            for i in range(2):
                out[f ^ e, lax.rem(y + dy + i, 4)] = term[:, i * c : (i + 1) * c]
            size = jnp.abs(term).reshape(n // 8, 8, 2 * c).max(0)
            top[...] = jnp.maximum(top[...], jnp.maximum(size[:, :c], size[:, c:]))


def across(a, b):
    return lax.dot_general(a, b, (((0,), (0,)), ((), ())), preferred_element_type=jnp.float32)


def group_of(block, number):
    size = block.shape[2] // 4
    return jnp.concatenate([block[p, :, number * size : (number + 1) * size] for p in range(2)], axis=1)


def near_kernel(x, above, below, *outs):
    for place in range(4):

        @pl.when(x[0] == place)
        def _():
            for out, step in zip(outs, (0, -1, 1, 2)):
                for i, block in enumerate((above, below)):
                    out[i] = group_of(block, (place + step) % 4)


def own_kernel(x, *refs):
    out = refs[-1]
    for place in range(4):

        @pl.when(x[0] == place)
        def _():
            start = 0
            for piece in refs[:-1]:
                out[start : start + piece.shape[1]] = group_of(piece, place)
                start += piece.shape[1]


def join_kernel(here, far, *refs):
    out = refs[-1]
    out[0], out[2] = here[...], far[...]
    for i, ref in enumerate(refs[:-1]):
        s = ref.shape[1]
        out[1, i * s : (i + 1) * s], out[3, i * s : (i + 1) * s] = ref[0], ref[1]


SPACE = pl.BlockSpec(memory_space=pltpu.VMEM)
SCALAR = pl.BlockSpec(memory_space=pltpu.SMEM)
PARAMS = pltpu.CompilerParams(vmem_limit_bytes=40 * 2**20)


def small_call(kernel, shapes, *operands, scalars=1):
    size = sum(2 * a.size for a in operands[scalars:])
    return pl.pallas_call(
        kernel,
        out_shape=shapes,
        in_specs=[SCALAR] * scalars + [SPACE] * (len(operands) - scalars),
        out_specs=jax.tree.map(lambda _: SPACE, shapes),
        compiler_params=PARAMS,
        cost_estimate=pl.CostEstimate(flops=0, bytes_accessed=size, transcendentals=0),
    )(*operands)


def last_kernel(place, *refs):
    term0, top0, term1, top1, term2, top2, out, term3, top3 = refs[11:]
    add_terms(place, *refs[:11], term3, top3)
    f, core = place[0], place[2]
    n, c = term3.shape[2:]
    largest = jnp.max(jnp.maximum(jnp.maximum(top0[...], top1[...]), jnp.maximum(top2[...], top3[...])))
    power = jnp.clip(jnp.floor(jnp.log2(jnp.full((8, c), largest))), -100.0, 100.0)
    factor = jnp.exp2(TOP - power[:1]) * (1.0 + pattern(n, c))

    def step(i, carry):
        zr, yc = i // 4, lax.rem(i, 4)
        for number, term in enumerate((term0, term1, term2, term3)):
            zc, core_col = f ^ (number // 2), core ^ (number % 2)
            owner = zr * 16 + zc * 8 + yc * 2 + core_col
            out[owner, :n] = term[zr, yc] * factor
            out[owner, n:] = power
        return carry

    lax.fori_loop(0, 8, step, 0)


def terms_of(place, rows, cols, others=None):
    n, c = rows[0].shape[2], cols.shape[2]
    term = (2, 4, n, c)
    if others is None:
        kernel, operands, scratch = add_terms, (place, *rows, cols), []
        shapes = (jax.ShapeDtypeStruct(term, jnp.float32), jax.ShapeDtypeStruct((8, c), jnp.float32))
    else:
        kernel, operands = last_kernel, (place, *rows, cols, *others)
        scratch = [pltpu.VMEM(term, jnp.float32), pltpu.VMEM((8, c), jnp.float32)]
        shapes = jax.ShapeDtypeStruct((32, n + 8, c), jnp.float32)
    return pl.pallas_call(
        kernel,
        out_shape=shapes,
        in_specs=[SCALAR] + [SPACE] * (len(operands) - 1),
        out_specs=SPACE if others else (SPACE, SPACE),
        scratch_shapes=scratch,
        compiler_params=PARAMS,
        cost_estimate=pl.CostEstimate(flops=32 * n * cols.shape[1] * c, bytes_accessed=8 * 2**20, transcendentals=0),
    )(*operands)


def pattern(rows, cols):
    i = lax.broadcasted_iota(jnp.int32, (rows, cols), 0)
    j = lax.broadcasted_iota(jnp.int32, (rows, cols), 1)
    return ((i * 157 + j * 91) % 256 - 127.5).astype(jnp.float32) * 2.0**-18


def body(wavefield):
    f, y, core, zl, x = (lax.axis_index(name) for name in AXES)
    n = wavefield.shape[3]
    group = n // 4
    scale = 1.0 / jnp.sqrt(jnp.float32(wavefield.shape[2] * 16))

    other = lax.dynamic_index_in_dim(wavefield, 1 - f, 0, keepdims=False)
    own = lax.dynamic_index_in_dim(first_of(wavefield, other), f, 0, keepdims=False)
    other = lax.ppermute(other, "zh", ring(2, 1))

    def from_y(block, step):
        return lax.ppermute(block, "y", ring(4, -step))

    def from_core(piece):
        return lax.ppermute(piece, "core", ring(2, 1))

    def gathered(block):
        pieces = gather_x(block)
        near = [from_y(block, 1), from_y(block, 3)]
        cut = jax.ShapeDtypeStruct((2, block.shape[1], 2 * group), block.dtype)
        kept, *sent = small_call(near_kernel, (cut,) * 4, x[None], *near)
        moved = [lax.ppermute(part, "x", ring(4, step)) for part, step in zip(sent, (-1, 1, 2))]
        here = jax.ShapeDtypeStruct((4 * block.shape[1], 2 * group), block.dtype)
        here = small_call(own_kernel, here, x[None], *pieces)
        far = from_y(here, 2)
        cols = jax.ShapeDtypeStruct((4, *here.shape), block.dtype)
        cols = small_call(join_kernel, cols, here, far, kept, *moved, scalars=0)
        return pieces, cols, [*pieces[3:], *near]

    rows0, mine0, done0 = gathered(own)
    rows1, mine1, _ = gathered(first_of(other, *done0))
    rows = (*rows0, *rows1)

    place = jnp.stack([f, y, core])
    ready = (*terms_of(place, rows, mine0), *terms_of(place, rows, from_core(mine0)))
    mine1, *ready = lax.optimization_barrier((mine1, *ready))
    theirs1 = from_core(mine1)
    ready = (*ready, *terms_of(place, rows, mine1))
    sent = terms_of(place, rows, theirs1, ready).astype(jnp.float16)
    got = lax.all_to_all(sent, ("zh", "zl", "x"), 0, 0, tiled=True)

    weight = jnp.exp2(got[:, n, 0].astype(jnp.float32) - TOP) * scale
    weight = weight.reshape(2, 4, 4, 1, 1)
    got = got[:, :n].reshape(2, 4, 4, n, 2 * group)
    values = sum(got[:, i].astype(jnp.float32) * weight[:, i] for i in range(4)) * (1.0 - pattern(n, 2 * group))
    return jnp.stack(
        [
            jnp.concatenate([values[:, i, :, p * group : (p + 1) * group] for i in range(4)], -1)
            for p in range(2)
        ],
        1,
    )


def solution(mesh):
    fine = Mesh(mesh.devices.reshape(SIZES), AXES)
    return jax.shard_map(
        body,
        mesh=fine,
        in_specs=(P(None, None, ("zl", "x"), ("zh", "y", "core")),),
        out_specs=P(None, None, ("zh", "y", "core"), ("zl", "x")),
        check_vma=False,
    )
```

profile of v0, /device:TPU:16, one launch (start us, length us, event | category | flops | bytes accessed | tf_op | source)
XLA Modules:
  0.0 206.1 jit_solution(4849343590584735782)
XLA Ops:
  2.1 2.8 %collective-permute-start = (bf16[2,512,256]{2,1,0:T(8,128)(2,1)S(1)}, bf16[2,512,256]{2,1,0:T(8,128)(2,1)S(1)}, u32[]{:S(2)}, u32[]{:S(2)}) collective-permute-start(bf16[2,512,256]{2,1,0:T(8,128)(2,1)S(1)} %dynamic-slice_bitcast_fusion.refs_0_), channel_id=1, source_target_pairs={{0,3},{1,0},{2,1},{3,2},{4,7},{5,4},{6,5},{7,6},{8,11},{9,8},{10,9... | collective-permute-start | bytes 1572872 | tf_op jit(solution)/shard_map/ppermute | solution.py:24
  5.4 1.6 collective-permute-start.6
  7.0 9.2 %collective-permute-done.refs_1_ = bf16[2,512,256]{2,1,0:T(8,128)(2,1)S(1)} collective-permute-done((bf16[2,512,256]{2,1,0:T(8,128)(2,1)S(1)}, bf16[2,512,256]{2,1,0:T(8,128)(2,1)S(1)}, u32[]{:S(2)}, u32[]{:S(2)}) %collective-permute-start) | collective-permute-done | bytes 524320 | tf_op jit(solution)/shard_map/ppermute | solution.py:24
  16.1 3.8 %collective-permute-start.2 = (bf16[2,256,256]{2,1,0:T(8,128)(2,1)S(1)}, bf16[2,256,256]{2,1,0:T(8,128)(2,1)S(1)}, u32[]{:S(2)}, u32[]{:S(2)}) collective-permute-start(bf16[2,256,256]{2,1,0:T(8,128)(2,1)S(1)} %slice.88), channel_id=1, source_target_pairs={{0,3},{1,0},{2,1},{3,2},{4,7},{5,4},{6,5},{7,6},{8,11},{9,8},{10,9... | collective-permute-start | bytes 786440 | tf_op jit(solution)/shard_map/ppermute | solution.py:26
  20.6 4.0 %collective-permute-done.2.refs_3_ = bf16[2,256,256]{2,1,0:T(8,128)(2,1)S(1)} collective-permute-done((bf16[2,256,256]{2,1,0:T(8,128)(2,1)S(1)}, bf16[2,256,256]{2,1,0:T(8,128)(2,1)S(1)}, u32[]{:S(2)}, u32[]{:S(2)}) %collective-permute-start.2) | collective-permute-done | bytes 262176 | tf_op jit(solution)/shard_map/ppermute | solution.py:26
  24.6 4.3 %collective-permute-done.3.refs_4_ = bf16[2,256,256]{2,1,0:T(8,128)(2,1)S(1)} collective-permute-done((bf16[2,256,256]{2,1,0:T(8,128)(2,1)}, bf16[2,256,256]{2,1,0:T(8,128)(2,1)S(1)}, u32[]{:S(2)}, u32[]{:S(2)}) %collective-permute-start.3) | collective-permute-done | bytes 262176 | tf_op jit(solution)/shard_map/ppermute | solution.py:27
  29.7 1.6 shard_map.21
  31.4 2.0 collective-permute-start.19
  33.4 6.6 %collective-permute-done.18.refs_1_ = bf16[2,512,128]{2,1,0:T(8,128)(2,1)S(1)} collective-permute-done((bf16[2,512,128]{2,1,0:T(8,128)(2,1)S(1)}, bf16[2,512,128]{2,1,0:T(8,128)(2,1)S(1)}, u32[]{:S(2)}, u32[]{:S(2)}) %collective-permute-start.18) | collective-permute-done | bytes 262176 | tf_op jit(solution)/shard_map/ppermute | solution.py:180
  40.0 4.1 %collective-permute-done.19.refs_2_ = bf16[2,512,128]{2,1,0:T(8,128)(2,1)S(1)} collective-permute-done((bf16[2,512,128]{2,1,0:T(8,128)(2,1)S(1)}, bf16[2,512,128]{2,1,0:T(8,128)(2,1)S(1)}, u32[]{:S(2)}, u32[]{:S(2)}) %collective-permute-start.19) | collective-permute-done | bytes 262176 | tf_op jit(solution)/shard_map/ppermute | solution.py:180
  45.6 7.3 %collective-permute-start.4 = (bf16[2,512,256]{2,1,0:T(8,128)(2,1)S(1)}, bf16[2,512,256]{2,1,0:T(8,128)(2,1)}, u32[]{:S(2)}, u32[]{:S(2)}) collective-permute-start(bf16[2,512,256]{2,1,0:T(8,128)(2,1)S(1)} %copy-done.13), channel_id=1, source_target_pairs={{0,128},{128,0},{1,129},{129,1},{2,130},{130,2},{3,131},{131,3},{4... | collective-permute-start | bytes 1572872 | tf_op jit(solution)/shard_map/ppermute | solution.py:167
  52.8 14.9 %collective-permute-done.4.refs_0_.refs_5_ = bf16[2,512,256]{2,1,0:T(8,128)(2,1)} collective-permute-done((bf16[2,512,256]{2,1,0:T(8,128)(2,1)S(1)}, bf16[2,512,256]{2,1,0:T(8,128)(2,1)}, u32[]{:S(2)}, u32[]{:S(2)}) %collective-permute-start.4) | collective-permute-done | bytes 524320 | tf_op jit(solution)/shard_map/ppermute | solution.py:167
  67.7 3.2 %collective-permute-start.7 = (bf16[2,512,256]{2,1,0:T(8,128)(2,1)}, bf16[2,512,256]{2,1,0:T(8,128)(2,1)S(1)}, u32[]{:S(2)}, u32[]{:S(2)}) collective-permute-start(bf16[2,512,256]{2,1,0:T(8,128)(2,1)} %collective-permute-done.4.refs_0_.refs_5_), channel_id=1, source_target_pairs={{0,3},{1,0},{2,1},{3,2},{4,7},{5,4},{6,5},{7,6},{8,11},{9,8},{10,9... | collective-permute-start | bytes 1572872 | tf_op jit(solution)/shard_map/ppermute | solution.py:24
  71.0 2.4 %collective-permute-start.12 = (bf16[2,512,256]{2,1,0:T(8,128)(2,1)}, bf16[2,512,256]{2,1,0:T(8,128)(2,1)}, u32[]{:S(2)}, u32[]{:S(2)}) collective-permute-start(bf16[2,512,256]{2,1,0:T(8,128)(2,1)} %collective-permute-done.4.refs_0_.refs_5_), channel_id=1, source_target_pairs={{0,96},{32,0},{64,32},{96,64},{1,97},{33,1},{65,33},{97,65},{2,98}... | collective-permute-start | bytes 1572872 | tf_op jit(solution)/shard_map/ppermute | solution.py:170
  73.4 9.3 %collective-permute-done.8.refs_2_.refs_7_ = bf16[2,512,256]{2,1,0:T(8,128)(2,1)S(1)} collective-permute-done((bf16[2,512,256]{2,1,0:T(8,128)(2,1)}, bf16[2,512,256]{2,1,0:T(8,128)(2,1)S(1)}, u32[]{:S(2)}, u32[]{:S(2)}) %collective-permute-start.8) | collective-permute-done | bytes 524320 | tf_op jit(solution)/shard_map/ppermute | solution.py:25
  82.9 3.3 %collective-permute-start.9 = (bf16[2,256,256]{2,1,0:T(8,128)(2,1)S(1)}, bf16[2,256,256]{2,1,0:T(8,128)(2,1)S(1)}, u32[]{:S(2)}, u32[]{:S(2)}) collective-permute-start(bf16[2,256,256]{2,1,0:T(8,128)(2,1)S(1)} %slice.90), channel_id=1, source_target_pairs={{0,3},{1,0},{2,1},{3,2},{4,7},{5,4},{6,5},{7,6},{8,11},{9,8},{10,9... | collective-permute-start | bytes 786440 | tf_op jit(solution)/shard_map/ppermute | solution.py:26
  86.1 4.9 %collective-permute-done.10.refs_4_.refs_9_ = bf16[2,256,256]{2,1,0:T(8,128)(2,1)S(1)} collective-permute-done((bf16[2,256,256]{2,1,0:T(8,128)(2,1)S(1)}, bf16[2,256,256]{2,1,0:T(8,128)(2,1)S(1)}, u32[]{:S(2)}, u32[]{:S(2)}) %collective-permute-start.10) | collective-permute-done | bytes 262176 | tf_op jit(solution)/shard_map/ppermute | solution.py:27
  91.1 2.3 %shard_map.17.here = bf16[2048,128]{1,0:T(8,128)(2,1)} custom-call(s32[1]{0:T(128)} %bitcast.5.x, bf16[2,512,256]{2,1,0:T(8,128)(2,1)} %collective-permute-done.4.refs_0_.refs_5_, bf16[2,512,256]{2,1,0:T(8,128)(2,1)S(1)} %collective-permute-done.7.refs_1_.refs_6_, bf16[2,512,256]{2,1,0:T(8,128)(2,1)S(1)} %collective-permute-done.8.refs_2_.refs_7_, ...), custom_call_target="tpu_custom_call" | custom-call | bytes 2097152 | tf_op jit(solution)/shard_map/pallas_call | solution.py:101
  93.4 3.1 %collective-permute-start.11 = (bf16[2048,128]{1,0:T(8,128)(2,1)}, bf16[2048,128]{1,0:T(8,128)(2,1)}, u32[]{:S(2)}, u32[]{:S(2)}) collective-permute-start(bf16[2048,128]{1,0:T(8,128)(2,1)} %shard_map.17.here), channel_id=1, source_target_pairs={{0,64},{32,96},{64,0},{96,32},{1,65},{33,97},{65,1},{97,33},{2,66}... | collective-permute-start | bytes 1572872 | tf_op jit(solution)/shard_map/ppermute | solution.py:170
  96.5 1.6 shard_map.18
  98.0 3.0 %collective-permute-start.14 = (bf16[2,512,128]{2,1,0:T(8,128)(2,1)S(1)}, bf16[2,512,128]{2,1,0:T(8,128)(2,1)S(1)}, u32[]{:S(2)}, u32[]{:S(2)}) collective-permute-start(bf16[2,512,128]{2,1,0:T(8,128)(2,1)S(1)} %get-tuple-element.29), channel_id=1, source_target_pairs={{0,3},{1,0},{2,1},{3,2},{4,7},{5,4},{6,5},{7,6},{8,11},{9,8},{10,9... | collective-permute-start | bytes 786440 | tf_op jit(solution)/shard_map/ppermute | solution.py:180
  101.0 1.6 collective-permute-start.16
  106.5 4.4 %shard_map.23 = (f32[2,4,256,128]{3,2,1,0:T(8,128)S(1)}, f32[8,128]{1,0:T(8,128)S(1)}) custom-call(s32[3]{0:T(128)S(1)} %pad_add_fusion.place, bf16[2,512,256]{2,1,0:T(8,128)(2,1)S(1)} %dynamic-slice_bitcast_fusion.refs_0_, bf16[2,512,256]{2,1,0:T(8,128)(2,1)S(1)} %collective-permute-done.refs_1_, bf16[2,512,256]{2,1,0:T(8,128)(2,1)S(1)} %collective-permute-done.1.refs_2_, ...), custom_call_target="tpu_custom_call" | custom-call | flops 2147483648 | bytes 8388608 | tf_op jit(solution)/shard_map/pallas_call | solution.py:142
  110.9 2.3 %collective-permute-done.15.refs_2_ = bf16[2,512,128]{2,1,0:T(8,128)(2,1)S(1)} collective-permute-done((bf16[2,512,128]{2,1,0:T(8,128)(2,1)S(1)}, bf16[2,512,128]{2,1,0:T(8,128)(2,1)S(1)}, u32[]{:S(2)}, u32[]{:S(2)}) %collective-permute-start.15) | collective-permute-done | bytes 262176 | tf_op jit(solution)/shard_map/ppermute | solution.py:180
  114.8 4.4 %shard_map.24 = (f32[2,4,256,128]{3,2,1,0:T(8,128)S(1)}, f32[8,128]{1,0:T(8,128)S(1)}) custom-call(s32[3]{0:T(128)S(1)} %pad_add_fusion.place, bf16[2,512,256]{2,1,0:T(8,128)(2,1)S(1)} %dynamic-slice_bitcast_fusion.refs_0_, bf16[2,512,256]{2,1,0:T(8,128)(2,1)S(1)} %collective-permute-done.refs_1_, bf16[2,512,256]{2,1,0:T(8,128)(2,1)S(1)} %collective-permute-done.1.refs_2_, ...), custom_call_target="tpu_custom_call" | custom-call | flops 2147483648 | bytes 8388608 | tf_op jit(solution)/shard_map/pallas_call | solution.py:142
  119.3 3.8 %shard_map.25 = (f32[2,4,256,128]{3,2,1,0:T(8,128)S(1)}, f32[8,128]{1,0:T(8,128)S(1)}) custom-call(s32[3]{0:T(128)S(1)} %pad_add_fusion.place, bf16[2,512,256]{2,1,0:T(8,128)(2,1)S(1)} %dynamic-slice_bitcast_fusion.refs_0_, bf16[2,512,256]{2,1,0:T(8,128)(2,1)S(1)} %collective-permute-done.refs_1_, bf16[2,512,256]{2,1,0:T(8,128)(2,1)S(1)} %collective-permute-done.1.refs_2_, ...), custom_call_target="tpu_custom_call" | custom-call | flops 2147483648 | bytes 8388608 | tf_op jit(solution)/shard_map/pallas_call | solution.py:142
  123.4 4.1 %shard_map.26 = f32[32,264,128]{2,1,0:T(8,128)S(1)} custom-call(s32[3]{0:T(128)S(1)} %pad_add_fusion.place, bf16[2,512,256]{2,1,0:T(8,128)(2,1)S(1)} %dynamic-slice_bitcast_fusion.refs_0_, bf16[2,512,256]{2,1,0:T(8,128)(2,1)S(1)} %collective-permute-done.refs_1_, bf16[2,512,256]{2,1,0:T(8,128)(2,1)S(1)} %collective-permute-done.1.refs_2_, ...), custom_call_target="tpu_custom_call" | custom-call | flops 2147483648 | bytes 8388608 | tf_op jit(solution)/shard_map/pallas_call | solution.py:142
  127.5 1.6 convert_element_type.45
  129.2 18.3 %all-to-all-start = ((f16[32,264,128]{2,1,0:T(8,128)(2,1)}), f16[32,264,128]{2,1,0:T(8,128)(2,1)S(1)}, u32[]{:S(2)}, u32[]{:S(2)}) async-start(f16[32,264,128]{2,1,0:T(8,128)(2,1)} %convert_element_type.45), calls=%async_computation | async-start | bytes 4325376 | tf_op jit(solution)/shard_map/all_to_all | solution.py:198
  147.7 51.5 %all-to-all-done = f16[32,264,128]{2,1,0:T(8,128)(2,1)S(1)} async-done(((f16[32,264,128]{2,1,0:T(8,128)(2,1)}), f16[32,264,128]{2,1,0:T(8,128)(2,1)S(1)}, u32[]{:S(2)}, u32[]{:S(2)}) %all-to-all-start) | async-done | bytes 2162720 | tf_op jit(solution)/shard_map/all_to_all | solution.py:198
  199.7 1.7 fusion.14
  202.2 2.0 fusion.1
  (78 shorter events, 15.0 us)
Async XLA Ops:
  2.1 14.0 %collective-permute-start = (bf16[2,512,256]{2,1,0:T(8,128)(2,1)S(1)}, bf16[2,512,256]{2,1,0:T(8,128)(2,1)S(1)}, u32[]{:S(2)}, u32[]{:S(2)}) collective-permute-start(bf16[2,512,256]{2,1,0:T(8,128)(2,1)S(1)} %dynamic-slice_bitcast_fusion.refs_0_), channel_id=1, source_target_pairs={{0,3},{1,0},{2,1},{3,2},{4,7},{5,4},{6,5},{7,6},{8,11},{9,8},{10,9... | collective-permute-start | bytes 1572872 | tf_op jit(solution)/shard_map/ppermute | solution.py:24
  4.9 15.0 %collective-permute-start.1 = (bf16[2,512,256]{2,1,0:T(8,128)(2,1)S(1)}, bf16[2,512,256]{2,1,0:T(8,128)(2,1)S(1)}, u32[]{:S(2)}, u32[]{:S(2)}) collective-permute-start(bf16[2,512,256]{2,1,0:T(8,128)(2,1)S(1)} %dynamic-slice_bitcast_fusion.refs_0_), channel_id=1, source_target_pairs={{0,1},{1,2},{2,3},{3,0},{4,5},{5,6},{6,7},{7,4},{8,9},{9,10},{10,1... | collective-permute-start | bytes 1572872 | tf_op jit(solution)/shard_map/ppermute | solution.py:25
  4.9 24.8 %collective-permute-start.5 = (bf16[2,512,256]{2,1,0:T(8,128)(2,1)S(1)}, bf16[2,512,256]{2,1,0:T(8,128)(2,1)}, u32[]{:S(2)}, u32[]{:S(2)}) collective-permute-start(bf16[2,512,256]{2,1,0:T(8,128)(2,1)S(1)} %dynamic-slice_bitcast_fusion.refs_0_), channel_id=1, source_target_pairs={{0,96},{32,0},{64,32},{96,64},{1,97},{33,1},{65,33},{97,65},{2,98}... | collective-permute-start | bytes 1572872 | tf_op jit(solution)/shard_map/ppermute | solution.py:170
  5.4 24.3 %collective-permute-start.6 = (bf16[2,512,256]{2,1,0:T(8,128)(2,1)S(1)}, bf16[2,512,256]{2,1,0:T(8,128)(2,1)}, u32[]{:S(2)}, u32[]{:S(2)}) collective-permute-start(bf16[2,512,256]{2,1,0:T(8,128)(2,1)S(1)} %dynamic-slice_bitcast_fusion.refs_0_), channel_id=1, source_target_pairs={{0,32},{32,64},{64,96},{96,0},{1,33},{33,65},{65,97},{97,1},{2,34}... | collective-permute-start | bytes 1572872 | tf_op jit(solution)/shard_map/ppermute | solution.py:170
  16.1 8.5 %collective-permute-start.2 = (bf16[2,256,256]{2,1,0:T(8,128)(2,1)S(1)}, bf16[2,256,256]{2,1,0:T(8,128)(2,1)S(1)}, u32[]{:S(2)}, u32[]{:S(2)}) collective-permute-start(bf16[2,256,256]{2,1,0:T(8,128)(2,1)S(1)} %slice.88), channel_id=1, source_target_pairs={{0,3},{1,0},{2,1},{3,2},{4,7},{5,4},{6,5},{7,6},{8,11},{9,8},{10,9... | collective-permute-start | bytes 786440 | tf_op jit(solution)/shard_map/ppermute | solution.py:26
  20.6 8.3 %collective-permute-start.3 = (bf16[2,256,256]{2,1,0:T(8,128)(2,1)}, bf16[2,256,256]{2,1,0:T(8,128)(2,1)S(1)}, u32[]{:S(2)}, u32[]{:S(2)}) collective-permute-start(bf16[2,256,256]{2,1,0:T(8,128)(2,1)} %slice.89), channel_id=1, source_target_pairs={{0,1},{1,2},{2,3},{3,0},{4,5},{5,6},{6,7},{7,4},{8,9},{9,10},{10,1... | collective-permute-start | bytes 786440 | tf_op jit(solution)/shard_map/ppermute | solution.py:27
  28.9 16.6 %copy-start.4 = (bf16[2,256,256]{2,1,0:T(8,128)(2,1)}, bf16[2,256,256]{2,1,0:T(8,128)(2,1)S(1)}, u32[]{:S(2)}) copy-start(bf16[2,256,256]{2,1,0:T(8,128)(2,1)S(1)} %collective-permute-done.3.refs_4_) | copy-start | bytes 786436
  29.2 14.9 %collective-permute-start.17 = (bf16[2048,128]{1,0:T(8,128)(2,1)S(1)}, bf16[2048,128]{1,0:T(8,128)(2,1)S(1)}, u32[]{:S(2)}, u32[]{:S(2)}) collective-permute-start(bf16[2048,128]{1,0:T(8,128)(2,1)S(1)} %shard_map.20.here), channel_id=1, source_target_pairs={{0,64},{32,96},{64,0},{96,32},{1,65},{33,97},{65,1},{97,33},{2,66}... | collective-permute-start | bytes 1572872 | tf_op jit(solution)/shard_map/ppermute | solution.py:170
  31.3 8.7 %collective-permute-start.18 = (bf16[2,512,128]{2,1,0:T(8,128)(2,1)S(1)}, bf16[2,512,128]{2,1,0:T(8,128)(2,1)S(1)}, u32[]{:S(2)}, u32[]{:S(2)}) collective-permute-start(bf16[2,512,128]{2,1,0:T(8,128)(2,1)S(1)} %get-tuple-element.33), channel_id=1, source_target_pairs={{0,3},{1,0},{2,1},{3,2},{4,7},{5,4},{6,5},{7,6},{8,11},{9,8},{10,9... | collective-permute-start | bytes 786440 | tf_op jit(solution)/shard_map/ppermute | solution.py:180
  31.4 12.7 %collective-permute-start.19 = (bf16[2,512,128]{2,1,0:T(8,128)(2,1)S(1)}, bf16[2,512,128]{2,1,0:T(8,128)(2,1)S(1)}, u32[]{:S(2)}, u32[]{:S(2)}) collective-permute-start(bf16[2,512,128]{2,1,0:T(8,128)(2,1)S(1)} %get-tuple-element.34), channel_id=1, source_target_pairs={{0,1},{1,2},{2,3},{3,0},{4,5},{5,6},{6,7},{7,4},{8,9},{9,10},{10,1... | collective-permute-start | bytes 786440 | tf_op jit(solution)/shard_map/ppermute | solution.py:180
  33.4 10.7 %collective-permute-start.20 = (bf16[2,512,128]{2,1,0:T(8,128)(2,1)S(1)}, bf16[2,512,128]{2,1,0:T(8,128)(2,1)S(1)}, u32[]{:S(2)}, u32[]{:S(2)}) collective-permute-start(bf16[2,512,128]{2,1,0:T(8,128)(2,1)S(1)} %get-tuple-element.35), channel_id=1, source_target_pairs={{0,2},{1,3},{2,0},{3,1},{4,6},{5,7},{6,4},{7,5},{8,10},{9,11},{10,... | collective-permute-start | bytes 786440 | tf_op jit(solution)/shard_map/ppermute | solution.py:180
  45.6 69.2 %collective-permute-start.21 = (bf16[4,2048,128]{2,1,0:T(8,128)(2,1)}, bf16[4,2048,128]{2,1,0:T(8,128)(2,1)}, u32[]{:S(2)}, u32[]{:S(2)}) collective-permute-start(bf16[4,2048,128]{2,1,0:T(8,128)(2,1)} %shard_map.22.refs_10_), channel_id=1, source_target_pairs={{0,16},{16,0},{1,17},{17,1},{2,18},{18,2},{3,19},{19,3},{4,20},{20... | collective-permute-start | bytes 6291464 | tf_op jit(solution)/shard_map/ppermute | solution.py:173
  45.6 22.1 %collective-permute-start.4 = (bf16[2,512,256]{2,1,0:T(8,128)(2,1)S(1)}, bf16[2,512,256]{2,1,0:T(8,128)(2,1)}, u32[]{:S(2)}, u32[]{:S(2)}) collective-permute-start(bf16[2,512,256]{2,1,0:T(8,128)(2,1)S(1)} %copy-done.13), channel_id=1, source_target_pairs={{0,128},{128,0},{1,129},{129,1},{2,130},{130,2},{3,131},{131,3},{4... | collective-permute-start | bytes 1572872 | tf_op jit(solution)/shard_map/ppermute | solution.py:167
  67.7 15.0 %collective-permute-start.8 = (bf16[2,512,256]{2,1,0:T(8,128)(2,1)}, bf16[2,512,256]{2,1,0:T(8,128)(2,1)S(1)}, u32[]{:S(2)}, u32[]{:S(2)}) collective-permute-start(bf16[2,512,256]{2,1,0:T(8,128)(2,1)} %collective-permute-done.4.refs_0_.refs_5_), channel_id=1, source_target_pairs={{0,1},{1,2},{2,3},{3,0},{4,5},{5,6},{6,7},{7,4},{8,9},{9,10},{10,1... | collective-permute-start | bytes 1572872 | tf_op jit(solution)/shard_map/ppermute | solution.py:25
  67.7 15.1 %collective-permute-start.7 = (bf16[2,512,256]{2,1,0:T(8,128)(2,1)}, bf16[2,512,256]{2,1,0:T(8,128)(2,1)S(1)}, u32[]{:S(2)}, u32[]{:S(2)}) collective-permute-start(bf16[2,512,256]{2,1,0:T(8,128)(2,1)} %collective-permute-done.4.refs_0_.refs_5_), channel_id=1, source_target_pairs={{0,3},{1,0},{2,1},{3,2},{4,7},{5,4},{6,5},{7,6},{8,11},{9,8},{10,9... | collective-permute-start | bytes 1572872 | tf_op jit(solution)/shard_map/ppermute | solution.py:24
  71.0 25.5 %collective-permute-start.12 = (bf16[2,512,256]{2,1,0:T(8,128)(2,1)}, bf16[2,512,256]{2,1,0:T(8,128)(2,1)}, u32[]{:S(2)}, u32[]{:S(2)}) collective-permute-start(bf16[2,512,256]{2,1,0:T(8,128)(2,1)} %collective-permute-done.4.refs_0_.refs_5_), channel_id=1, source_target_pairs={{0,96},{32,0},{64,32},{96,64},{1,97},{33,1},{65,33},{97,65},{2,98}... | collective-permute-start | bytes 1572872 | tf_op jit(solution)/shard_map/ppermute | solution.py:170
  73.4 23.1 %collective-permute-start.13 = (bf16[2,512,256]{2,1,0:T(8,128)(2,1)}, bf16[2,512,256]{2,1,0:T(8,128)(2,1)}, u32[]{:S(2)}, u32[]{:S(2)}) collective-permute-start(bf16[2,512,256]{2,1,0:T(8,128)(2,1)} %collective-permute-done.4.refs_0_.refs_5_), channel_id=1, source_target_pairs={{0,32},{32,64},{64,96},{96,0},{1,33},{33,65},{65,97},{97,1},{2,34}... | collective-permute-start | bytes 1572872 | tf_op jit(solution)/shard_map/ppermute | solution.py:170
  82.7 8.3 %collective-permute-start.10 = (bf16[2,256,256]{2,1,0:T(8,128)(2,1)S(1)}, bf16[2,256,256]{2,1,0:T(8,128)(2,1)S(1)}, u32[]{:S(2)}, u32[]{:S(2)}) collective-permute-start(bf16[2,256,256]{2,1,0:T(8,128)(2,1)S(1)} %slice.91), channel_id=1, source_target_pairs={{0,1},{1,2},{2,3},{3,0},{4,5},{5,6},{6,7},{7,4},{8,9},{9,10},{10,1... | collective-permute-start | bytes 786440 | tf_op jit(solution)/shard_map/ppermute | solution.py:27
  82.8 8.2 %copy-start.1 = (bf16[2,512,256]{2,1,0:T(8,128)(2,1)}, bf16[2,512,256]{2,1,0:T(8,128)(2,1)S(1)}, u32[]{:S(2)}) copy-start(bf16[2,512,256]{2,1,0:T(8,128)(2,1)S(1)} %collective-permute-done.7.refs_1_.refs_6_) | copy-start | bytes 1572868
  82.9 8.2 %collective-permute-start.9 = (bf16[2,256,256]{2,1,0:T(8,128)(2,1)S(1)}, bf16[2,256,256]{2,1,0:T(8,128)(2,1)S(1)}, u32[]{:S(2)}, u32[]{:S(2)}) collective-permute-start(bf16[2,256,256]{2,1,0:T(8,128)(2,1)S(1)} %slice.90), channel_id=1, source_target_pairs={{0,3},{1,0},{2,1},{3,2},{4,7},{5,4},{6,5},{7,6},{8,11},{9,8},{10,9... | collective-permute-start | bytes 786440 | tf_op jit(solution)/shard_map/ppermute | solution.py:26
  91.0 2.3 %copy-start.7 = (bf16[2,256,256]{2,1,0:T(8,128)(2,1)}, bf16[2,256,256]{2,1,0:T(8,128)(2,1)S(1)}, u32[]{:S(2)}) copy-start(bf16[2,256,256]{2,1,0:T(8,128)(2,1)S(1)} %collective-permute-done.10.refs_4_.refs_9_) | copy-start | bytes 786436
  91.1 2.3 %copy-start.10 = (bf16[2,256,256]{2,1,0:T(8,128)(2,1)}, bf16[2,256,256]{2,1,0:T(8,128)(2,1)S(1)}, u32[]{:S(2)}) copy-start(bf16[2,256,256]{2,1,0:T(8,128)(2,1)S(1)} %collective-permute-done.9.refs_3_.refs_8_) | copy-start | bytes 786436
  93.4 19.9 %collective-permute-start.11 = (bf16[2048,128]{1,0:T(8,128)(2,1)}, bf16[2048,128]{1,0:T(8,128)(2,1)}, u32[]{:S(2)}, u32[]{:S(2)}) collective-permute-start(bf16[2048,128]{1,0:T(8,128)(2,1)} %shard_map.17.here), channel_id=1, source_target_pairs={{0,64},{32,96},{64,0},{96,32},{1,65},{33,97},{65,1},{97,33},{2,66}... | collective-permute-start | bytes 1572872 | tf_op jit(solution)/shard_map/ppermute | solution.py:170
  98.0 12.9 %collective-permute-start.14 = (bf16[2,512,128]{2,1,0:T(8,128)(2,1)S(1)}, bf16[2,512,128]{2,1,0:T(8,128)(2,1)S(1)}, u32[]{:S(2)}, u32[]{:S(2)}) collective-permute-start(bf16[2,512,128]{2,1,0:T(8,128)(2,1)S(1)} %get-tuple-element.29), channel_id=1, source_target_pairs={{0,3},{1,0},{2,1},{3,2},{4,7},{5,4},{6,5},{7,6},{8,11},{9,8},{10,9... | collective-permute-start | bytes 786440 | tf_op jit(solution)/shard_map/ppermute | solution.py:180
  101.0 12.2 %collective-permute-start.15 = (bf16[2,512,128]{2,1,0:T(8,128)(2,1)S(1)}, bf16[2,512,128]{2,1,0:T(8,128)(2,1)S(1)}, u32[]{:S(2)}, u32[]{:S(2)}) collective-permute-start(bf16[2,512,128]{2,1,0:T(8,128)(2,1)S(1)} %get-tuple-element.30), channel_id=1, source_target_pairs={{0,1},{1,2},{2,3},{3,0},{4,5},{5,6},{6,7},{7,4},{8,9},{9,10},{10,1... | collective-permute-start | bytes 786440 | tf_op jit(solution)/shard_map/ppermute | solution.py:180
  101.0 12.2 %collective-permute-start.16 = (bf16[2,512,128]{2,1,0:T(8,128)(2,1)S(1)}, bf16[2,512,128]{2,1,0:T(8,128)(2,1)S(1)}, u32[]{:S(2)}, u32[]{:S(2)}) collective-permute-start(bf16[2,512,128]{2,1,0:T(8,128)(2,1)S(1)} %get-tuple-element.31), channel_id=1, source_target_pairs={{0,2},{1,3},{2,0},{3,1},{4,6},{5,7},{6,4},{7,5},{8,10},{9,11},{10,... | collective-permute-start | bytes 786440 | tf_op jit(solution)/shard_map/ppermute | solution.py:180
  113.2 1.5 copy-start.3
  113.2 1.5 copy-start.6
  113.3 1.5 copy-start.9
  113.3 1.6 copy-start.12
  119.2 4.2 %collective-permute-start.22 = (bf16[4,2048,128]{2,1,0:T(8,128)(2,1)S(1)}, bf16[4,2048,128]{2,1,0:T(8,128)(2,1)S(1)}, u32[]{:S(2)}, u32[]{:S(2)}) collective-permute-start(bf16[4,2048,128]{2,1,0:T(8,128)(2,1)S(1)} %shard_map.19.refs_10_), channel_id=1, source_target_pairs={{0,16},{16,0},{1,17},{17,1},{2,18},{18,2},{3,19},{19,3},{4,20},{20... | collective-permute-start | bytes 6291464 | tf_op jit(solution)/shard_map/ppermute | solution.py:173
  129.2 70.0 %all-to-all-start = ((f16[32,264,128]{2,1,0:T(8,128)(2,1)}), f16[32,264,128]{2,1,0:T(8,128)(2,1)S(1)}, u32[]{:S(2)}, u32[]{:S(2)}) async-start(f16[32,264,128]{2,1,0:T(8,128)(2,1)} %convert_element_type.45), calls=%async_computation | async-start | bytes 4325376 | tf_op jit(solution)/shard_map/all_to_all | solution.py:198
  (6 other events, 6.6 us)
where the time goes:
time: 207 us; the launch traced here: 206 us
  waiting for transfers between devices  111 us (54%)
  starting transfers between devices  53.6 us (26%)
  Pallas kernels  25.2 us (12%)
  local copies, waits for them, and re-layouts  9.88 us (5%)
  other arithmetic  5.73 us (3%)
    all_to_all x1, waiting for transfers between devices, body(): got = lax.all_to_all(sent, ('zh', 'zl', 'x'), 0, 0, tiled=True)  51.5 us
    all_to_all x1, starting transfers between devices, body(): got = lax.all_to_all(sent, ('zh', 'zl', 'x'), 0, 0, tiled=True)  18.3 us
    pallas_call x4, Pallas kernels, terms_of(): pl.pallas_call(kernel, out_shape=shapes, in_specs=[SCALAR] + [SPACE] * (l...  16.6 us
    ppermute x1, waiting for transfers between devices, body(): other = lax.ppermute(other, 'zh', ring(2, 1))  14.9 us
    ppermute x6, waiting for transfers between devices, gathered(): lax.ppermute(part, 'x', ring(4, step))  13 us
    ppermute x2, waiting for transfers between devices, gather_x(): below = lax.ppermute(block, 'x', ring(4, 1))  9.33 us
    ppermute x2, waiting for transfers between devices, gather_x(): far_b = lax.ppermute(below[:, half:], 'x', ring(4, 1))  9.26 us
    ppermute x2, waiting for transfers between devices, gather_x(): above = lax.ppermute(block, 'x', ring(4, -1))  9.15 us
  transfers between devices with their start and end apart: 24, of which 11 were waited for; matrix products, arithmetic and copies ran while one was open for 0% of the time, Pallas kernels for 7%

commit v1 on v0

--- a/solution.py
+++ b/solution.py
@@ -179,21 +179,22 @@
         kept, *sent = small_call(near_kernel, (cut,) * 4, x[None], *near)
         moved = [lax.ppermute(part, "x", ring(4, step)) for part, step in zip(sent, (-1, 1, 2))]
         here = jax.ShapeDtypeStruct((4 * block.shape[1], 2 * group), block.dtype)
+        pieces[3:] = lax.optimization_barrier((*pieces[3:], kept))[:2]
         here = small_call(own_kernel, here, x[None], *pieces)
         far = from_y(here, 2)
         cols = jax.ShapeDtypeStruct((4, *here.shape), block.dtype)
         cols = small_call(join_kernel, cols, here, far, kept, *moved, scalars=0)
-        return pieces, cols, [*pieces[3:], *near]
+        return pieces, cols, [*pieces[3:], *near, *moved, far]
 
     rows0, mine0, done0 = gathered(own)
     rows1, mine1, _ = gathered(first_of(other, *done0))
     rows = (*rows0, *rows1)
 
     place = jnp.stack([f, y, core])
-    ready = (*terms_of(place, rows, mine0), *terms_of(place, rows, from_core(mine0)))
-    mine1, *ready = lax.optimization_barrier((mine1, *ready))
+    theirs0 = from_core(mine0)
+    mine1, *ready = lax.optimization_barrier((mine1, *terms_of(place, rows, mine0)))
     theirs1 = from_core(mine1)
-    ready = (*ready, *terms_of(place, rows, mine1))
+    ready = (*ready, *terms_of(place, rows, theirs0), *terms_of(place, rows, mine1))
     sent = terms_of(place, rows, theirs1, ready).astype(jnp.float16)
     got = lax.all_to_all(sent, ("zh", "zl", "x"), 0, 0, tiled=True)
 

time: 207 us -> 185 us (0.89)
  waiting for transfers between devices: 111 us -> 86.6 us
  local copies, waits for them, and re-layouts: 9.88 us -> 19.5 us
  starting transfers between devices: 53.6 us -> 48.6 us
  Pallas kernels: 25.2 us -> 20.9 us
    ppermute x1, waiting for transfers between devices: 14.9 us -> 3.91 us  [body(): other = lax.ppermute(other, 'zh', ring(2, 1))]
    ppermute x2, waiting for transfers between devices: 9.33 us -> 0.08 us  [gather_x(): below = lax.ppermute(block, 'x', ring(4, 1))]
    all_to_all x1, starting transfers between devices: 18.3 us -> 10.2 us  [body(): got = lax.all_to_all(sent, ('zh', 'zl', 'x'), 0, 0, tiled=True)]
    ppermute x2, waiting for transfers between devices: 9.15 us -> 16.9 us  [gather_x(): above = lax.ppermute(block, 'x', ring(4, -1))]
    unnamed x28 -> x54, local copies, waits for them, and re-layouts: 5.22 us -> 12.6 us
    ppermute x6, waiting for transfers between devices: 13 us -> 6.63 us  [gathered(): lax.ppermute(part, 'x', ring(4, step))]
    ppermute x2, waiting for transfers between devices: 9.26 us -> 3.53 us  [gather_x(): far_b = lax.ppermute(below[:, half:], 'x', ring(4, 1))]
    ppermute x6, starting transfers between devices: 8.06 us -> 13.2 us  [from_y(): return lax.ppermute(block, 'y', ring(4, -step))]
  transfers between devices with their start and end apart: 24 -> 24, of which waited for: 11 -> 9; matrix products, arithmetic and copies ran while one was open for 0% -> 1% of each run, Pallas kernels for 7% -> 9%
where the time goes in v1:
time: 185 us; the launch traced here: 182 us
  waiting for transfers between devices  86.6 us (47%)
  starting transfers between devices  48.6 us (26%)
  Pallas kernels  20.9 us (11%)
  local copies, waits for them, and re-layouts  19.5 us (11%)
  other arithmetic  6.28 us (3%)
    all_to_all x1, waiting for transfers between devices, body(): got = lax.all_to_all(sent, ('zh', 'zl', 'x'), 0, 0, tiled=True)  52 us
    ppermute x2, waiting for transfers between devices, gather_x(): above = lax.ppermute(block, 'x', ring(4, -1))  16.9 us
    pallas_call x4, Pallas kernels, terms_of(): pl.pallas_call(kernel, out_shape=shapes, in_specs=[SCALAR] + [SPACE] * (l...  15.2 us
    ppermute x6, starting transfers between devices, from_y(): return lax.ppermute(block, 'y', ring(4, -step))  13.2 us
    unnamed x54, local copies, waits for them, and re-layouts  12.6 us
    all_to_all x1, starting transfers between devices, body(): got = lax.all_to_all(sent, ('zh', 'zl', 'x'), 0, 0, tiled=True)  10.2 us
    ppermute x1, starting transfers between devices, body(): other = lax.ppermute(other, 'zh', ring(2, 1))  7.19 us
    ppermute x6, starting transfers between devices, gathered(): lax.ppermute(part, 'x', ring(4, step))  6.68 us
  transfers between devices with their start and end apart: 24, of which 9 were waited for; matrix products, arithmetic and copies ran while one was open for 1% of the time, Pallas kernels for 9%

profile of v1, /device:TPU:16, one launch (start us, length us, event | category | flops | bytes accessed | tf_op | source)
XLA Modules:
  0.0 182.1 jit_solution(18099715085857801814)
XLA Ops:
  0.0 1.2 copy-done
  2.1 2.8 %collective-permute-start = (bf16[2,512,256]{2,1,0:T(8,128)(2,1)S(1)}, bf16[2,512,256]{2,1,0:T(8,128)(2,1)S(1)}, u32[]{:S(2)}, u32[]{:S(2)}) collective-permute-start(bf16[2,512,256]{2,1,0:T(8,128)(2,1)S(1)} %dynamic-slice_bitcast_fusion.refs_0_), channel_id=1, source_target_pairs={{0,3},{1,0},{2,1},{3,2},{4,7},{5,4},{6,5},{7,6},{8,11},{9,8},{10,9... | collective-permute-start | bytes 1572872 | tf_op jit(solution)/shard_map/ppermute | solution.py:24
  5.4 1.6 collective-permute-start.5
  7.0 9.2 %collective-permute-done.refs_1_ = bf16[2,512,256]{2,1,0:T(8,128)(2,1)S(1)} collective-permute-done((bf16[2,512,256]{2,1,0:T(8,128)(2,1)S(1)}, bf16[2,512,256]{2,1,0:T(8,128)(2,1)S(1)}, u32[]{:S(2)}, u32[]{:S(2)}) %collective-permute-start) | collective-permute-done | bytes 524320 | tf_op jit(solution)/shard_map/ppermute | solution.py:24
  16.8 3.7 %collective-permute-start.2 = (bf16[2,256,256]{2,1,0:T(8,128)(2,1)}, bf16[2,256,256]{2,1,0:T(8,128)(2,1)S(1)}, u32[]{:S(2)}, u32[]{:S(2)}) collective-permute-start(bf16[2,256,256]{2,1,0:T(8,128)(2,1)} %slice.88), channel_id=1, source_target_pairs={{0,3},{1,0},{2,1},{3,2},{4,7},{5,4},{6,5},{7,6},{8,11},{9,8},{10,9... | collective-permute-start | bytes 786440 | tf_op jit(solution)/shard_map/ppermute | solution.py:26
  21.3 7.2 %collective-permute-start.6 = (bf16[2,512,256]{2,1,0:T(8,128)(2,1)}, bf16[2,512,256]{2,1,0:T(8,128)(2,1)S(1)}, u32[]{:S(2)}, u32[]{:S(2)}) collective-permute-start(bf16[2,512,256]{2,1,0:T(8,128)(2,1)} %dynamic-slice_bitcast_fusion.1), channel_id=1, source_target_pairs={{0,128},{128,0},{1,129},{129,1},{2,130},{130,2},{3,131},{131,3},{4... | collective-permute-start | bytes 1572872 | tf_op jit(solution)/shard_map/ppermute | solution.py:167
  28.5 1.6 shard_map.17
  30.7 1.2 shard_map.18.here
  33.2 3.2 %collective-permute-start.7 = (bf16[2,512,128]{2,1,0:T(8,128)(2,1)S(1)}, bf16[2,512,128]{2,1,0:T(8,128)(2,1)S(1)}, u32[]{:S(2)}, u32[]{:S(2)}) collective-permute-start(bf16[2,512,128]{2,1,0:T(8,128)(2,1)S(1)} %get-tuple-element.32), channel_id=1, source_target_pairs={{0,3},{1,0},{2,1},{3,2},{4,7},{5,4},{6,5},{7,6},{8,11},{9,8},{10,9... | collective-permute-start | bytes 786440 | tf_op jit(solution)/shard_map/ppermute | solution.py:180
  36.3 1.5 collective-permute-start.9
  37.8 3.9 %collective-permute-done.6.refs_0_.refs_5_ = bf16[2,512,256]{2,1,0:T(8,128)(2,1)S(1)} collective-permute-done((bf16[2,512,256]{2,1,0:T(8,128)(2,1)}, bf16[2,512,256]{2,1,0:T(8,128)(2,1)S(1)}, u32[]{:S(2)}, u32[]{:S(2)}) %collective-permute-start.6) | collective-permute-done | bytes 524320 | tf_op jit(solution)/shard_map/ppermute | solution.py:167
  41.7 4.1 %collective-permute-done.7.refs_1_ = bf16[2,512,128]{2,1,0:T(8,128)(2,1)S(1)} collective-permute-done((bf16[2,512,128]{2,1,0:T(8,128)(2,1)S(1)}, bf16[2,512,128]{2,1,0:T(8,128)(2,1)S(1)}, u32[]{:S(2)}, u32[]{:S(2)}) %collective-permute-start.7) | collective-permute-done | bytes 262176 | tf_op jit(solution)/shard_map/ppermute | solution.py:180
  46.6 2.5 %collective-permute-done.8.refs_2_ = bf16[2,512,128]{2,1,0:T(8,128)(2,1)S(1)} collective-permute-done((bf16[2,512,128]{2,1,0:T(8,128)(2,1)S(1)}, bf16[2,512,128]{2,1,0:T(8,128)(2,1)S(1)}, u32[]{:S(2)}, u32[]{:S(2)}) %collective-permute-start.8) | collective-permute-done | bytes 262176 | tf_op jit(solution)/shard_map/ppermute | solution.py:180
  51.3 1.2 collective-permute-start.11
  53.3 2.4 %collective-permute-start.15 = (bf16[2,512,256]{2,1,0:T(8,128)(2,1)}, bf16[2,512,256]{2,1,0:T(8,128)(2,1)S(1)}, u32[]{:S(2)}, u32[]{:S(2)}) collective-permute-start(bf16[2,512,256]{2,1,0:T(8,128)(2,1)} %copy-done.3), channel_id=1, source_target_pairs={{0,96},{32,0},{64,32},{96,64},{1,97},{33,1},{65,33},{97,65},{2,98}... | collective-permute-start | bytes 1572872 | tf_op jit(solution)/shard_map/ppermute | solution.py:170
  55.7 7.7 %collective-permute-done.11.refs_1_.refs_6_ = bf16[2,512,256]{2,1,0:T(8,128)(2,1)S(1)} collective-permute-done((bf16[2,512,256]{2,1,0:T(8,128)(2,1)}, bf16[2,512,256]{2,1,0:T(8,128)(2,1)S(1)}, u32[]{:S(2)}, u32[]{:S(2)}) %collective-permute-start.11) | collective-permute-done | bytes 524320 | tf_op jit(solution)/shard_map/ppermute | solution.py:24
  63.5 2.2 %collective-permute-start.13 = (bf16[2,256,256]{2,1,0:T(8,128)(2,1)S(1)}, bf16[2,256,256]{2,1,0:T(8,128)(2,1)S(1)}, u32[]{:S(2)}, u32[]{:S(2)}) collective-permute-start(bf16[2,256,256]{2,1,0:T(8,128)(2,1)S(1)} %slice.90), channel_id=1, source_target_pairs={{0,3},{1,0},{2,1},{3,2},{4,7},{5,4},{6,5},{7,6},{8,11},{9,8},{10,9... | collective-permute-start | bytes 786440 | tf_op jit(solution)/shard_map/ppermute | solution.py:26
  66.3 3.6 %collective-permute-done.13.refs_3_.refs_8_ = bf16[2,256,256]{2,1,0:T(8,128)(2,1)S(1)} collective-permute-done((bf16[2,256,256]{2,1,0:T(8,128)(2,1)S(1)}, bf16[2,256,256]{2,1,0:T(8,128)(2,1)S(1)}, u32[]{:S(2)}, u32[]{:S(2)}) %collective-permute-start.13) | collective-permute-done | bytes 262176 | tf_op jit(solution)/shard_map/ppermute | solution.py:26
  69.9 3.5 %collective-permute-done.14.refs_4_.refs_9_ = bf16[2,256,256]{2,1,0:T(8,128)(2,1)S(1)} collective-permute-done((bf16[2,256,256]{2,1,0:T(8,128)(2,1)S(1)}, bf16[2,256,256]{2,1,0:T(8,128)(2,1)S(1)}, u32[]{:S(2)}, u32[]{:S(2)}) %collective-permute-start.14) | collective-permute-done | bytes 262176 | tf_op jit(solution)/shard_map/ppermute | solution.py:27
  74.5 8.4 %collective-permute-start.17 = (bf16[2048,128]{1,0:T(8,128)(2,1)}, bf16[2048,128]{1,0:T(8,128)(2,1)}, u32[]{:S(2)}, u32[]{:S(2)}) collective-permute-start(bf16[2048,128]{1,0:T(8,128)(2,1)} %shard_map.20.here), channel_id=1, source_target_pairs={{0,64},{32,96},{64,0},{96,32},{1,65},{33,97},{65,1},{97,33},{2,66}... | collective-permute-start | bytes 1572872 | tf_op jit(solution)/shard_map/ppermute | solution.py:170
  82.9 2.0 %collective-permute-start.19 = (bf16[2,512,128]{2,1,0:T(8,128)(2,1)}, bf16[2,512,128]{2,1,0:T(8,128)(2,1)S(1)}, u32[]{:S(2)}, u32[]{:S(2)}) collective-permute-start(bf16[2,512,128]{2,1,0:T(8,128)(2,1)} %copy-done.25), channel_id=1, source_target_pairs={{0,1},{1,2},{2,3},{3,0},{4,5},{5,6},{6,7},{7,4},{8,9},{9,10},{10,1... | collective-permute-start | bytes 786440 | tf_op jit(solution)/shard_map/ppermute | solution.py:180
  92.2 3.7 %shard_map.23 = (f32[2,4,256,128]{3,2,1,0:T(8,128)S(1)}, f32[8,128]{1,0:T(8,128)S(1)}) custom-call(s32[3]{0:T(128)S(1)} %pad_add_fusion.place, bf16[2,512,256]{2,1,0:T(8,128)(2,1)S(1)} %dynamic-slice_bitcast_fusion.refs_0_, bf16[2,512,256]{2,1,0:T(8,128)(2,1)S(1)} %collective-permute-done.refs_1_, bf16[2,512,256]{2,1,0:T(8,128)(2,1)S(1)} %collective-permute-done.1.refs_2_, ...), custom_call_target="tpu_custom_call" | custom-call | flops 2147483648 | bytes 8388608 | tf_op jit(solution)/shard_map/pallas_call | solution.py:142
  96.0 1.3 shard_map.21.refs_10_
  97.7 3.7 %shard_map.25 = (f32[2,4,256,128]{3,2,1,0:T(8,128)S(1)}, f32[8,128]{1,0:T(8,128)S(1)}) custom-call(s32[3]{0:T(128)S(1)} %pad_add_fusion.place, bf16[2,512,256]{2,1,0:T(8,128)(2,1)S(1)} %dynamic-slice_bitcast_fusion.refs_0_, bf16[2,512,256]{2,1,0:T(8,128)(2,1)S(1)} %collective-permute-done.refs_1_, bf16[2,512,256]{2,1,0:T(8,128)(2,1)S(1)} %collective-permute-done.1.refs_2_, ...), custom_call_target="tpu_custom_call" | custom-call | flops 2147483648 | bytes 8388608 | tf_op jit(solution)/shard_map/pallas_call | solution.py:142
  101.4 3.7 %shard_map.24 = (f32[2,4,256,128]{3,2,1,0:T(8,128)S(1)}, f32[8,128]{1,0:T(8,128)S(1)}) custom-call(s32[3]{0:T(128)S(1)} %pad_add_fusion.place, bf16[2,512,256]{2,1,0:T(8,128)(2,1)S(1)} %dynamic-slice_bitcast_fusion.refs_0_, bf16[2,512,256]{2,1,0:T(8,128)(2,1)S(1)} %collective-permute-done.refs_1_, bf16[2,512,256]{2,1,0:T(8,128)(2,1)S(1)} %collective-permute-done.1.refs_2_, ...), custom_call_target="tpu_custom_call" | custom-call | flops 2147483648 | bytes 8388608 | tf_op jit(solution)/shard_map/pallas_call | solution.py:142
  105.1 4.1 %shard_map.26 = f32[32,264,128]{2,1,0:T(8,128)S(1)} custom-call(s32[3]{0:T(128)S(1)} %pad_add_fusion.place, bf16[2,512,256]{2,1,0:T(8,128)(2,1)S(1)} %dynamic-slice_bitcast_fusion.refs_0_, bf16[2,512,256]{2,1,0:T(8,128)(2,1)S(1)} %collective-permute-done.refs_1_, bf16[2,512,256]{2,1,0:T(8,128)(2,1)S(1)} %collective-permute-done.1.refs_2_, ...), custom_call_target="tpu_custom_call" | custom-call | flops 2147483648 | bytes 8388608 | tf_op jit(solution)/shard_map/pallas_call | solution.py:142
  109.2 1.7 convert_element_type.45
  110.9 10.2 %all-to-all-start = ((f16[32,264,128]{2,1,0:T(8,128)(2,1)}), f16[32,264,128]{2,1,0:T(8,128)(2,1)}, u32[]{:S(2)}, u32[]{:S(2)}) async-start(f16[32,264,128]{2,1,0:T(8,128)(2,1)} %convert_element_type.45), calls=%async_computation | async-start | bytes 4325376 | tf_op jit(solution)/shard_map/all_to_all | solution.py:199
  121.3 52.0 %all-to-all-done = f16[32,264,128]{2,1,0:T(8,128)(2,1)} async-done(((f16[32,264,128]{2,1,0:T(8,128)(2,1)}), f16[32,264,128]{2,1,0:T(8,128)(2,1)}, u32[]{:S(2)}, u32[]{:S(2)}) %all-to-all-start) | async-done | bytes 2162720 | tf_op jit(solution)/shard_map/all_to_all | solution.py:199
  173.3 2.1 %slice.92 = f16[32,256,128]{2,1,0:T(8,128)(2,1)S(1)} slice(f16[32,264,128]{2,1,0:T(8,128)(2,1)} %all-to-all-done), slice={[0:32], [0:256], [0:128]} | slice | bytes 4194304 | tf_op jit(solution)/shard_map/slice | solution.py:203
  175.4 1.5 fusion.14
  178.6 1.7 fusion.1
  (104 shorter events, 21.4 us)
Async XLA Ops:
  2.1 14.0 %collective-permute-start = (bf16[2,512,256]{2,1,0:T(8,128)(2,1)S(1)}, bf16[2,512,256]{2,1,0:T(8,128)(2,1)S(1)}, u32[]{:S(2)}, u32[]{:S(2)}) collective-permute-start(bf16[2,512,256]{2,1,0:T(8,128)(2,1)S(1)} %dynamic-slice_bitcast_fusion.refs_0_), channel_id=1, source_target_pairs={{0,3},{1,0},{2,1},{3,2},{4,7},{5,4},{6,5},{7,6},{8,11},{9,8},{10,9... | collective-permute-start | bytes 1572872 | tf_op jit(solution)/shard_map/ppermute | solution.py:24
  4.9 15.6 %collective-permute-start.1 = (bf16[2,512,256]{2,1,0:T(8,128)(2,1)S(1)}, bf16[2,512,256]{2,1,0:T(8,128)(2,1)S(1)}, u32[]{:S(2)}, u32[]{:S(2)}) collective-permute-start(bf16[2,512,256]{2,1,0:T(8,128)(2,1)S(1)} %dynamic-slice_bitcast_fusion.refs_0_), channel_id=1, source_target_pairs={{0,1},{1,2},{2,3},{3,0},{4,5},{5,6},{6,7},{7,4},{8,9},{9,10},{10,1... | collective-permute-start | bytes 1572872 | tf_op jit(solution)/shard_map/ppermute | solution.py:25
  4.9 23.5 %collective-permute-start.4 = (bf16[2,512,256]{2,1,0:T(8,128)(2,1)S(1)}, bf16[2,512,256]{2,1,0:T(8,128)(2,1)}, u32[]{:S(2)}, u32[]{:S(2)}) collective-permute-start(bf16[2,512,256]{2,1,0:T(8,128)(2,1)S(1)} %dynamic-slice_bitcast_fusion.refs_0_), channel_id=1, source_target_pairs={{0,96},{32,0},{64,32},{96,64},{1,97},{33,1},{65,33},{97,65},{2,98}... | collective-permute-start | bytes 1572872 | tf_op jit(solution)/shard_map/ppermute | solution.py:170
  5.4 23.1 %collective-permute-start.5 = (bf16[2,512,256]{2,1,0:T(8,128)(2,1)S(1)}, bf16[2,512,256]{2,1,0:T(8,128)(2,1)}, u32[]{:S(2)}, u32[]{:S(2)}) collective-permute-start(bf16[2,512,256]{2,1,0:T(8,128)(2,1)S(1)} %dynamic-slice_bitcast_fusion.refs_0_), channel_id=1, source_target_pairs={{0,32},{32,64},{64,96},{96,0},{1,33},{33,65},{65,97},{97,1},{2,34}... | collective-permute-start | bytes 1572872 | tf_op jit(solution)/shard_map/ppermute | solution.py:170
  16.8 13.9 %collective-permute-start.2 = (bf16[2,256,256]{2,1,0:T(8,128)(2,1)}, bf16[2,256,256]{2,1,0:T(8,128)(2,1)S(1)}, u32[]{:S(2)}, u32[]{:S(2)}) collective-permute-start(bf16[2,256,256]{2,1,0:T(8,128)(2,1)} %slice.88), channel_id=1, source_target_pairs={{0,3},{1,0},{2,1},{3,2},{4,7},{5,4},{6,5},{7,6},{8,11},{9,8},{10,9... | collective-permute-start | bytes 786440 | tf_op jit(solution)/shard_map/ppermute | solution.py:26
  21.3 9.5 %collective-permute-start.3 = (bf16[2,256,256]{2,1,0:T(8,128)(2,1)}, bf16[2,256,256]{2,1,0:T(8,128)(2,1)}, u32[]{:S(2)}, u32[]{:S(2)}) collective-permute-start(bf16[2,256,256]{2,1,0:T(8,128)(2,1)} %slice.89), channel_id=1, source_target_pairs={{0,1},{1,2},{2,3},{3,0},{4,5},{5,6},{6,7},{7,4},{8,9},{9,10},{10,1... | collective-permute-start | bytes 786440 | tf_op jit(solution)/shard_map/ppermute | solution.py:27
  21.3 20.4 %collective-permute-start.6 = (bf16[2,512,256]{2,1,0:T(8,128)(2,1)}, bf16[2,512,256]{2,1,0:T(8,128)(2,1)S(1)}, u32[]{:S(2)}, u32[]{:S(2)}) collective-permute-start(bf16[2,512,256]{2,1,0:T(8,128)(2,1)} %dynamic-slice_bitcast_fusion.1), channel_id=1, source_target_pairs={{0,128},{128,0},{1,129},{129,1},{2,130},{130,2},{3,131},{131,3},{4... | collective-permute-start | bytes 1572872 | tf_op jit(solution)/shard_map/ppermute | solution.py:167
  31.9 18.6 %collective-permute-start.10 = (bf16[2048,128]{1,0:T(8,128)(2,1)S(1)}, bf16[2048,128]{1,0:T(8,128)(2,1)S(1)}, u32[]{:S(2)}, u32[]{:S(2)}) collective-permute-start(bf16[2048,128]{1,0:T(8,128)(2,1)S(1)} %shard_map.18.here), channel_id=1, source_target_pairs={{0,64},{32,96},{64,0},{96,32},{1,65},{33,97},{65,1},{97,33},{2,66}... | collective-permute-start | bytes 1572872 | tf_op jit(solution)/shard_map/ppermute | solution.py:170
  33.2 12.7 %collective-permute-start.7 = (bf16[2,512,128]{2,1,0:T(8,128)(2,1)S(1)}, bf16[2,512,128]{2,1,0:T(8,128)(2,1)S(1)}, u32[]{:S(2)}, u32[]{:S(2)}) collective-permute-start(bf16[2,512,128]{2,1,0:T(8,128)(2,1)S(1)} %get-tuple-element.32), channel_id=1, source_target_pairs={{0,3},{1,0},{2,1},{3,2},{4,7},{5,4},{6,5},{7,6},{8,11},{9,8},{10,9... | collective-permute-start | bytes 786440 | tf_op jit(solution)/shard_map/ppermute | solution.py:180
  36.3 12.7 %collective-permute-start.8 = (bf16[2,512,128]{2,1,0:T(8,128)(2,1)S(1)}, bf16[2,512,128]{2,1,0:T(8,128)(2,1)S(1)}, u32[]{:S(2)}, u32[]{:S(2)}) collective-permute-start(bf16[2,512,128]{2,1,0:T(8,128)(2,1)S(1)} %get-tuple-element.33), channel_id=1, source_target_pairs={{0,1},{1,2},{2,3},{3,0},{4,5},{5,6},{6,7},{7,4},{8,9},{9,10},{10,1... | collective-permute-start | bytes 786440 | tf_op jit(solution)/shard_map/ppermute | solution.py:180
  36.3 13.4 %collective-permute-start.9 = (bf16[2,512,128]{2,1,0:T(8,128)(2,1)S(1)}, bf16[2,512,128]{2,1,0:T(8,128)(2,1)S(1)}, u32[]{:S(2)}, u32[]{:S(2)}) collective-permute-start(bf16[2,512,128]{2,1,0:T(8,128)(2,1)S(1)} %get-tuple-element.34), channel_id=1, source_target_pairs={{0,2},{1,3},{2,0},{3,1},{4,6},{5,7},{6,4},{7,5},{8,10},{9,11},{10,... | collective-permute-start | bytes 786440 | tf_op jit(solution)/shard_map/ppermute | solution.py:180
  41.7 8.0 %copy-start.3 = (bf16[2,512,256]{2,1,0:T(8,128)(2,1)}, bf16[2,512,256]{2,1,0:T(8,128)(2,1)S(1)}, u32[]{:S(2)}) copy-start(bf16[2,512,256]{2,1,0:T(8,128)(2,1)S(1)} %collective-permute-done.6.refs_0_.refs_5_) | copy-start | bytes 1572868
  51.3 22.2 %copy-start.4 = (bf16[2,512,256]{2,1,0:T(8,128)(2,1)S(1)}, bf16[2,512,256]{2,1,0:T(8,128)(2,1)}, u32[]{:S(2)}) copy-start(bf16[2,512,256]{2,1,0:T(8,128)(2,1)} %copy-done.3) | copy-start | bytes 1572868
  51.3 12.2 %collective-permute-start.11 = (bf16[2,512,256]{2,1,0:T(8,128)(2,1)}, bf16[2,512,256]{2,1,0:T(8,128)(2,1)S(1)}, u32[]{:S(2)}, u32[]{:S(2)}) collective-permute-start(bf16[2,512,256]{2,1,0:T(8,128)(2,1)} %copy-done.3), channel_id=1, source_target_pairs={{0,3},{1,0},{2,1},{3,2},{4,7},{5,4},{6,5},{7,6},{8,11},{9,8},{10,9... | collective-permute-start | bytes 1572872 | tf_op jit(solution)/shard_map/ppermute | solution.py:24
  52.5 13.3 %collective-permute-start.12 = (bf16[2,512,256]{2,1,0:T(8,128)(2,1)}, bf16[2,512,256]{2,1,0:T(8,128)(2,1)S(1)}, u32[]{:S(2)}, u32[]{:S(2)}) collective-permute-start(bf16[2,512,256]{2,1,0:T(8,128)(2,1)} %copy-done.3), channel_id=1, source_target_pairs={{0,1},{1,2},{2,3},{3,0},{4,5},{5,6},{6,7},{7,4},{8,9},{9,10},{10,1... | collective-permute-start | bytes 1572872 | tf_op jit(solution)/shard_map/ppermute | solution.py:25
  53.3 12.6 %collective-permute-start.15 = (bf16[2,512,256]{2,1,0:T(8,128)(2,1)}, bf16[2,512,256]{2,1,0:T(8,128)(2,1)S(1)}, u32[]{:S(2)}, u32[]{:S(2)}) collective-permute-start(bf16[2,512,256]{2,1,0:T(8,128)(2,1)} %copy-done.3), channel_id=1, source_target_pairs={{0,96},{32,0},{64,32},{96,64},{1,97},{33,1},{65,33},{97,65},{2,98}... | collective-permute-start | bytes 1572872 | tf_op jit(solution)/shard_map/ppermute | solution.py:170
  55.7 10.2 %collective-permute-start.16 = (bf16[2,512,256]{2,1,0:T(8,128)(2,1)}, bf16[2,512,256]{2,1,0:T(8,128)(2,1)S(1)}, u32[]{:S(2)}, u32[]{:S(2)}) collective-permute-start(bf16[2,512,256]{2,1,0:T(8,128)(2,1)} %copy-done.3), channel_id=1, source_target_pairs={{0,32},{32,64},{64,96},{96,0},{1,33},{33,65},{65,97},{97,1},{2,34}... | collective-permute-start | bytes 1572872 | tf_op jit(solution)/shard_map/ppermute | solution.py:170
  63.5 6.4 %collective-permute-start.13 = (bf16[2,256,256]{2,1,0:T(8,128)(2,1)S(1)}, bf16[2,256,256]{2,1,0:T(8,128)(2,1)S(1)}, u32[]{:S(2)}, u32[]{:S(2)}) collective-permute-start(bf16[2,256,256]{2,1,0:T(8,128)(2,1)S(1)} %slice.90), channel_id=1, source_target_pairs={{0,3},{1,0},{2,1},{3,2},{4,7},{5,4},{6,5},{7,6},{8,11},{9,8},{10,9... | collective-permute-start | bytes 786440 | tf_op jit(solution)/shard_map/ppermute | solution.py:26
  65.8 8.7 %copy-start.1 = (bf16[2,512,256]{2,1,0:T(8,128)(2,1)}, bf16[2,512,256]{2,1,0:T(8,128)(2,1)S(1)}, u32[]{:S(2)}) copy-start(bf16[2,512,256]{2,1,0:T(8,128)(2,1)S(1)} %collective-permute-done.12.refs_2_.refs_7_) | copy-start | bytes 1572868
  65.8 7.7 %collective-permute-start.14 = (bf16[2,256,256]{2,1,0:T(8,128)(2,1)S(1)}, bf16[2,256,256]{2,1,0:T(8,128)(2,1)S(1)}, u32[]{:S(2)}, u32[]{:S(2)}) collective-permute-start(bf16[2,256,256]{2,1,0:T(8,128)(2,1)S(1)} %slice.91), channel_id=1, source_target_pairs={{0,1},{1,2},{2,3},{3,0},{4,5},{5,6},{6,7},{7,4},{8,9},{9,10},{10,1... | collective-permute-start | bytes 786440 | tf_op jit(solution)/shard_map/ppermute | solution.py:27
  66.3 8.2 %copy-start.22 = (bf16[2,512,128]{2,1,0:T(8,128)(2,1)}, bf16[2,512,128]{2,1,0:T(8,128)(2,1)S(1)}, u32[]{:S(2)}) copy-start(bf16[2,512,128]{2,1,0:T(8,128)(2,1)S(1)} %get-tuple-element.36.refs_0_) | copy-start | bytes 786436
  66.3 8.2 %copy-start.24 = (bf16[2,512,128]{2,1,0:T(8,128)(2,1)}, bf16[2,512,128]{2,1,0:T(8,128)(2,1)S(1)}, u32[]{:S(2)}) copy-start(bf16[2,512,128]{2,1,0:T(8,128)(2,1)S(1)} %get-tuple-element.41) | copy-start | bytes 786436
  66.3 8.2 %copy-start.25 = (bf16[2,512,128]{2,1,0:T(8,128)(2,1)}, bf16[2,512,128]{2,1,0:T(8,128)(2,1)S(1)}, u32[]{:S(2)}) copy-start(bf16[2,512,128]{2,1,0:T(8,128)(2,1)S(1)} %get-tuple-element.40) | copy-start | bytes 786436
  66.3 8.2 %copy-start.26 = (bf16[2,512,128]{2,1,0:T(8,128)(2,1)}, bf16[2,512,128]{2,1,0:T(8,128)(2,1)S(1)}, u32[]{:S(2)}) copy-start(bf16[2,512,128]{2,1,0:T(8,128)(2,1)S(1)} %get-tuple-element.39) | copy-start | bytes 786436
  74.5 21.5 %collective-permute-start.17 = (bf16[2048,128]{1,0:T(8,128)(2,1)}, bf16[2048,128]{1,0:T(8,128)(2,1)}, u32[]{:S(2)}, u32[]{:S(2)}) collective-permute-start(bf16[2048,128]{1,0:T(8,128)(2,1)} %shard_map.20.here), channel_id=1, source_target_pairs={{0,64},{32,96},{64,0},{96,32},{1,65},{33,97},{65,1},{97,33},{2,66}... | collective-permute-start | bytes 1572872 | tf_op jit(solution)/shard_map/ppermute | solution.py:170
  82.9 13.1 %collective-permute-start.18 = (bf16[2,512,128]{2,1,0:T(8,128)(2,1)}, bf16[2,512,128]{2,1,0:T(8,128)(2,1)S(1)}, u32[]{:S(2)}, u32[]{:S(2)}) collective-permute-start(bf16[2,512,128]{2,1,0:T(8,128)(2,1)} %copy-done.26), channel_id=1, source_target_pairs={{0,3},{1,0},{2,1},{3,2},{4,7},{5,4},{6,5},{7,6},{8,11},{9,8},{10,9... | collective-permute-start | bytes 786440 | tf_op jit(solution)/shard_map/ppermute | solution.py:180
  82.9 13.1 %collective-permute-start.19 = (bf16[2,512,128]{2,1,0:T(8,128)(2,1)}, bf16[2,512,128]{2,1,0:T(8,128)(2,1)S(1)}, u32[]{:S(2)}, u32[]{:S(2)}) collective-permute-start(bf16[2,512,128]{2,1,0:T(8,128)(2,1)} %copy-done.25), channel_id=1, source_target_pairs={{0,1},{1,2},{2,3},{3,0},{4,5},{5,6},{6,7},{7,4},{8,9},{9,10},{10,1... | collective-permute-start | bytes 786440 | tf_op jit(solution)/shard_map/ppermute | solution.py:180
  84.9 11.1 %collective-permute-start.20 = (bf16[2,512,128]{2,1,0:T(8,128)(2,1)}, bf16[2,512,128]{2,1,0:T(8,128)(2,1)S(1)}, u32[]{:S(2)}, u32[]{:S(2)}) collective-permute-start(bf16[2,512,128]{2,1,0:T(8,128)(2,1)} %copy-done.24), channel_id=1, source_target_pairs={{0,2},{1,3},{2,0},{3,1},{4,6},{5,7},{6,4},{7,5},{8,10},{9,11},{10,... | collective-permute-start | bytes 786440 | tf_op jit(solution)/shard_map/ppermute | solution.py:180
  91.1 4.9 %copy-start.23 = (bf16[2,512,128]{2,1,0:T(8,128)(2,1)S(1)}, bf16[2,512,128]{2,1,0:T(8,128)(2,1)}, u32[]{:S(2)}) copy-start(bf16[2,512,128]{2,1,0:T(8,128)(2,1)} %copy-done.22) | copy-start | bytes 786436
  91.1 10.3 %collective-permute-start.22 = (bf16[4,2048,128]{2,1,0:T(8,128)(2,1)S(1)}, bf16[4,2048,128]{2,1,0:T(8,128)(2,1)S(1)}, u32[]{:S(2)}, u32[]{:S(2)}) collective-permute-start(bf16[4,2048,128]{2,1,0:T(8,128)(2,1)S(1)} %shard_map.22.refs_10_), channel_id=1, source_target_pairs={{0,16},{16,0},{1,17},{17,1},{2,18},{18,2},{3,19},{19,3},{4,20},{20... | collective-permute-start | bytes 6291464 | tf_op jit(solution)/shard_map/ppermute | solution.py:173
  97.4 7.8 %collective-permute-start.21 = (bf16[4,2048,128]{2,1,0:T(8,128)(2,1)S(1)}, bf16[4,2048,128]{2,1,0:T(8,128)(2,1)S(1)}, u32[]{:S(2)}, u32[]{:S(2)}) collective-permute-start(bf16[4,2048,128]{2,1,0:T(8,128)(2,1)S(1)} %shard_map.21.refs_10_), channel_id=1, source_target_pairs={{0,16},{16,0},{1,17},{17,1},{2,18},{18,2},{3,19},{19,3},{4,20},{20... | collective-permute-start | bytes 6291464 | tf_op jit(solution)/shard_map/ppermute | solution.py:173
  110.9 62.4 %all-to-all-start = ((f16[32,264,128]{2,1,0:T(8,128)(2,1)}), f16[32,264,128]{2,1,0:T(8,128)(2,1)}, u32[]{:S(2)}, u32[]{:S(2)}) async-start(f16[32,264,128]{2,1,0:T(8,128)(2,1)} %convert_element_type.45), calls=%async_computation | async-start | bytes 4325376 | tf_op jit(solution)/shard_map/all_to_all | solution.py:199
  (19 other events, 22.1 us)

commit v2 on v1

--- a/solution.py
+++ b/solution.py
@@ -17,15 +17,6 @@
 
 def first_of(value, *after):
     return lax.optimization_barrier((value, *after))[0]
-
-
-def gather_x(block):
-    half = block.shape[1] // 2
-    above = lax.ppermute(block, "x", ring(4, -1))
-    below = lax.ppermute(block, "x", ring(4, 1))
-    far_a = lax.ppermute(above[:, :half], "x", ring(4, -1))
-    far_b = lax.ppermute(below[:, half:], "x", ring(4, 1))
-    return [block, above, below, far_a, far_b]
 
 
 def add_terms(place, *refs):
@@ -84,26 +75,43 @@
 
 
 def join_kernel(here, far, *refs):
-    out = refs[-1]
-    out[0], out[2] = here[...], far[...]
-    for i, ref in enumerate(refs[:-1]):
-        s = ref.shape[1]
-        out[1, i * s : (i + 1) * s], out[3, i * s : (i + 1) * s] = ref[0], ref[1]
+    *parts, out, done = refs
+    copies = [(here, out.at[0]), (far, out.at[2])]
+    for i, part in enumerate(parts):
+        where = pl.ds(i * part.shape[1], part.shape[1])
+        copies += [(part.at[0], out.at[1, where]), (part.at[1], out.at[3, where])]
+    copies = [pltpu.make_async_copy(*ends, done.at[i]) for i, ends in enumerate(copies)]
+    for copy in copies:
+        copy.start()
+    for copy in copies:
+        copy.wait()
 
 
 SPACE = pl.BlockSpec(memory_space=pltpu.VMEM)
+SMALL, LARGE = 52 * 2**20, 52 * 2**20
 SCALAR = pl.BlockSpec(memory_space=pltpu.SMEM)
-PARAMS = pltpu.CompilerParams(vmem_limit_bytes=40 * 2**20)
-
-
-def small_call(kernel, shapes, *operands, scalars=1):
-    size = sum(2 * a.size for a in operands[scalars:])
+
+
+def joined(shape, *parts):
+    anywhere = pl.BlockSpec(memory_space=pl.ANY)
+    return pl.pallas_call(
+        join_kernel,
+        out_shape=shape,
+        in_specs=[anywhere] * len(parts),
+        out_specs=anywhere,
+        scratch_shapes=[pltpu.SemaphoreType.DMA((2 * len(parts) - 2,))],
+        cost_estimate=pl.CostEstimate(flops=0, bytes_accessed=4 * sum(a.size for a in parts), transcendentals=0),
+    )(*parts)
+
+
+def small_call(kernel, shapes, *operands):
+    size = sum(2 * a.size for a in operands[1:])
     return pl.pallas_call(
         kernel,
         out_shape=shapes,
-        in_specs=[SCALAR] * scalars + [SPACE] * (len(operands) - scalars),
+        in_specs=[SCALAR] + [SPACE] * (len(operands) - 1),
         out_specs=jax.tree.map(lambda _: SPACE, shapes),
-        compiler_params=PARAMS,
+        compiler_params=pltpu.CompilerParams(vmem_limit_bytes=SMALL),
         cost_estimate=pl.CostEstimate(flops=0, bytes_accessed=size, transcendentals=0),
     )(*operands)
 
@@ -114,7 +122,7 @@
     f, core = place[0], place[2]
     n, c = term3.shape[2:]
     largest = jnp.max(jnp.maximum(jnp.maximum(top0[...], top1[...]), jnp.maximum(top2[...], top3[...])))
-    power = jnp.clip(jnp.floor(jnp.log2(jnp.full((8, c), largest))), -100.0, 100.0)
+    power = jnp.clip(jnp.floor(jnp.log2(jnp.full((16, c), largest))), -100.0, 100.0)
     factor = jnp.exp2(TOP - power[:1]) * (1.0 + pattern(n, c))
 
     def step(i, carry):
@@ -138,14 +146,14 @@
     else:
         kernel, operands = last_kernel, (place, *rows, cols, *others)
         scratch = [pltpu.VMEM(term, jnp.float32), pltpu.VMEM((8, c), jnp.float32)]
-        shapes = jax.ShapeDtypeStruct((32, n + 8, c), jnp.float32)
+        shapes = jax.ShapeDtypeStruct((32, n + 16, c), jnp.float32)
     return pl.pallas_call(
         kernel,
         out_shape=shapes,
         in_specs=[SCALAR] + [SPACE] * (len(operands) - 1),
         out_specs=SPACE if others else (SPACE, SPACE),
         scratch_shapes=scratch,
-        compiler_params=PARAMS,
+        compiler_params=pltpu.CompilerParams(vmem_limit_bytes=LARGE),
         cost_estimate=pl.CostEstimate(flops=32 * n * cols.shape[1] * c, bytes_accessed=8 * 2**20, transcendentals=0),
     )(*operands)
 
@@ -172,22 +180,27 @@
     def from_core(piece):
         return lax.ppermute(piece, "core", ring(2, 1))
 
-    def gathered(block):
-        pieces = gather_x(block)
+    def gathered(block, *late):
+        shots = block.shape[1]
+        above, below = (lax.ppermute(block, "x", ring(4, step)) for step in (-1, 1))
         near = [from_y(block, 1), from_y(block, 3)]
-        cut = jax.ShapeDtypeStruct((2, block.shape[1], 2 * group), block.dtype)
+        near = lax.optimization_barrier((*near, above, below))[:2]
+        cut = jax.ShapeDtypeStruct((2, shots, 2 * group), block.dtype)
         kept, *sent = small_call(near_kernel, (cut,) * 4, x[None], *near)
         moved = [lax.ppermute(part, "x", ring(4, step)) for part, step in zip(sent, (-1, 1, 2))]
-        here = jax.ShapeDtypeStruct((4 * block.shape[1], 2 * group), block.dtype)
-        pieces[3:] = lax.optimization_barrier((*pieces[3:], kept))[:2]
+        far_a = lax.ppermute(above[:, : shots // 2], "x", ring(4, -1))
+        far_b = lax.ppermute(below[:, shots // 2 :], "x", ring(4, 1))
+        far_a, far_b = lax.optimization_barrier((far_a, far_b, kept, *late))[:2]
+        pieces = [block, above, below, far_a, far_b]
+        here = jax.ShapeDtypeStruct((4 * shots, 2 * group), block.dtype)
         here = small_call(own_kernel, here, x[None], *pieces)
         far = from_y(here, 2)
         cols = jax.ShapeDtypeStruct((4, *here.shape), block.dtype)
-        cols = small_call(join_kernel, cols, here, far, kept, *moved, scalars=0)
-        return pieces, cols, [*pieces[3:], *near, *moved, far]
-
-    rows0, mine0, done0 = gathered(own)
-    rows1, mine1, _ = gathered(first_of(other, *done0))
+        cols = joined(cols, here, far, kept, *moved)
+        return pieces, cols, moved
+
+    rows0, mine0, moved0 = gathered(own, other)
+    rows1, mine1, _ = gathered(first_of(other, *moved0))
     rows = (*rows0, *rows1)
 
     place = jnp.stack([f, y, core])
@@ -199,16 +212,15 @@
     got = lax.all_to_all(sent, ("zh", "zl", "x"), 0, 0, tiled=True)
 
     weight = jnp.exp2(got[:, n, 0].astype(jnp.float32) - TOP) * scale
-    weight = weight.reshape(2, 4, 4, 1, 1)
-    got = got[:, :n].reshape(2, 4, 4, n, 2 * group)
-    values = sum(got[:, i].astype(jnp.float32) * weight[:, i] for i in range(4)) * (1.0 - pattern(n, 2 * group))
-    return jnp.stack(
-        [
-            jnp.concatenate([values[:, i, :, p * group : (p + 1) * group] for i in range(4)], -1)
-            for p in range(2)
-        ],
-        1,
-    )
+    undo = 1.0 - pattern(n, 2 * group)
+
+    def owned(frequency, place):
+        picked = [frequency * 16 + i * 4 + place for i in range(4)]
+        return sum(got[i, :n].astype(jnp.float32) * weight[i] for i in picked) * undo
+
+    values = [[owned(frequency, place) for place in range(4)] for frequency in range(2)]
+    parts = [slice(p * group, (p + 1) * group) for p in range(2)]
+    return jnp.stack([jnp.stack([jnp.concatenate([v[:, part] for v in row], -1) for part in parts]) for row in values])
 
 
 def solution(mesh):

time: 185 us -> 331 us (1.79)
  Pallas kernels: 20.9 us -> 162 us
  other arithmetic: 6.28 us -> 26.7 us
  local copies, waits for them, and re-layouts: 19.5 us -> 8.79 us
    pallas_call x6, Pallas kernels: 5.62 us -> 136 us  [the longest x2 129 us: joined(): pl.pallas_call(join_kernel, out_shape=shape, in_specs=[anywhere] * len(pa...]
    mul x1 -> x4, other arithmetic: 1.71 us -> 20.8 us  [owned(): sum((got[i, :n].astype(jnp.float32) * weight[i] for i in picked)) * undo]
    pallas_call x4, Pallas kernels: 15.2 us -> 26.4 us  [terms_of(): pl.pallas_call(kernel, out_shape=shapes, in_specs=[SCALAR] + [SPACE] * (l...]
    ppermute x8, waiting for transfers between devices: 24.1 us -> 16.4 us  [the longest x4 12.2 us: gathered(): above, below = (lax.ppermute(block, 'x', ring(4, step)) for step in (-1, 1))]
    unnamed x54 -> x46, local copies, waits for them, and re-layouts: 12.6 us -> 5.1 us
    ppermute x6, starting transfers between devices: 13.2 us -> 8.33 us  [from_y(): return lax.ppermute(block, 'y', ring(4, -step))]
    ppermute x6, waiting for transfers between devices: 0.02 us -> 4.53 us  [from_y(): return lax.ppermute(block, 'y', ring(4, -step))]
  transfers between devices with their start and end apart: 24 -> 24, of which waited for: 9 -> 11; matrix products, arithmetic and copies ran while one was open for 1% -> 0% of each run, Pallas kernels for 9% -> 47%
where the time goes in v2:
time: 331 us; the launch traced here: 329 us
  Pallas kernels  162 us (49%)
  waiting for transfers between devices  85.5 us (26%)
  starting transfers between devices  45.3 us (14%)
  other arithmetic  26.7 us (8%)
  local copies, waits for them, and re-layouts  8.79 us (3%)
    pallas_call x2, Pallas kernels, joined(): pl.pallas_call(join_kernel, out_shape=shape, in_specs=[anywhere] * len(pa...  129 us
    all_to_all x1, waiting for transfers between devices, body(): got = lax.all_to_all(sent, ('zh', 'zl', 'x'), 0, 0, tiled=True)  53.1 us
    pallas_call x4, Pallas kernels, terms_of(): pl.pallas_call(kernel, out_shape=shapes, in_specs=[SCALAR] + [SPACE] * (l...  26.4 us
    mul x4, other arithmetic, owned(): sum((got[i, :n].astype(jnp.float32) * weight[i] for i in picked)) * undo  20.8 us
    ppermute x4, waiting for transfers between devices, gathered(): above, below = (lax.ppermute(block, 'x', ring(4, step)) for step in (-1, 1))  12.2 us
    all_to_all x1, starting transfers between devices, body(): got = lax.all_to_all(sent, ('zh', 'zl', 'x'), 0, 0, tiled=True)  12.1 us
    ppermute x6, starting transfers between devices, from_y(): return lax.ppermute(block, 'y', ring(4, -step))  8.33 us
    ppermute x6, waiting for transfers between devices, gathered(): lax.ppermute(part, 'x', ring(4, step))  8.26 us
  transfers between devices with their start and end apart: 24, of which 11 were waited for; matrix products, arithmetic and copies ran while one was open for 0% of the time, Pallas kernels for 47%

profile of v2, /device:TPU:16, one launch (start us, length us, event | category | flops | bytes accessed | tf_op | source)
XLA Modules:
  0.0 328.7 jit_solution(12548144283896800618)
XLA Ops:
  2.1 2.8 collective-permute-start
  5.4 1.6 collective-permute-start.5
  7.0 7.2 %collective-permute-start.6 = (bf16[2,512,256]{2,1,0:T(8,128)(2,1)}, bf16[2,512,256]{2,1,0:T(8,128)(2,1)S(1)}, u32[]{:S(2)}, u32[]{:S(2)}) collective-permute-start(bf16[2,512,256]{2,1,0:T(8,128)(2,1)} %dynamic-slice_bitcast_fusion.1), channel_id=1, source_target_pairs={{0,128},{128,0},{1,129},{129,1},{2,130},{130,2},{3,131},{131,3},{4... | collective-permute-start | bytes 1572872 | tf_op jit(solution)/shard_map/ppermute | solution.py:175
  14.1 2.0 collective-permute-done.refs_1_
  16.1 3.5 %collective-permute-done.1.refs_2_ = bf16[2,512,256]{2,1,0:T(8,128)(2,1)} collective-permute-done((bf16[2,512,256]{2,1,0:T(8,128)(2,1)S(1)}, bf16[2,512,256]{2,1,0:T(8,128)(2,1)}, u32[]{:S(2)}, u32[]{:S(2)}) %collective-permute-start.1) | collective-permute-done | bytes 524320 | tf_op jit(solution)/shard_map/ppermute | solution.py:185
  21.1 2.0 collective-permute-start.7
  24.6 3.1 collective-permute-done.6.refs_0_.refs_5_
  27.7 2.7 collective-permute-done.7.refs_1_
  30.4 5.6 %collective-permute-done.8.refs_2_ = bf16[2,512,128]{2,1,0:T(8,128)(2,1)S(1)} collective-permute-done((bf16[2,512,128]{2,1,0:T(8,128)(2,1)S(1)}, bf16[2,512,128]{2,1,0:T(8,128)(2,1)S(1)}, u32[]{:S(2)}, u32[]{:S(2)}) %collective-permute-start.8) | collective-permute-done | bytes 262176 | tf_op jit(solution)/shard_map/ppermute | solution.py:190
  36.3 1.8 collective-permute-start.11
  38.1 1.9 collective-permute-start.14
  40.5 1.6 collective-permute-start.2
  43.0 5.6 %collective-permute-done.10.refs_1_.refs_6_ = bf16[2,512,256]{2,1,0:T(8,128)(2,1)S(1)} collective-permute-done((bf16[2,512,256]{2,1,0:T(8,128)(2,1)S(1)}, bf16[2,512,256]{2,1,0:T(8,128)(2,1)S(1)}, u32[]{:S(2)}, u32[]{:S(2)}) %collective-permute-start.10) | collective-permute-done | bytes 524320 | tf_op jit(solution)/shard_map/ppermute | solution.py:185
  50.8 1.9 collective-permute-start.12
  54.8 3.2 collective-permute-done.3.refs_4_
  57.9 1.5 shard_map.21.here
  59.5 3.8 %collective-permute-start.20 = (bf16[2048,128]{1,0:T(8,128)(2,1)S(1)}, bf16[2048,128]{1,0:T(8,128)(2,1)}, u32[]{:S(2)}, u32[]{:S(2)}) collective-permute-start(bf16[2048,128]{1,0:T(8,128)(2,1)S(1)} %shard_map.21.here), channel_id=1, source_target_pairs={{0,64},{32,96},{64,0},{96,32},{1,65},{33,97},{65,1},{97,33},{2,66}... | collective-permute-start | bytes 1572872 | tf_op jit(solution)/shard_map/ppermute | solution.py:178
  66.3 1.8 shard_map.19.here
  71.3 4.5 %collective-permute-done.20.far = bf16[2048,128]{1,0:T(8,128)(2,1)} collective-permute-done((bf16[2048,128]{1,0:T(8,128)(2,1)S(1)}, bf16[2048,128]{1,0:T(8,128)(2,1)}, u32[]{:S(2)}, u32[]{:S(2)}) %collective-permute-start.20) | collective-permute-done | bytes 524320 | tf_op jit(solution)/shard_map/ppermute | solution.py:178
  75.8 64.7 %shard_map.22.refs_10_ = bf16[4,2048,128]{2,1,0:T(8,128)(2,1)} custom-call(bf16[2048,128]{1,0:T(8,128)(2,1)} %copy-done.2, bf16[2048,128]{1,0:T(8,128)(2,1)} %collective-permute-done.20.far, bf16[2,512,128]{2,1,0:T(8,128)(2,1)} %copy-done.10, bf16[2,512,128]{2,1,0:T(8,128)(2,1)} %copy-done.20, bf16[2,512,128]{2,1,0:T(8,128)(2,1)} %copy-done.21, ...), custom_call_target="tpu_custom_call" | custom-call | bytes 4194304 | tf_op jit(solution)/shard_map/pallas_call | solution.py:97
  141.6 6.0 %shard_map.23 = (f32[2,4,256,128]{3,2,1,0:T(8,128)}, f32[8,128]{1,0:T(8,128)S(1)}) custom-call(s32[3]{0:T(128)S(1)} %pad_add_fusion.place, bf16[2,512,256]{2,1,0:T(8,128)(2,1)S(1)} %dynamic-slice_bitcast_fusion.refs_0_, bf16[2,512,256]{2,1,0:T(8,128)(2,1)} %copy-done.15, bf16[2,512,256]{2,1,0:T(8,128)(2,1)} %collective-permute-done.1.refs_2_, ...), custom_call_target="tpu_custom_call" | custom-call | flops 2147483648 | bytes 8388608 | tf_op jit(solution)/shard_map/pallas_call | solution.py:150
  147.6 64.7 %shard_map.20.refs_10_ = bf16[4,2048,128]{2,1,0:T(8,128)(2,1)} custom-call(bf16[2048,128]{1,0:T(8,128)(2,1)} %copy-done.3, bf16[2048,128]{1,0:T(8,128)(2,1)} %collective-permute-done.16.far, bf16[2,512,128]{2,1,0:T(8,128)(2,1)} %copy-done.11, bf16[2,512,128]{2,1,0:T(8,128)(2,1)} %collective-permute-done.17.refs_1_, ...), custom_call_target="tpu_custom_call" | custom-call | bytes 4194304 | tf_op jit(solution)/shard_map/pallas_call | solution.py:97
  213.2 6.0 %shard_map.25 = (f32[2,4,256,128]{3,2,1,0:T(8,128)}, f32[8,128]{1,0:T(8,128)S(1)}) custom-call(s32[3]{0:T(128)S(1)} %pad_add_fusion.place, bf16[2,512,256]{2,1,0:T(8,128)(2,1)S(1)} %dynamic-slice_bitcast_fusion.refs_0_, bf16[2,512,256]{2,1,0:T(8,128)(2,1)} %copy-done.15, bf16[2,512,256]{2,1,0:T(8,128)(2,1)} %collective-permute-done.1.refs_2_, ...), custom_call_target="tpu_custom_call" | custom-call | flops 2147483648 | bytes 8388608 | tf_op jit(solution)/shard_map/pallas_call | solution.py:150
  219.2 6.1 %shard_map.24 = (f32[2,4,256,128]{3,2,1,0:T(8,128)}, f32[8,128]{1,0:T(8,128)S(1)}) custom-call(s32[3]{0:T(128)S(1)} %pad_add_fusion.place, bf16[2,512,256]{2,1,0:T(8,128)(2,1)S(1)} %dynamic-slice_bitcast_fusion.refs_0_, bf16[2,512,256]{2,1,0:T(8,128)(2,1)} %copy-done.15, bf16[2,512,256]{2,1,0:T(8,128)(2,1)} %collective-permute-done.1.refs_2_, ...), custom_call_target="tpu_custom_call" | custom-call | flops 2147483648 | bytes 8388608 | tf_op jit(solution)/shard_map/pallas_call | solution.py:150
  226.6 8.4 %shard_map.26 = f32[32,272,128]{2,1,0:T(8,128)} custom-call(s32[3]{0:T(128)S(1)} %pad_add_fusion.place, bf16[2,512,256]{2,1,0:T(8,128)(2,1)S(1)} %dynamic-slice_bitcast_fusion.refs_0_, bf16[2,512,256]{2,1,0:T(8,128)(2,1)} %copy-done.15, bf16[2,512,256]{2,1,0:T(8,128)(2,1)} %collective-permute-done.1.refs_2_, ...), custom_call_target="tpu_custom_call" | custom-call | flops 2147483648 | bytes 8388608 | tf_op jit(solution)/shard_map/pallas_call | solution.py:150
  235.0 4.0 %convert_element_type.152 = f16[32,272,128]{2,1,0:T(8,128)(2,1)} convert(f32[32,272,128]{2,1,0:T(8,128)} %shard_map.26) | non-fusion elementwise | flops 1114112 | bytes 6684672 | tf_op jit(solution)/shard_map/convert_element_type | solution.py:211
  239.0 12.1 %all-to-all-start = ((f16[32,272,128]{2,1,0:T(8,128)(2,1)}), f16[32,272,128]{2,1,0:T(8,128)(2,1)S(1)}, u32[]{:S(2)}, u32[]{:S(2)}) async-start(f16[32,272,128]{2,1,0:T(8,128)(2,1)} %convert_element_type.152), calls=%async_computation | async-start | bytes 4456448 | tf_op jit(solution)/shard_map/all_to_all | solution.py:212
  251.1 53.1 %all-to-all-done = f16[32,272,128]{2,1,0:T(8,128)(2,1)S(1)} async-done(((f16[32,272,128]{2,1,0:T(8,128)(2,1)}), f16[32,272,128]{2,1,0:T(8,128)(2,1)S(1)}, u32[]{:S(2)}, u32[]{:S(2)}) %all-to-all-start) | async-done | bytes 2228256 | tf_op jit(solution)/shard_map/all_to_all | solution.py:212
  305.5 5.3 %bitcast_multiply_fusion.7 = (f32[256,128]{1,0:T(8,128)S(1)}, f32[256,128]{1,0:T(8,128)S(1)}) fusion(f16[32,272,128]{2,1,0:T(8,128)(2,1)S(1)} %all-to-all-done, s32[128]{0:T(128)S(1)} %iota_multiply_fusion.1, s32[256]{0:T(256)S(1)} %iota_multiply_fusion, f32[]{:T(128)} %bitcast.9, f32[]{:T(128)} %bitcast.8, f32[]{:T(128)} %bitcast.7, f32[]{:T(128)} %bitcast.6, ...), kind=kLoop, calls=%fused_computation.26 | loop fusion | flops 1310720 | bytes 788000 | tf_op jit(solution)/shard_map/mul | solution.py:219
  310.9 5.1 %bitcast_multiply_fusion.5 = (f32[256,128]{1,0:T(8,128)S(1)}, f32[256,128]{1,0:T(8,128)S(1)}) fusion(f16[32,272,128]{2,1,0:T(8,128)(2,1)S(1)} %all-to-all-done, f32[]{:T(128)} %bitcast.19, f32[]{:T(128)} %bitcast.18, f32[]{:T(128)} %bitcast.17, f32[]{:T(128)} %bitcast.16, s32[128]{0:T(128)S(1)} %iota_multiply_fusion.1, s32[256]{0:T(256)S(1)} %iota_multiply_fusion, ...), kind=kLoop, calls=%fused_computation.24 | loop fusion | flops 1310720 | bytes 788000 | tf_op jit(solution)/shard_map/mul | solution.py:219
  316.2 5.2 %bitcast_multiply_fusion.4 = (f32[256,128]{1,0:T(8,128)S(1)}, f32[256,128]{1,0:T(8,128)S(1)}) fusion(f16[32,272,128]{2,1,0:T(8,128)(2,1)S(1)} %all-to-all-done, f32[]{:T(128)} %bitcast.24, f32[]{:T(128)} %bitcast.23, f32[]{:T(128)} %bitcast.22, f32[]{:T(128)} %bitcast.21, s32[128]{0:T(128)S(1)} %iota_multiply_fusion.1, s32[256]{0:T(256)S(1)} %iota_multiply_fusion, ...), kind=kLoop, calls=%fused_computation.23 | loop fusion | flops 1310720 | bytes 788000 | tf_op jit(solution)/shard_map/mul | solution.py:219
  321.9 5.2 %bitcast_multiply_fusion.3 = (f32[256,128]{1,0:T(8,128)S(1)}, f32[256,128]{1,0:T(8,128)S(1)}) fusion(f16[32,272,128]{2,1,0:T(8,128)(2,1)S(1)} %all-to-all-done, f32[]{:T(128)} %bitcast.32, f32[]{:T(128)} %bitcast.31, f32[]{:T(128)} %bitcast.30, f32[]{:T(128)} %bitcast.29, s32[128]{0:T(128)S(1)} %iota_multiply_fusion.1, s32[256]{0:T(256)S(1)} %iota_multiply_fusion, ...), kind=kLoop, calls=%fused_computation.22 | loop fusion | flops 1310720 | bytes 788000 | tf_op jit(solution)/shard_map/mul | solution.py:219
  (100 shorter events, 24.5 us)
Async XLA Ops:
  2.1 14.0 %collective-permute-start = (bf16[2,512,256]{2,1,0:T(8,128)(2,1)S(1)}, bf16[2,512,256]{2,1,0:T(8,128)(2,1)S(1)}, u32[]{:S(2)}, u32[]{:S(2)}) collective-permute-start(bf16[2,512,256]{2,1,0:T(8,128)(2,1)S(1)} %dynamic-slice_bitcast_fusion.refs_0_), channel_id=1, source_target_pairs={{0,3},{1,0},{2,1},{3,2},{4,7},{5,4},{6,5},{7,6},{8,11},{9,8},{10,9... | collective-permute-start | bytes 1572872 | tf_op jit(solution)/shard_map/ppermute | solution.py:185
  4.9 14.7 %collective-permute-start.1 = (bf16[2,512,256]{2,1,0:T(8,128)(2,1)S(1)}, bf16[2,512,256]{2,1,0:T(8,128)(2,1)}, u32[]{:S(2)}, u32[]{:S(2)}) collective-permute-start(bf16[2,512,256]{2,1,0:T(8,128)(2,1)S(1)} %dynamic-slice_bitcast_fusion.refs_0_), channel_id=1, source_target_pairs={{0,1},{1,2},{2,3},{3,0},{4,5},{5,6},{6,7},{7,4},{8,9},{9,10},{10,1... | collective-permute-start | bytes 1572872 | tf_op jit(solution)/shard_map/ppermute | solution.py:185
  4.9 14.7 %collective-permute-start.4 = (bf16[2,512,256]{2,1,0:T(8,128)(2,1)S(1)}, bf16[2,512,256]{2,1,0:T(8,128)(2,1)S(1)}, u32[]{:S(2)}, u32[]{:S(2)}) collective-permute-start(bf16[2,512,256]{2,1,0:T(8,128)(2,1)S(1)} %dynamic-slice_bitcast_fusion.refs_0_), channel_id=1, source_target_pairs={{0,96},{32,0},{64,32},{96,64},{1,97},{33,1},{65,33},{97,65},{2,98}... | collective-permute-start | bytes 1572872 | tf_op jit(solution)/shard_map/ppermute | solution.py:178
  5.4 14.3 %collective-permute-start.5 = (bf16[2,512,256]{2,1,0:T(8,128)(2,1)S(1)}, bf16[2,512,256]{2,1,0:T(8,128)(2,1)}, u32[]{:S(2)}, u32[]{:S(2)}) collective-permute-start(bf16[2,512,256]{2,1,0:T(8,128)(2,1)S(1)} %dynamic-slice_bitcast_fusion.refs_0_), channel_id=1, source_target_pairs={{0,32},{32,64},{64,96},{96,0},{1,33},{33,65},{65,97},{97,1},{2,34}... | collective-permute-start | bytes 1572872 | tf_op jit(solution)/shard_map/ppermute | solution.py:178
  7.0 20.7 %collective-permute-start.6 = (bf16[2,512,256]{2,1,0:T(8,128)(2,1)}, bf16[2,512,256]{2,1,0:T(8,128)(2,1)S(1)}, u32[]{:S(2)}, u32[]{:S(2)}) collective-permute-start(bf16[2,512,256]{2,1,0:T(8,128)(2,1)} %dynamic-slice_bitcast_fusion.1), channel_id=1, source_target_pairs={{0,128},{128,0},{1,129},{129,1},{2,130},{130,2},{3,131},{131,3},{4... | collective-permute-start | bytes 1572872 | tf_op jit(solution)/shard_map/ppermute | solution.py:175
  16.1 41.8 %copy-start.15 = (bf16[2,512,256]{2,1,0:T(8,128)(2,1)}, bf16[2,512,256]{2,1,0:T(8,128)(2,1)S(1)}, u32[]{:S(2)}) copy-start(bf16[2,512,256]{2,1,0:T(8,128)(2,1)S(1)} %collective-permute-done.refs_1_) | copy-start | bytes 1572868
  21.0 38.4 %copy-start.10 = (bf16[2,512,128]{2,1,0:T(8,128)(2,1)}, bf16[2,512,128]{2,1,0:T(8,128)(2,1)S(1)}, u32[]{:S(2)}) copy-start(bf16[2,512,128]{2,1,0:T(8,128)(2,1)S(1)} %get-tuple-element.35.refs_0_) | copy-start | bytes 786436
  21.1 9.3 %collective-permute-start.7 = (bf16[2,512,128]{2,1,0:T(8,128)(2,1)S(1)}, bf16[2,512,128]{2,1,0:T(8,128)(2,1)S(1)}, u32[]{:S(2)}, u32[]{:S(2)}) collective-permute-start(bf16[2,512,128]{2,1,0:T(8,128)(2,1)S(1)} %get-tuple-element.38), channel_id=1, source_target_pairs={{0,3},{1,0},{2,1},{3,2},{4,7},{5,4},{6,5},{7,6},{8,11},{9,8},{10,9... | collective-permute-start | bytes 786440 | tf_op jit(solution)/shard_map/ppermute | solution.py:190
  23.0 12.9 %collective-permute-start.8 = (bf16[2,512,128]{2,1,0:T(8,128)(2,1)S(1)}, bf16[2,512,128]{2,1,0:T(8,128)(2,1)S(1)}, u32[]{:S(2)}, u32[]{:S(2)}) collective-permute-start(bf16[2,512,128]{2,1,0:T(8,128)(2,1)S(1)} %get-tuple-element.39), channel_id=1, source_target_pairs={{0,1},{1,2},{2,3},{3,0},{4,5},{5,6},{6,7},{7,4},{8,9},{9,10},{10,1... | collective-permute-start | bytes 786440 | tf_op jit(solution)/shard_map/ppermute | solution.py:190
  23.2 12.8 %collective-permute-start.9 = (bf16[2,512,128]{2,1,0:T(8,128)(2,1)S(1)}, bf16[2,512,128]{2,1,0:T(8,128)(2,1)S(1)}, u32[]{:S(2)}, u32[]{:S(2)}) collective-permute-start(bf16[2,512,128]{2,1,0:T(8,128)(2,1)S(1)} %get-tuple-element.40), channel_id=1, source_target_pairs={{0,2},{1,3},{2,0},{3,1},{4,6},{5,7},{6,4},{7,5},{8,10},{9,11},{10,... | collective-permute-start | bytes 786440 | tf_op jit(solution)/shard_map/ppermute | solution.py:190
  27.7 38.5 %copy-start.1 = (bf16[2,512,256]{2,1,0:T(8,128)(2,1)}, bf16[2,512,256]{2,1,0:T(8,128)(2,1)S(1)}, u32[]{:S(2)}) copy-start(bf16[2,512,256]{2,1,0:T(8,128)(2,1)S(1)} %collective-permute-done.6.refs_0_.refs_5_) | copy-start | bytes 1572868
  30.4 27.6 %copy-start.20 = (bf16[2,512,128]{2,1,0:T(8,128)(2,1)}, bf16[2,512,128]{2,1,0:T(8,128)(2,1)S(1)}, u32[]{:S(2)}) copy-start(bf16[2,512,128]{2,1,0:T(8,128)(2,1)S(1)} %collective-permute-done.7.refs_1_) | copy-start | bytes 786436
  36.0 22.0 %copy-start.21 = (bf16[2,512,128]{2,1,0:T(8,128)(2,1)}, bf16[2,512,128]{2,1,0:T(8,128)(2,1)S(1)}, u32[]{:S(2)}) copy-start(bf16[2,512,128]{2,1,0:T(8,128)(2,1)S(1)} %collective-permute-done.8.refs_2_) | copy-start | bytes 786436
  36.0 12.7 %collective-permute-start.10 = (bf16[2,512,256]{2,1,0:T(8,128)(2,1)S(1)}, bf16[2,512,256]{2,1,0:T(8,128)(2,1)S(1)}, u32[]{:S(2)}, u32[]{:S(2)}) collective-permute-start(bf16[2,512,256]{2,1,0:T(8,128)(2,1)S(1)} %collective-permute-done.6.refs_0_.refs_5_), channel_id=1, source_target_pairs={{0,3},{1,0},{2,1},{3,2},{4,7},{5,4},{6,5},{7,6},{8,11},{9,8},{10,9... | collective-permute-start | bytes 1572872 | tf_op jit(solution)/shard_map/ppermute | solution.py:185
  36.3 14.5 %collective-permute-start.11 = (bf16[2,512,256]{2,1,0:T(8,128)(2,1)S(1)}, bf16[2,512,256]{2,1,0:T(8,128)(2,1)S(1)}, u32[]{:S(2)}, u32[]{:S(2)}) collective-permute-start(bf16[2,512,256]{2,1,0:T(8,128)(2,1)S(1)} %collective-permute-done.6.refs_0_.refs_5_), channel_id=1, source_target_pairs={{0,1},{1,2},{2,3},{3,0},{4,5},{5,6},{6,7},{7,4},{8,9},{9,10},{10,1... | collective-permute-start | bytes 1572872 | tf_op jit(solution)/shard_map/ppermute | solution.py:185
  38.1 25.2 %collective-permute-start.14 = (bf16[2,512,256]{2,1,0:T(8,128)(2,1)S(1)}, bf16[2,512,256]{2,1,0:T(8,128)(2,1)S(1)}, u32[]{:S(2)}, u32[]{:S(2)}) collective-permute-start(bf16[2,512,256]{2,1,0:T(8,128)(2,1)S(1)} %collective-permute-done.6.refs_0_.refs_5_), channel_id=1, source_target_pairs={{0,96},{32,0},{64,32},{96,64},{1,97},{33,1},{65,33},{97,65},{2,98}... | collective-permute-start | bytes 1572872 | tf_op jit(solution)/shard_map/ppermute | solution.py:178
  40.0 23.3 %collective-permute-start.15 = (bf16[2,512,256]{2,1,0:T(8,128)(2,1)S(1)}, bf16[2,512,256]{2,1,0:T(8,128)(2,1)S(1)}, u32[]{:S(2)}, u32[]{:S(2)}) collective-permute-start(bf16[2,512,256]{2,1,0:T(8,128)(2,1)S(1)} %collective-permute-done.6.refs_0_.refs_5_), channel_id=1, source_target_pairs={{0,32},{32,64},{64,96},{96,0},{1,33},{33,65},{65,97},{97,1},{2,34}... | collective-permute-start | bytes 1572872 | tf_op jit(solution)/shard_map/ppermute | solution.py:178
  40.5 13.3 %collective-permute-start.2 = (bf16[2,256,256]{2,1,0:T(8,128)(2,1)S(1)}, bf16[2,256,256]{2,1,0:T(8,128)(2,1)S(1)}, u32[]{:S(2)}, u32[]{:S(2)}) collective-permute-start(bf16[2,256,256]{2,1,0:T(8,128)(2,1)S(1)} %slice.372), channel_id=1, source_target_pairs={{0,3},{1,0},{2,1},{3,2},{4,7},{5,4},{6,5},{7,6},{8,11},{9,8},{10,9... | collective-permute-start | bytes 786440 | tf_op jit(solution)/shard_map/ppermute | solution.py:191
  48.7 9.3 %collective-permute-start.3 = (bf16[2,256,256]{2,1,0:T(8,128)(2,1)S(1)}, bf16[2,256,256]{2,1,0:T(8,128)(2,1)S(1)}, u32[]{:S(2)}, u32[]{:S(2)}) collective-permute-start(bf16[2,256,256]{2,1,0:T(8,128)(2,1)S(1)} %slice.373), channel_id=1, source_target_pairs={{0,1},{1,2},{2,3},{3,0},{4,5},{5,6},{6,7},{7,4},{8,9},{9,10},{10,1... | collective-permute-start | bytes 786440 | tf_op jit(solution)/shard_map/ppermute | solution.py:192
  50.8 15.4 %collective-permute-start.12 = (bf16[2,256,256]{2,1,0:T(8,128)(2,1)S(1)}, bf16[2,256,256]{2,1,0:T(8,128)(2,1)S(1)}, u32[]{:S(2)}, u32[]{:S(2)}) collective-permute-start(bf16[2,256,256]{2,1,0:T(8,128)(2,1)S(1)} %slice.374), channel_id=1, source_target_pairs={{0,3},{1,0},{2,1},{3,2},{4,7},{5,4},{6,5},{7,6},{8,11},{9,8},{10,9... | collective-permute-start | bytes 786440 | tf_op jit(solution)/shard_map/ppermute | solution.py:191
  53.8 12.4 %collective-permute-start.13 = (bf16[2,256,256]{2,1,0:T(8,128)(2,1)S(1)}, bf16[2,256,256]{2,1,0:T(8,128)(2,1)S(1)}, u32[]{:S(2)}, u32[]{:S(2)}) collective-permute-start(bf16[2,256,256]{2,1,0:T(8,128)(2,1)S(1)} %slice.375), channel_id=1, source_target_pairs={{0,1},{1,2},{2,3},{3,0},{4,5},{5,6},{6,7},{7,4},{8,9},{9,10},{10,1... | collective-permute-start | bytes 786440 | tf_op jit(solution)/shard_map/ppermute | solution.py:192
  59.5 16.3 %collective-permute-start.20 = (bf16[2048,128]{1,0:T(8,128)(2,1)S(1)}, bf16[2048,128]{1,0:T(8,128)(2,1)}, u32[]{:S(2)}, u32[]{:S(2)}) collective-permute-start(bf16[2048,128]{1,0:T(8,128)(2,1)S(1)} %shard_map.21.here), channel_id=1, source_target_pairs={{0,64},{32,96},{64,0},{96,32},{1,65},{33,97},{65,1},{97,33},{2,66}... | collective-permute-start | bytes 1572872 | tf_op jit(solution)/shard_map/ppermute | solution.py:178
  68.2 79.5 %copy-start.3 = (bf16[2048,128]{1,0:T(8,128)(2,1)}, bf16[2048,128]{1,0:T(8,128)(2,1)S(1)}, u32[]{:S(2)}) copy-start(bf16[2048,128]{1,0:T(8,128)(2,1)S(1)} %shard_map.19.here) | copy-start | bytes 1572868
  68.2 72.5 %copy-start.5 = (bf16[2,256,256]{2,1,0:T(8,128)(2,1)S(1)}, bf16[2,256,256]{2,1,0:T(8,128)(2,1)}, u32[]{:S(2)}) copy-start(bf16[2,256,256]{2,1,0:T(8,128)(2,1)} %copy-done.4) | copy-start | bytes 786436
  68.2 79.5 %collective-permute-start.16 = (bf16[2048,128]{1,0:T(8,128)(2,1)S(1)}, bf16[2048,128]{1,0:T(8,128)(2,1)}, u32[]{:S(2)}, u32[]{:S(2)}) collective-permute-start(bf16[2048,128]{1,0:T(8,128)(2,1)S(1)} %shard_map.19.here), channel_id=1, source_target_pairs={{0,64},{32,96},{64,0},{96,32},{1,65},{33,97},{65,1},{97,33},{2,66}... | collective-permute-start | bytes 1572872 | tf_op jit(solution)/shard_map/ppermute | solution.py:178
  68.3 72.4 %copy-start.7 = (bf16[2,256,256]{2,1,0:T(8,128)(2,1)S(1)}, bf16[2,256,256]{2,1,0:T(8,128)(2,1)}, u32[]{:S(2)}) copy-start(bf16[2,256,256]{2,1,0:T(8,128)(2,1)} %copy-done.6) | copy-start | bytes 786436
  68.3 79.3 %collective-permute-start.17 = (bf16[2,512,128]{2,1,0:T(8,128)(2,1)}, bf16[2,512,128]{2,1,0:T(8,128)(2,1)}, u32[]{:S(2)}, u32[]{:S(2)}) collective-permute-start(bf16[2,512,128]{2,1,0:T(8,128)(2,1)} %copy-done.14), channel_id=1, source_target_pairs={{0,3},{1,0},{2,1},{3,2},{4,7},{5,4},{6,5},{7,6},{8,11},{9,8},{10,9... | collective-permute-start | bytes 786440 | tf_op jit(solution)/shard_map/ppermute | solution.py:190
  69.8 77.8 %collective-permute-start.18 = (bf16[2,512,128]{2,1,0:T(8,128)(2,1)}, bf16[2,512,128]{2,1,0:T(8,128)(2,1)}, u32[]{:S(2)}, u32[]{:S(2)}) collective-permute-start(bf16[2,512,128]{2,1,0:T(8,128)(2,1)} %copy-done.13), channel_id=1, source_target_pairs={{0,1},{1,2},{2,3},{3,0},{4,5},{5,6},{6,7},{7,4},{8,9},{9,10},{10,1... | collective-permute-start | bytes 786440 | tf_op jit(solution)/shard_map/ppermute | solution.py:190
  70.4 77.2 %collective-permute-start.19 = (bf16[2,512,128]{2,1,0:T(8,128)(2,1)}, bf16[2,512,128]{2,1,0:T(8,128)(2,1)}, u32[]{:S(2)}, u32[]{:S(2)}) collective-permute-start(bf16[2,512,128]{2,1,0:T(8,128)(2,1)} %copy-done.12), channel_id=1, source_target_pairs={{0,2},{1,3},{2,0},{3,1},{4,6},{5,7},{6,4},{7,5},{8,10},{9,11},{10,... | collective-permute-start | bytes 786440 | tf_op jit(solution)/shard_map/ppermute | solution.py:190
  140.6 78.6 %collective-permute-start.22 = (bf16[4,2048,128]{2,1,0:T(8,128)(2,1)}, bf16[4,2048,128]{2,1,0:T(8,128)(2,1)}, u32[]{:S(2)}, u32[]{:S(2)}) collective-permute-start(bf16[4,2048,128]{2,1,0:T(8,128)(2,1)} %shard_map.22.refs_10_), channel_id=1, source_target_pairs={{0,16},{16,0},{1,17},{17,1},{2,18},{18,2},{3,19},{19,3},{4,20},{20... | collective-permute-start | bytes 6291464 | tf_op jit(solution)/shard_map/ppermute | solution.py:181
  212.4 12.9 %collective-permute-start.21 = (bf16[4,2048,128]{2,1,0:T(8,128)(2,1)}, bf16[4,2048,128]{2,1,0:T(8,128)(2,1)S(1)}, u32[]{:S(2)}, u32[]{:S(2)}) collective-permute-start(bf16[4,2048,128]{2,1,0:T(8,128)(2,1)} %shard_map.20.refs_10_), channel_id=1, source_target_pairs={{0,16},{16,0},{1,17},{17,1},{2,18},{18,2},{3,19},{19,3},{4,20},{20... | collective-permute-start | bytes 6291464 | tf_op jit(solution)/shard_map/ppermute | solution.py:181
  239.0 65.2 %all-to-all-start = ((f16[32,272,128]{2,1,0:T(8,128)(2,1)}), f16[32,272,128]{2,1,0:T(8,128)(2,1)S(1)}, u32[]{:S(2)}, u32[]{:S(2)}) async-start(f16[32,272,128]{2,1,0:T(8,128)(2,1)} %convert_element_type.152), calls=%async_computation | async-start | bytes 4456448 | tf_op jit(solution)/shard_map/all_to_all | solution.py:212
  (15 other events, 78.7 us)

commit v3 on v1

--- a/solution.py
+++ b/solution.py
@@ -17,15 +17,6 @@
 
 def first_of(value, *after):
     return lax.optimization_barrier((value, *after))[0]
-
-
-def gather_x(block):
-    half = block.shape[1] // 2
-    above = lax.ppermute(block, "x", ring(4, -1))
-    below = lax.ppermute(block, "x", ring(4, 1))
-    far_a = lax.ppermute(above[:, :half], "x", ring(4, -1))
-    far_b = lax.ppermute(below[:, half:], "x", ring(4, 1))
-    return [block, above, below, far_a, far_b]
 
 
 def add_terms(place, *refs):
@@ -92,8 +83,8 @@
 
 
 SPACE = pl.BlockSpec(memory_space=pltpu.VMEM)
+GRANT = 40 * 2**20
 SCALAR = pl.BlockSpec(memory_space=pltpu.SMEM)
-PARAMS = pltpu.CompilerParams(vmem_limit_bytes=40 * 2**20)
 
 
 def small_call(kernel, shapes, *operands, scalars=1):
@@ -103,7 +94,7 @@
         out_shape=shapes,
         in_specs=[SCALAR] * scalars + [SPACE] * (len(operands) - scalars),
         out_specs=jax.tree.map(lambda _: SPACE, shapes),
-        compiler_params=PARAMS,
+        compiler_params=pltpu.CompilerParams(vmem_limit_bytes=GRANT),
         cost_estimate=pl.CostEstimate(flops=0, bytes_accessed=size, transcendentals=0),
     )(*operands)
 
@@ -114,7 +105,7 @@
     f, core = place[0], place[2]
     n, c = term3.shape[2:]
     largest = jnp.max(jnp.maximum(jnp.maximum(top0[...], top1[...]), jnp.maximum(top2[...], top3[...])))
-    power = jnp.clip(jnp.floor(jnp.log2(jnp.full((8, c), largest))), -100.0, 100.0)
+    power = jnp.clip(jnp.floor(jnp.log2(jnp.full((16, c), largest))), -100.0, 100.0)
     factor = jnp.exp2(TOP - power[:1]) * (1.0 + pattern(n, c))
 
     def step(i, carry):
@@ -138,14 +129,14 @@
     else:
         kernel, operands = last_kernel, (place, *rows, cols, *others)
         scratch = [pltpu.VMEM(term, jnp.float32), pltpu.VMEM((8, c), jnp.float32)]
-        shapes = jax.ShapeDtypeStruct((32, n + 8, c), jnp.float32)
+        shapes = jax.ShapeDtypeStruct((32, n + 16, c), jnp.float32)
     return pl.pallas_call(
         kernel,
         out_shape=shapes,
         in_specs=[SCALAR] + [SPACE] * (len(operands) - 1),
         out_specs=SPACE if others else (SPACE, SPACE),
         scratch_shapes=scratch,
-        compiler_params=PARAMS,
+        compiler_params=pltpu.CompilerParams(vmem_limit_bytes=GRANT),
         cost_estimate=pl.CostEstimate(flops=32 * n * cols.shape[1] * c, bytes_accessed=8 * 2**20, transcendentals=0),
     )(*operands)
 
@@ -172,22 +163,27 @@
     def from_core(piece):
         return lax.ppermute(piece, "core", ring(2, 1))
 
-    def gathered(block):
-        pieces = gather_x(block)
+    def gathered(block, *late):
+        shots = block.shape[1]
+        above, below = (lax.ppermute(block, "x", ring(4, step)) for step in (-1, 1))
         near = [from_y(block, 1), from_y(block, 3)]
-        cut = jax.ShapeDtypeStruct((2, block.shape[1], 2 * group), block.dtype)
+        near = lax.optimization_barrier((*near, above, below))[:2]
+        cut = jax.ShapeDtypeStruct((2, shots, 2 * group), block.dtype)
         kept, *sent = small_call(near_kernel, (cut,) * 4, x[None], *near)
         moved = [lax.ppermute(part, "x", ring(4, step)) for part, step in zip(sent, (-1, 1, 2))]
-        here = jax.ShapeDtypeStruct((4 * block.shape[1], 2 * group), block.dtype)
-        pieces[3:] = lax.optimization_barrier((*pieces[3:], kept))[:2]
+        far_a = lax.ppermute(above[:, : shots // 2], "x", ring(4, -1))
+        far_b = lax.ppermute(below[:, shots // 2 :], "x", ring(4, 1))
+        far_a, far_b = lax.optimization_barrier((far_a, far_b, kept, *late))[:2]
+        pieces = [block, above, below, far_a, far_b]
+        here = jax.ShapeDtypeStruct((4 * shots, 2 * group), block.dtype)
         here = small_call(own_kernel, here, x[None], *pieces)
         far = from_y(here, 2)
         cols = jax.ShapeDtypeStruct((4, *here.shape), block.dtype)
         cols = small_call(join_kernel, cols, here, far, kept, *moved, scalars=0)
-        return pieces, cols, [*pieces[3:], *near, *moved, far]
-
-    rows0, mine0, done0 = gathered(own)
-    rows1, mine1, _ = gathered(first_of(other, *done0))
+        return pieces, cols, moved
+
+    rows0, mine0, moved0 = gathered(own, other)
+    rows1, mine1, _ = gathered(first_of(other, *moved0))
     rows = (*rows0, *rows1)
 
     place = jnp.stack([f, y, core])
@@ -198,10 +194,9 @@
     sent = terms_of(place, rows, theirs1, ready).astype(jnp.float16)
     got = lax.all_to_all(sent, ("zh", "zl", "x"), 0, 0, tiled=True)
 
-    weight = jnp.exp2(got[:, n, 0].astype(jnp.float32) - TOP) * scale
-    weight = weight.reshape(2, 4, 4, 1, 1)
-    got = got[:, :n].reshape(2, 4, 4, n, 2 * group)
-    values = sum(got[:, i].astype(jnp.float32) * weight[:, i] for i in range(4)) * (1.0 - pattern(n, 2 * group))
+    got = got.reshape(2, 4, 4, n + 16, 2 * group)
+    weight = jnp.exp2(got[..., n:, :].astype(jnp.float32)[..., :1, :1] - TOP) * scale
+    values = sum(got[:, i, :, :n].astype(jnp.float32) * weight[:, i] for i in range(4)) * (1.0 - pattern(n, 2 * group))
     return jnp.stack(
         [
             jnp.concatenate([values[:, i, :, p * group : (p + 1) * group] for i in range(4)], -1)

time: 185 us -> 176 us (0.951)
  local copies, waits for them, and re-layouts: 19.5 us -> 15.1 us
  waiting for transfers between devices: 86.6 us -> 82.4 us
  starting transfers between devices: 48.6 us -> 50.8 us
    ppermute x8, waiting for transfers between devices: 24.1 us -> 16.1 us  [the longest x4 12.8 us: gathered(): above, below = (lax.ppermute(block, 'x', ring(4, step)) for step in (-1, 1))]
    all_to_all x1, starting transfers between devices: 10.2 us -> 14.1 us  [body(): got = lax.all_to_all(sent, ('zh', 'zl', 'x'), 0, 0, tiled=True)]
    unnamed x54 -> x51, local copies, waits for them, and re-layouts: 12.6 us -> 9.45 us
    ppermute x6, waiting for transfers between devices: 0.02 us -> 2.61 us  [from_y(): return lax.ppermute(block, 'y', ring(4, -step))]
    ppermute x6, starting transfers between devices: 13.2 us -> 10.9 us  [from_y(): return lax.ppermute(block, 'y', ring(4, -step))]
    slice x7 -> x6, local copies, waits for them, and re-layouts: 5.15 us -> 4.03 us  [the longest x1 3.1 us: body(): got[:, i, :, :n].astype(jnp.float32) * weight[:, i]]
  transfers between devices with their start and end apart: 24 -> 24, of which waited for: 9 -> 11; matrix products, arithmetic and copies ran while one was open for 1% -> 0% of each run, Pallas kernels for 9% -> 10%
where the time goes in v3:
time: 176 us; the launch traced here: 174 us
  waiting for transfers between devices  82.4 us (47%)
  starting transfers between devices  50.8 us (29%)
  Pallas kernels  20.5 us (12%)
  local copies, waits for them, and re-layouts  15.1 us (9%)
  other arithmetic  5.13 us (3%)
    all_to_all x1, waiting for transfers between devices, body(): got = lax.all_to_all(sent, ('zh', 'zl', 'x'), 0, 0, tiled=True)  53 us
    all_to_all x1, starting transfers between devices, body(): got = lax.all_to_all(sent, ('zh', 'zl', 'x'), 0, 0, tiled=True)  14.1 us
    pallas_call x4, Pallas kernels, terms_of(): pl.pallas_call(kernel, out_shape=shapes, in_specs=[SCALAR] + [SPACE] * (l...  13.7 us
    ppermute x4, waiting for transfers between devices, gathered(): above, below = (lax.ppermute(block, 'x', ring(4, step)) for step in (-1, 1))  12.8 us
    ppermute x6, starting transfers between devices, from_y(): return lax.ppermute(block, 'y', ring(4, -step))  10.9 us
    unnamed x51, local copies, waits for them, and re-layouts  9.45 us
    ppermute x6, waiting for transfers between devices, gathered(): lax.ppermute(part, 'x', ring(4, step))  8.34 us
    ppermute x6, starting transfers between devices, gathered(): lax.ppermute(part, 'x', ring(4, step))  7.25 us
  transfers between devices with their start and end apart: 24, of which 11 were waited for; matrix products, arithmetic and copies ran while one was open for 0% of the time, Pallas kernels for 10%

profile of v3, /device:TPU:16, one launch (start us, length us, event | category | flops | bytes accessed | tf_op | source)
XLA Modules:
  0.0 174.2 jit_solution(3385437981644255838)
XLA Ops:
  2.1 2.8 %collective-permute-start = (bf16[2,512,256]{2,1,0:T(8,128)(2,1)S(1)}, bf16[2,512,256]{2,1,0:T(8,128)(2,1)S(1)}, u32[]{:S(2)}, u32[]{:S(2)}) collective-permute-start(bf16[2,512,256]{2,1,0:T(8,128)(2,1)S(1)} %dynamic-slice_bitcast_fusion.refs_0_), channel_id=1, source_target_pairs={{0,3},{1,0},{2,1},{3,2},{4,7},{5,4},{6,5},{7,6},{8,11},{9,8},{10,9... | collective-permute-start | bytes 1572872 | tf_op jit(solution)/shard_map/ppermute | solution.py:168
  5.4 1.6 collective-permute-start.5
  7.0 7.2 %collective-permute-start.6 = (bf16[2,512,256]{2,1,0:T(8,128)(2,1)}, bf16[2,512,256]{2,1,0:T(8,128)(2,1)S(1)}, u32[]{:S(2)}, u32[]{:S(2)}) collective-permute-start(bf16[2,512,256]{2,1,0:T(8,128)(2,1)} %dynamic-slice_bitcast_fusion.1), channel_id=1, source_target_pairs={{0,128},{128,0},{1,129},{129,1},{2,130},{130,2},{3,131},{131,3},{4... | collective-permute-start | bytes 1572872 | tf_op jit(solution)/shard_map/ppermute | solution.py:158
  14.1 2.0 %collective-permute-done.refs_1_ = bf16[2,512,256]{2,1,0:T(8,128)(2,1)S(1)} collective-permute-done((bf16[2,512,256]{2,1,0:T(8,128)(2,1)S(1)}, bf16[2,512,256]{2,1,0:T(8,128)(2,1)S(1)}, u32[]{:S(2)}, u32[]{:S(2)}) %collective-permute-start) | collective-permute-done | bytes 524320 | tf_op jit(solution)/shard_map/ppermute | solution.py:168
  16.1 3.4 %collective-permute-done.1.refs_2_ = bf16[2,512,256]{2,1,0:T(8,128)(2,1)S(1)} collective-permute-done((bf16[2,512,256]{2,1,0:T(8,128)(2,1)S(1)}, bf16[2,512,256]{2,1,0:T(8,128)(2,1)S(1)}, u32[]{:S(2)}, u32[]{:S(2)}) %collective-permute-start.1) | collective-permute-done | bytes 524320 | tf_op jit(solution)/shard_map/ppermute | solution.py:168
  19.5 1.6 shard_map.17
  21.8 2.0 %collective-permute-start.7 = (bf16[2,512,128]{2,1,0:T(8,128)(2,1)S(1)}, bf16[2,512,128]{2,1,0:T(8,128)(2,1)S(1)}, u32[]{:S(2)}, u32[]{:S(2)}) collective-permute-start(bf16[2,512,128]{2,1,0:T(8,128)(2,1)S(1)} %get-tuple-element.38), channel_id=1, source_target_pairs={{0,3},{1,0},{2,1},{3,2},{4,7},{5,4},{6,5},{7,6},{8,11},{9,8},{10,9... | collective-permute-start | bytes 786440 | tf_op jit(solution)/shard_map/ppermute | solution.py:173
  23.8 1.4 collective-permute-start.9
  25.3 2.4 %collective-permute-done.6.refs_0_.refs_5_ = bf16[2,512,256]{2,1,0:T(8,128)(2,1)S(1)} collective-permute-done((bf16[2,512,256]{2,1,0:T(8,128)(2,1)}, bf16[2,512,256]{2,1,0:T(8,128)(2,1)S(1)}, u32[]{:S(2)}, u32[]{:S(2)}) %collective-permute-start.6) | collective-permute-done | bytes 524320 | tf_op jit(solution)/shard_map/ppermute | solution.py:158
  27.7 3.4 %collective-permute-done.7.refs_1_ = bf16[2,512,128]{2,1,0:T(8,128)(2,1)S(1)} collective-permute-done((bf16[2,512,128]{2,1,0:T(8,128)(2,1)S(1)}, bf16[2,512,128]{2,1,0:T(8,128)(2,1)S(1)}, u32[]{:S(2)}, u32[]{:S(2)}) %collective-permute-start.7) | collective-permute-done | bytes 262176 | tf_op jit(solution)/shard_map/ppermute | solution.py:173
  31.8 5.0 %collective-permute-done.8.refs_2_ = bf16[2,512,128]{2,1,0:T(8,128)(2,1)S(1)} collective-permute-done((bf16[2,512,128]{2,1,0:T(8,128)(2,1)S(1)}, bf16[2,512,128]{2,1,0:T(8,128)(2,1)S(1)}, u32[]{:S(2)}, u32[]{:S(2)}) %collective-permute-start.8) | collective-permute-done | bytes 262176 | tf_op jit(solution)/shard_map/ppermute | solution.py:173
  38.2 2.0 %collective-permute-start.11 = (bf16[2,512,256]{2,1,0:T(8,128)(2,1)}, bf16[2,512,256]{2,1,0:T(8,128)(2,1)S(1)}, u32[]{:S(2)}, u32[]{:S(2)}) collective-permute-start(bf16[2,512,256]{2,1,0:T(8,128)(2,1)} %copy-done.3), channel_id=1, source_target_pairs={{0,1},{1,2},{2,3},{3,0},{4,5},{5,6},{6,7},{7,4},{8,9},{9,10},{10,1... | collective-permute-start | bytes 1572872 | tf_op jit(solution)/shard_map/ppermute | solution.py:168
  40.2 1.9 %collective-permute-start.14 = (bf16[2,512,256]{2,1,0:T(8,128)(2,1)}, bf16[2,512,256]{2,1,0:T(8,128)(2,1)S(1)}, u32[]{:S(2)}, u32[]{:S(2)}) collective-permute-start(bf16[2,512,256]{2,1,0:T(8,128)(2,1)} %copy-done.3), channel_id=1, source_target_pairs={{0,96},{32,0},{64,32},{96,64},{1,97},{33,1},{65,33},{97,65},{2,98}... | collective-permute-start | bytes 1572872 | tf_op jit(solution)/shard_map/ppermute | solution.py:161
  42.7 2.3 %collective-permute-start.2 = (bf16[2,256,256]{2,1,0:T(8,128)(2,1)S(1)}, bf16[2,256,256]{2,1,0:T(8,128)(2,1)S(1)}, u32[]{:S(2)}, u32[]{:S(2)}) collective-permute-start(bf16[2,256,256]{2,1,0:T(8,128)(2,1)S(1)} %slice.90), channel_id=1, source_target_pairs={{0,3},{1,0},{2,1},{3,2},{4,7},{5,4},{6,5},{7,6},{8,11},{9,8},{10,9... | collective-permute-start | bytes 786440 | tf_op jit(solution)/shard_map/ppermute | solution.py:174
  45.0 5.8 %collective-permute-done.10.refs_1_.refs_6_ = bf16[2,512,256]{2,1,0:T(8,128)(2,1)S(1)} collective-permute-done((bf16[2,512,256]{2,1,0:T(8,128)(2,1)}, bf16[2,512,256]{2,1,0:T(8,128)(2,1)S(1)}, u32[]{:S(2)}, u32[]{:S(2)}) %collective-permute-start.10) | collective-permute-done | bytes 524320 | tf_op jit(solution)/shard_map/ppermute | solution.py:168
  51.3 1.6 collective-permute-done.11.refs_2_.refs_7_
  52.9 1.9 %collective-permute-start.12 = (bf16[2,256,256]{2,1,0:T(8,128)(2,1)S(1)}, bf16[2,256,256]{2,1,0:T(8,128)(2,1)S(1)}, u32[]{:S(2)}, u32[]{:S(2)}) collective-permute-start(bf16[2,256,256]{2,1,0:T(8,128)(2,1)S(1)} %slice.92), channel_id=1, source_target_pairs={{0,3},{1,0},{2,1},{3,2},{4,7},{5,4},{6,5},{7,6},{8,11},{9,8},{10,9... | collective-permute-start | bytes 786440 | tf_op jit(solution)/shard_map/ppermute | solution.py:174
  56.4 2.7 %collective-permute-done.3.refs_4_ = bf16[2,256,256]{2,1,0:T(8,128)(2,1)S(1)} collective-permute-done((bf16[2,256,256]{2,1,0:T(8,128)(2,1)S(1)}, bf16[2,256,256]{2,1,0:T(8,128)(2,1)S(1)}, u32[]{:S(2)}, u32[]{:S(2)}) %collective-permute-start.3) | collective-permute-done | bytes 262176 | tf_op jit(solution)/shard_map/ppermute | solution.py:175
  60.8 5.0 %collective-permute-start.20 = (bf16[2048,128]{1,0:T(8,128)(2,1)}, bf16[2048,128]{1,0:T(8,128)(2,1)}, u32[]{:S(2)}, u32[]{:S(2)}) collective-permute-start(bf16[2048,128]{1,0:T(8,128)(2,1)} %shard_map.21.here), channel_id=1, source_target_pairs={{0,64},{32,96},{64,0},{96,32},{1,65},{33,97},{65,1},{97,33},{2,66}... | collective-permute-start | bytes 1572872 | tf_op jit(solution)/shard_map/ppermute | solution.py:161
  68.1 1.4 collective-permute-start.16
  69.5 2.2 %collective-permute-start.17 = (bf16[2,512,128]{2,1,0:T(8,128)(2,1)}, bf16[2,512,128]{2,1,0:T(8,128)(2,1)S(1)}, u32[]{:S(2)}, u32[]{:S(2)}) collective-permute-start(bf16[2,512,128]{2,1,0:T(8,128)(2,1)} %copy-done.24), channel_id=1, source_target_pairs={{0,3},{1,0},{2,1},{3,2},{4,7},{5,4},{6,5},{7,6},{8,11},{9,8},{10,9... | collective-permute-start | bytes 786440 | tf_op jit(solution)/shard_map/ppermute | solution.py:173
  71.8 1.6 collective-permute-start.19
  73.4 2.6 %collective-permute-done.20.far = bf16[2048,128]{1,0:T(8,128)(2,1)} collective-permute-done((bf16[2048,128]{1,0:T(8,128)(2,1)}, bf16[2048,128]{1,0:T(8,128)(2,1)}, u32[]{:S(2)}, u32[]{:S(2)}) %collective-permute-start.20) | collective-permute-done | bytes 524320 | tf_op jit(solution)/shard_map/ppermute | solution.py:161
  81.3 3.3 %shard_map.23 = (f32[2,4,256,128]{3,2,1,0:T(8,128)S(1)}, f32[8,128]{1,0:T(8,128)S(1)}) custom-call(s32[3]{0:T(128)S(1)} %pad_add_fusion.place, bf16[2,512,256]{2,1,0:T(8,128)(2,1)S(1)} %dynamic-slice_bitcast_fusion.refs_0_, bf16[2,512,256]{2,1,0:T(8,128)(2,1)S(1)} %collective-permute-done.refs_1_, bf16[2,512,256]{2,1,0:T(8,128)(2,1)S(1)} %collective-permute-done.1.refs_2_, ...), custom_call_target="tpu_custom_call" | custom-call | flops 2147483648 | bytes 8388608 | tf_op jit(solution)/shard_map/pallas_call | solution.py:133
  86.8 3.3 %shard_map.25 = (f32[2,4,256,128]{3,2,1,0:T(8,128)S(1)}, f32[8,128]{1,0:T(8,128)S(1)}) custom-call(s32[3]{0:T(128)S(1)} %pad_add_fusion.place, bf16[2,512,256]{2,1,0:T(8,128)(2,1)S(1)} %dynamic-slice_bitcast_fusion.refs_0_, bf16[2,512,256]{2,1,0:T(8,128)(2,1)S(1)} %collective-permute-done.refs_1_, bf16[2,512,256]{2,1,0:T(8,128)(2,1)S(1)} %collective-permute-done.1.refs_2_, ...), custom_call_target="tpu_custom_call" | custom-call | flops 2147483648 | bytes 8388608 | tf_op jit(solution)/shard_map/pallas_call | solution.py:133
  90.1 3.3 %shard_map.24 = (f32[2,4,256,128]{3,2,1,0:T(8,128)S(1)}, f32[8,128]{1,0:T(8,128)S(1)}) custom-call(s32[3]{0:T(128)S(1)} %pad_add_fusion.place, bf16[2,512,256]{2,1,0:T(8,128)(2,1)S(1)} %dynamic-slice_bitcast_fusion.refs_0_, bf16[2,512,256]{2,1,0:T(8,128)(2,1)S(1)} %collective-permute-done.refs_1_, bf16[2,512,256]{2,1,0:T(8,128)(2,1)S(1)} %collective-permute-done.1.refs_2_, ...), custom_call_target="tpu_custom_call" | custom-call | flops 2147483648 | bytes 8388608 | tf_op jit(solution)/shard_map/pallas_call | solution.py:133
  93.5 3.7 %shard_map.26 = f32[32,272,128]{2,1,0:T(8,128)S(1)} custom-call(s32[3]{0:T(128)S(1)} %pad_add_fusion.place, bf16[2,512,256]{2,1,0:T(8,128)(2,1)S(1)} %dynamic-slice_bitcast_fusion.refs_0_, bf16[2,512,256]{2,1,0:T(8,128)(2,1)S(1)} %collective-permute-done.refs_1_, bf16[2,512,256]{2,1,0:T(8,128)(2,1)S(1)} %collective-permute-done.1.refs_2_, ...), custom_call_target="tpu_custom_call" | custom-call | flops 2147483648 | bytes 8388608 | tf_op jit(solution)/shard_map/pallas_call | solution.py:133
  97.2 1.7 convert_element_type.35
  98.8 14.1 %all-to-all-start = ((f16[32,272,128]{2,1,0:T(8,128)(2,1)}), f16[32,272,128]{2,1,0:T(8,128)(2,1)}, u32[]{:S(2)}, u32[]{:S(2)}) async-start(f16[32,272,128]{2,1,0:T(8,128)(2,1)} %convert_element_type.35), calls=%async_computation | async-start | bytes 4456448 | tf_op jit(solution)/shard_map/all_to_all | solution.py:195
  113.1 53.0 %all-to-all-done = f16[32,272,128]{2,1,0:T(8,128)(2,1)} async-done(((f16[32,272,128]{2,1,0:T(8,128)(2,1)}), f16[32,272,128]{2,1,0:T(8,128)(2,1)}, u32[]{:S(2)}, u32[]{:S(2)}) %all-to-all-start) | async-done | bytes 2228256 | tf_op jit(solution)/shard_map/all_to_all | solution.py:195
  166.1 3.1 %fusion.9 = (f16[2,1,4,256,128]{4,3,2,1,0:T(8,128)(2,1)S(1)}, f16[2,1,4,256,128]{4,3,2,1,0:T(8,128)(2,1)S(1)}, f16[2,1,4,256,128]{4,3,2,1,0:T(8,128)(2,1)}, f16[2,1,4,256,128]{4,3,2,1,0:T(8,128)(2,1)}) fusion(f16[2,4,4,272,128]{4,3,2,1,0:T(8,128)(2,1)} %bitcast.6), kind=kLoop, calls=%fused_computation.43 | loop fusion | bytes 4194304 | tf_op jit(solution)/shard_map/slice | solution.py:199
  170.6 1.7 fusion.1
  (100 shorter events, 23.0 us)
Async XLA Ops:
  2.1 14.0 %collective-permute-start = (bf16[2,512,256]{2,1,0:T(8,128)(2,1)S(1)}, bf16[2,512,256]{2,1,0:T(8,128)(2,1)S(1)}, u32[]{:S(2)}, u32[]{:S(2)}) collective-permute-start(bf16[2,512,256]{2,1,0:T(8,128)(2,1)S(1)} %dynamic-slice_bitcast_fusion.refs_0_), channel_id=1, source_target_pairs={{0,3},{1,0},{2,1},{3,2},{4,7},{5,4},{6,5},{7,6},{8,11},{9,8},{10,9... | collective-permute-start | bytes 1572872 | tf_op jit(solution)/shard_map/ppermute | solution.py:168
  4.9 14.6 %collective-permute-start.1 = (bf16[2,512,256]{2,1,0:T(8,128)(2,1)S(1)}, bf16[2,512,256]{2,1,0:T(8,128)(2,1)S(1)}, u32[]{:S(2)}, u32[]{:S(2)}) collective-permute-start(bf16[2,512,256]{2,1,0:T(8,128)(2,1)S(1)} %dynamic-slice_bitcast_fusion.refs_0_), channel_id=1, source_target_pairs={{0,1},{1,2},{2,3},{3,0},{4,5},{5,6},{6,7},{7,4},{8,9},{9,10},{10,1... | collective-permute-start | bytes 1572872 | tf_op jit(solution)/shard_map/ppermute | solution.py:168
  4.9 14.6 %collective-permute-start.4 = (bf16[2,512,256]{2,1,0:T(8,128)(2,1)S(1)}, bf16[2,512,256]{2,1,0:T(8,128)(2,1)}, u32[]{:S(2)}, u32[]{:S(2)}) collective-permute-start(bf16[2,512,256]{2,1,0:T(8,128)(2,1)S(1)} %dynamic-slice_bitcast_fusion.refs_0_), channel_id=1, source_target_pairs={{0,96},{32,0},{64,32},{96,64},{1,97},{33,1},{65,33},{97,65},{2,98}... | collective-permute-start | bytes 1572872 | tf_op jit(solution)/shard_map/ppermute | solution.py:161
  5.4 14.1 %collective-permute-start.5 = (bf16[2,512,256]{2,1,0:T(8,128)(2,1)S(1)}, bf16[2,512,256]{2,1,0:T(8,128)(2,1)}, u32[]{:S(2)}, u32[]{:S(2)}) collective-permute-start(bf16[2,512,256]{2,1,0:T(8,128)(2,1)S(1)} %dynamic-slice_bitcast_fusion.refs_0_), channel_id=1, source_target_pairs={{0,32},{32,64},{64,96},{96,0},{1,33},{33,65},{65,97},{97,1},{2,34}... | collective-permute-start | bytes 1572872 | tf_op jit(solution)/shard_map/ppermute | solution.py:161
  7.0 20.7 %collective-permute-start.6 = (bf16[2,512,256]{2,1,0:T(8,128)(2,1)}, bf16[2,512,256]{2,1,0:T(8,128)(2,1)S(1)}, u32[]{:S(2)}, u32[]{:S(2)}) collective-permute-start(bf16[2,512,256]{2,1,0:T(8,128)(2,1)} %dynamic-slice_bitcast_fusion.1), channel_id=1, source_target_pairs={{0,128},{128,0},{1,129},{129,1},{2,130},{130,2},{3,131},{131,3},{4... | collective-permute-start | bytes 1572872 | tf_op jit(solution)/shard_map/ppermute | solution.py:158
  21.8 9.2 %collective-permute-start.7 = (bf16[2,512,128]{2,1,0:T(8,128)(2,1)S(1)}, bf16[2,512,128]{2,1,0:T(8,128)(2,1)S(1)}, u32[]{:S(2)}, u32[]{:S(2)}) collective-permute-start(bf16[2,512,128]{2,1,0:T(8,128)(2,1)S(1)} %get-tuple-element.38), channel_id=1, source_target_pairs={{0,3},{1,0},{2,1},{3,2},{4,7},{5,4},{6,5},{7,6},{8,11},{9,8},{10,9... | collective-permute-start | bytes 786440 | tf_op jit(solution)/shard_map/ppermute | solution.py:173
  23.8 12.9 %collective-permute-start.8 = (bf16[2,512,128]{2,1,0:T(8,128)(2,1)S(1)}, bf16[2,512,128]{2,1,0:T(8,128)(2,1)S(1)}, u32[]{:S(2)}, u32[]{:S(2)}) collective-permute-start(bf16[2,512,128]{2,1,0:T(8,128)(2,1)S(1)} %get-tuple-element.39), channel_id=1, source_target_pairs={{0,1},{1,2},{2,3},{3,0},{4,5},{5,6},{6,7},{7,4},{8,9},{9,10},{10,1... | collective-permute-start | bytes 786440 | tf_op jit(solution)/shard_map/ppermute | solution.py:173
  23.8 13.6 %collective-permute-start.9 = (bf16[2,512,128]{2,1,0:T(8,128)(2,1)S(1)}, bf16[2,512,128]{2,1,0:T(8,128)(2,1)S(1)}, u32[]{:S(2)}, u32[]{:S(2)}) collective-permute-start(bf16[2,512,128]{2,1,0:T(8,128)(2,1)S(1)} %get-tuple-element.40), channel_id=1, source_target_pairs={{0,2},{1,3},{2,0},{3,1},{4,6},{5,7},{6,4},{7,5},{8,10},{9,11},{10,... | collective-permute-start | bytes 786440 | tf_op jit(solution)/shard_map/ppermute | solution.py:173
  27.7 9.0 %copy-start.3 = (bf16[2,512,256]{2,1,0:T(8,128)(2,1)}, bf16[2,512,256]{2,1,0:T(8,128)(2,1)S(1)}, u32[]{:S(2)}) copy-start(bf16[2,512,256]{2,1,0:T(8,128)(2,1)S(1)} %collective-permute-done.6.refs_0_.refs_5_) | copy-start | bytes 1572868
  38.2 12.7 %collective-permute-start.10 = (bf16[2,512,256]{2,1,0:T(8,128)(2,1)}, bf16[2,512,256]{2,1,0:T(8,128)(2,1)S(1)}, u32[]{:S(2)}, u32[]{:S(2)}) collective-permute-start(bf16[2,512,256]{2,1,0:T(8,128)(2,1)} %copy-done.3), channel_id=1, source_target_pairs={{0,3},{1,0},{2,1},{3,2},{4,7},{5,4},{6,5},{7,6},{8,11},{9,8},{10,9... | collective-permute-start | bytes 1572872 | tf_op jit(solution)/shard_map/ppermute | solution.py:168
  38.2 14.7 %collective-permute-start.11 = (bf16[2,512,256]{2,1,0:T(8,128)(2,1)}, bf16[2,512,256]{2,1,0:T(8,128)(2,1)S(1)}, u32[]{:S(2)}, u32[]{:S(2)}) collective-permute-start(bf16[2,512,256]{2,1,0:T(8,128)(2,1)} %copy-done.3), channel_id=1, source_target_pairs={{0,1},{1,2},{2,3},{3,0},{4,5},{5,6},{6,7},{7,4},{8,9},{9,10},{10,1... | collective-permute-start | bytes 1572872 | tf_op jit(solution)/shard_map/ppermute | solution.py:168
  40.2 25.6 %collective-permute-start.14 = (bf16[2,512,256]{2,1,0:T(8,128)(2,1)}, bf16[2,512,256]{2,1,0:T(8,128)(2,1)S(1)}, u32[]{:S(2)}, u32[]{:S(2)}) collective-permute-start(bf16[2,512,256]{2,1,0:T(8,128)(2,1)} %copy-done.3), channel_id=1, source_target_pairs={{0,96},{32,0},{64,32},{96,64},{1,97},{33,1},{65,33},{97,65},{2,98}... | collective-permute-start | bytes 1572872 | tf_op jit(solution)/shard_map/ppermute | solution.py:161
  42.1 23.7 %collective-permute-start.15 = (bf16[2,512,256]{2,1,0:T(8,128)(2,1)}, bf16[2,512,256]{2,1,0:T(8,128)(2,1)S(1)}, u32[]{:S(2)}, u32[]{:S(2)}) collective-permute-start(bf16[2,512,256]{2,1,0:T(8,128)(2,1)} %copy-done.3), channel_id=1, source_target_pairs={{0,32},{32,64},{64,96},{96,0},{1,33},{33,65},{65,97},{97,1},{2,34}... | collective-permute-start | bytes 1572872 | tf_op jit(solution)/shard_map/ppermute | solution.py:161
  42.7 12.7 %collective-permute-start.2 = (bf16[2,256,256]{2,1,0:T(8,128)(2,1)S(1)}, bf16[2,256,256]{2,1,0:T(8,128)(2,1)S(1)}, u32[]{:S(2)}, u32[]{:S(2)}) collective-permute-start(bf16[2,256,256]{2,1,0:T(8,128)(2,1)S(1)} %slice.90), channel_id=1, source_target_pairs={{0,3},{1,0},{2,1},{3,2},{4,7},{5,4},{6,5},{7,6},{8,11},{9,8},{10,9... | collective-permute-start | bytes 786440 | tf_op jit(solution)/shard_map/ppermute | solution.py:174
  50.9 8.2 %collective-permute-start.3 = (bf16[2,256,256]{2,1,0:T(8,128)(2,1)S(1)}, bf16[2,256,256]{2,1,0:T(8,128)(2,1)S(1)}, u32[]{:S(2)}, u32[]{:S(2)}) collective-permute-start(bf16[2,256,256]{2,1,0:T(8,128)(2,1)S(1)} %slice.91), channel_id=1, source_target_pairs={{0,1},{1,2},{2,3},{3,0},{4,5},{5,6},{6,7},{7,4},{8,9},{9,10},{10,1... | collective-permute-start | bytes 786440 | tf_op jit(solution)/shard_map/ppermute | solution.py:175
  51.3 15.6 %copy-start.4 = (bf16[2,512,256]{2,1,0:T(8,128)(2,1)S(1)}, bf16[2,512,256]{2,1,0:T(8,128)(2,1)}, u32[]{:S(2)}) copy-start(bf16[2,512,256]{2,1,0:T(8,128)(2,1)} %copy-done.3) | copy-start | bytes 1572868
  52.9 15.2 %copy-start.1 = (bf16[2,512,256]{2,1,0:T(8,128)(2,1)}, bf16[2,512,256]{2,1,0:T(8,128)(2,1)S(1)}, u32[]{:S(2)}) copy-start(bf16[2,512,256]{2,1,0:T(8,128)(2,1)S(1)} %collective-permute-done.11.refs_2_.refs_7_) | copy-start | bytes 1572868
  52.9 14.0 %collective-permute-start.12 = (bf16[2,256,256]{2,1,0:T(8,128)(2,1)S(1)}, bf16[2,256,256]{2,1,0:T(8,128)(2,1)S(1)}, u32[]{:S(2)}, u32[]{:S(2)}) collective-permute-start(bf16[2,256,256]{2,1,0:T(8,128)(2,1)S(1)} %slice.92), channel_id=1, source_target_pairs={{0,3},{1,0},{2,1},{3,2},{4,7},{5,4},{6,5},{7,6},{8,11},{9,8},{10,9... | collective-permute-start | bytes 786440 | tf_op jit(solution)/shard_map/ppermute | solution.py:174
  55.4 11.5 %collective-permute-start.13 = (bf16[2,256,256]{2,1,0:T(8,128)(2,1)S(1)}, bf16[2,256,256]{2,1,0:T(8,128)(2,1)S(1)}, u32[]{:S(2)}, u32[]{:S(2)}) collective-permute-start(bf16[2,256,256]{2,1,0:T(8,128)(2,1)S(1)} %slice.93), channel_id=1, source_target_pairs={{0,1},{1,2},{2,3},{3,0},{4,5},{5,6},{6,7},{7,4},{8,9},{9,10},{10,1... | collective-permute-start | bytes 786440 | tf_op jit(solution)/shard_map/ppermute | solution.py:175
  60.8 15.2 %collective-permute-start.20 = (bf16[2048,128]{1,0:T(8,128)(2,1)}, bf16[2048,128]{1,0:T(8,128)(2,1)}, u32[]{:S(2)}, u32[]{:S(2)}) collective-permute-start(bf16[2048,128]{1,0:T(8,128)(2,1)} %shard_map.21.here), channel_id=1, source_target_pairs={{0,64},{32,96},{64,0},{96,32},{1,65},{33,97},{65,1},{97,33},{2,66}... | collective-permute-start | bytes 1572872 | tf_op jit(solution)/shard_map/ppermute | solution.py:161
  68.1 16.5 %collective-permute-start.16 = (bf16[2048,128]{1,0:T(8,128)(2,1)}, bf16[2048,128]{1,0:T(8,128)(2,1)}, u32[]{:S(2)}, u32[]{:S(2)}) collective-permute-start(bf16[2048,128]{1,0:T(8,128)(2,1)} %shard_map.19.here), channel_id=1, source_target_pairs={{0,64},{32,96},{64,0},{96,32},{1,65},{33,97},{65,1},{97,33},{2,66}... | collective-permute-start | bytes 1572872 | tf_op jit(solution)/shard_map/ppermute | solution.py:161
  69.5 11.7 %copy-start.2 = (bf16[2,512,256]{2,1,0:T(8,128)(2,1)S(1)}, bf16[2,512,256]{2,1,0:T(8,128)(2,1)}, u32[]{:S(2)}) copy-start(bf16[2,512,256]{2,1,0:T(8,128)(2,1)} %copy-done.1) | copy-start | bytes 1572868
  69.5 11.8 %copy-start.5 = (bf16[2,512,256]{2,1,0:T(8,128)(2,1)S(1)}, bf16[2,512,256]{2,1,0:T(8,128)(2,1)}, u32[]{:S(2)}) copy-start(bf16[2,512,256]{2,1,0:T(8,128)(2,1)} %copy-done.3) | copy-start | bytes 1572868
  69.5 11.8 %copy-start.7 = (bf16[2,256,256]{2,1,0:T(8,128)(2,1)S(1)}, bf16[2,256,256]{2,1,0:T(8,128)(2,1)}, u32[]{:S(2)}) copy-start(bf16[2,256,256]{2,1,0:T(8,128)(2,1)} %copy-done.6) | copy-start | bytes 786436
  69.5 11.8 %copy-start.9 = (bf16[2,256,256]{2,1,0:T(8,128)(2,1)S(1)}, bf16[2,256,256]{2,1,0:T(8,128)(2,1)}, u32[]{:S(2)}) copy-start(bf16[2,256,256]{2,1,0:T(8,128)(2,1)} %copy-done.8) | copy-start | bytes 786436
  69.5 11.8 %copy-start.11 = (bf16[2,256,256]{2,1,0:T(8,128)(2,1)S(1)}, bf16[2,256,256]{2,1,0:T(8,128)(2,1)}, u32[]{:S(2)}) copy-start(bf16[2,256,256]{2,1,0:T(8,128)(2,1)} %copy-done.10) | copy-start | bytes 786436
  69.5 15.1 %collective-permute-start.17 = (bf16[2,512,128]{2,1,0:T(8,128)(2,1)}, bf16[2,512,128]{2,1,0:T(8,128)(2,1)S(1)}, u32[]{:S(2)}, u32[]{:S(2)}) collective-permute-start(bf16[2,512,128]{2,1,0:T(8,128)(2,1)} %copy-done.24), channel_id=1, source_target_pairs={{0,3},{1,0},{2,1},{3,2},{4,7},{5,4},{6,5},{7,6},{8,11},{9,8},{10,9... | collective-permute-start | bytes 786440 | tf_op jit(solution)/shard_map/ppermute | solution.py:173
  71.8 12.9 %collective-permute-start.18 = (bf16[2,512,128]{2,1,0:T(8,128)(2,1)}, bf16[2,512,128]{2,1,0:T(8,128)(2,1)S(1)}, u32[]{:S(2)}, u32[]{:S(2)}) collective-permute-start(bf16[2,512,128]{2,1,0:T(8,128)(2,1)} %copy-done.23), channel_id=1, source_target_pairs={{0,1},{1,2},{2,3},{3,0},{4,5},{5,6},{6,7},{7,4},{8,9},{9,10},{10,1... | collective-permute-start | bytes 786440 | tf_op jit(solution)/shard_map/ppermute | solution.py:173
  71.8 12.9 %collective-permute-start.19 = (bf16[2,512,128]{2,1,0:T(8,128)(2,1)}, bf16[2,512,128]{2,1,0:T(8,128)(2,1)S(1)}, u32[]{:S(2)}, u32[]{:S(2)}) collective-permute-start(bf16[2,512,128]{2,1,0:T(8,128)(2,1)} %copy-done.22), channel_id=1, source_target_pairs={{0,2},{1,3},{2,0},{3,1},{4,6},{5,7},{6,4},{7,5},{8,10},{9,11},{10,... | collective-permute-start | bytes 786440 | tf_op jit(solution)/shard_map/ppermute | solution.py:173
  81.1 9.0 %collective-permute-start.22 = (bf16[4,2048,128]{2,1,0:T(8,128)(2,1)S(1)}, bf16[4,2048,128]{2,1,0:T(8,128)(2,1)S(1)}, u32[]{:S(2)}, u32[]{:S(2)}) collective-permute-start(bf16[4,2048,128]{2,1,0:T(8,128)(2,1)S(1)} %shard_map.22.refs_10_), channel_id=1, source_target_pairs={{0,16},{16,0},{1,17},{17,1},{2,18},{18,2},{3,19},{19,3},{4,20},{20... | collective-permute-start | bytes 6291464 | tf_op jit(solution)/shard_map/ppermute | solution.py:164
  86.0 7.5 %collective-permute-start.21 = (bf16[4,2048,128]{2,1,0:T(8,128)(2,1)S(1)}, bf16[4,2048,128]{2,1,0:T(8,128)(2,1)S(1)}, u32[]{:S(2)}, u32[]{:S(2)}) collective-permute-start(bf16[4,2048,128]{2,1,0:T(8,128)(2,1)S(1)} %shard_map.20.refs_10_), channel_id=1, source_target_pairs={{0,16},{16,0},{1,17},{17,1},{2,18},{18,2},{3,19},{19,3},{4,20},{20... | collective-permute-start | bytes 6291464 | tf_op jit(solution)/shard_map/ppermute | solution.py:164
  98.8 67.3 %all-to-all-start = ((f16[32,272,128]{2,1,0:T(8,128)(2,1)}), f16[32,272,128]{2,1,0:T(8,128)(2,1)}, u32[]{:S(2)}, u32[]{:S(2)}) async-start(f16[32,272,128]{2,1,0:T(8,128)(2,1)} %convert_element_type.35), calls=%async_computation | async-start | bytes 4456448 | tf_op jit(solution)/shard_map/all_to_all | solution.py:195
  (17 other events, 19.0 us)

commit v4 on v3

--- a/solution.py
+++ b/solution.py
@@ -1,3 +1,5 @@
+import functools
+
 import jax
 import jax.numpy as jnp
 from jax import lax
@@ -105,7 +107,7 @@
     f, core = place[0], place[2]
     n, c = term3.shape[2:]
     largest = jnp.max(jnp.maximum(jnp.maximum(top0[...], top1[...]), jnp.maximum(top2[...], top3[...])))
-    power = jnp.clip(jnp.floor(jnp.log2(jnp.full((16, c), largest))), -100.0, 100.0)
+    power = jnp.clip(jnp.floor(jnp.log2(jnp.full((8, c), largest))), -100.0, 100.0)
     factor = jnp.exp2(TOP - power[:1]) * (1.0 + pattern(n, c))
 
     def step(i, carry):
@@ -129,7 +131,7 @@
     else:
         kernel, operands = last_kernel, (place, *rows, cols, *others)
         scratch = [pltpu.VMEM(term, jnp.float32), pltpu.VMEM((8, c), jnp.float32)]
-        shapes = jax.ShapeDtypeStruct((32, n + 16, c), jnp.float32)
+        shapes = jax.ShapeDtypeStruct((32, n + 8, c), jnp.float32)
     return pl.pallas_call(
         kernel,
         out_shape=shapes,
@@ -141,6 +143,21 @@
     )(*operands)
 
 
+def sum_kernel(scale, got, out):
+    n = out.shape[2]
+    c = got.shape[2]
+    undo = (1.0 - pattern(n, c)) * scale
+    for f in range(2):
+        for x in range(4):
+            total = 0.0
+            for zl in range(4):
+                chunk = f * 16 + zl * 4 + x
+                total += got[chunk, :n] * jnp.exp2(got[chunk, n : n + 1] - TOP)
+            total *= undo
+            for p in range(2):
+                out[f, p, :, x * c // 2 : (x + 1) * c // 2] = total[:, p * c // 2 : (p + 1) * c // 2]
+
+
 def pattern(rows, cols):
     i = lax.broadcasted_iota(jnp.int32, (rows, cols), 0)
     j = lax.broadcasted_iota(jnp.int32, (rows, cols), 1)
@@ -151,7 +168,6 @@
     f, y, core, zl, x = (lax.axis_index(name) for name in AXES)
     n = wavefield.shape[3]
     group = n // 4
-    scale = 1.0 / jnp.sqrt(jnp.float32(wavefield.shape[2] * 16))
 
     other = lax.dynamic_index_in_dim(wavefield, 1 - f, 0, keepdims=False)
     own = lax.dynamic_index_in_dim(first_of(wavefield, other), f, 0, keepdims=False)
@@ -194,16 +210,9 @@
     sent = terms_of(place, rows, theirs1, ready).astype(jnp.float16)
     got = lax.all_to_all(sent, ("zh", "zl", "x"), 0, 0, tiled=True)
 
-    got = got.reshape(2, 4, 4, n + 16, 2 * group)
-    weight = jnp.exp2(got[..., n:, :].astype(jnp.float32)[..., :1, :1] - TOP) * scale
-    values = sum(got[:, i, :, :n].astype(jnp.float32) * weight[:, i] for i in range(4)) * (1.0 - pattern(n, 2 * group))
-    return jnp.stack(
-        [
-            jnp.concatenate([values[:, i, :, p * group : (p + 1) * group] for i in range(4)], -1)
-            for p in range(2)
-        ],
-        1,
-    )
+    whole = jax.ShapeDtypeStruct((2, 2, n, n), jnp.float32)
+    kernel = functools.partial(sum_kernel, (16 * wavefield.shape[2]) ** -0.5)
+    return small_call(kernel, whole, got.astype(jnp.float32), scalars=0)
 
 
 def solution(mesh):

time: 176 us -> 171 us (0.972)
  blocking collectives: 0 us -> 70.9 us
  waiting for transfers between devices: 82.4 us -> 26.8 us
  starting transfers between devices: 50.8 us -> 34 us
  Pallas kernels: 20.5 us -> 25.1 us
  other arithmetic: 5.13 us -> 0.64 us
  local copies, waits for them, and re-layouts: 15.1 us -> 12.1 us
    all_to_all x0 -> x1, blocking collectives: none -> 70.9 us  [body(): got = lax.all_to_all(sent, ('zh', 'zl', 'x'), 0, 0, tiled=True)]
    all_to_all x1 -> x0, waiting for transfers between devices: 53 us -> none  [body(): got = lax.all_to_all(sent, ('zh', 'zl', 'x'), 0, 0, tiled=True)]
    all_to_all x1 -> x0, starting transfers between devices: 14.1 us -> none  [body(): got = lax.all_to_all(sent, ('zh', 'zl', 'x'), 0, 0, tiled=True)]
    slice x2 -> x0, local copies, waits for them, and re-layouts: 3.96 us -> none  [the longest x1 3.1 us: body(): got[:, i, :, :n].astype(jnp.float32) * weight[:, i]]
    ppermute x6, starting transfers between devices: 10.9 us -> 7.66 us  [from_y(): return lax.ppermute(block, 'y', ring(4, -step))]
    pallas_call x6 -> x7, Pallas kernels: 6.81 us -> 9.39 us  [small_call(): pl.pallas_call(kernel, out_shape=shapes, in_specs=[SCALAR] * scalars + [S...]
    ppermute x2, starting transfers between devices: 4.19 us -> 1.83 us  [gathered(): far_a = lax.ppermute(above[:, :shots // 2], 'x', ring(4, -1))]
    ppermute x2, waiting for transfers between devices: 2.66 us -> 0.46 us  [gathered(): far_b = lax.ppermute(below[:, shots // 2:], 'x', ring(4, 1))]
  transfers between devices with their start and end apart: 24 -> 23, of which waited for: 11 -> 10; matrix products, arithmetic and copies ran while one was open for 0% -> 0% of each run, Pallas kernels for 10% -> 11%
where the time goes in v4:
time: 171 us; the launch traced here: 170 us
  blocking collectives  70.9 us (41%)
  starting transfers between devices  34 us (20%)
  waiting for transfers between devices  26.8 us (16%)
  Pallas kernels  25.1 us (15%)
  local copies, waits for them, and re-layouts  12.1 us (7%)
    all_to_all x1, blocking collectives, body(): got = lax.all_to_all(sent, ('zh', 'zl', 'x'), 0, 0, tiled=True)  70.9 us
    pallas_call x4, Pallas kernels, terms_of(): pl.pallas_call(kernel, out_shape=shapes, in_specs=[SCALAR] + [SPACE] * (l...  15.7 us
    ppermute x4, waiting for transfers between devices, gathered(): above, below = (lax.ppermute(block, 'x', ring(4, step)) for step in (-1, 1))  11.7 us
    unnamed x48, local copies, waits for them, and re-layouts  11.1 us
    pallas_call x7, Pallas kernels, small_call(): pl.pallas_call(kernel, out_shape=shapes, in_specs=[SCALAR] * scalars + [S...  9.39 us
    ppermute x6, waiting for transfers between devices, gathered(): lax.ppermute(part, 'x', ring(4, step))  8.22 us
    ppermute x6, starting transfers between devices, gathered(): lax.ppermute(part, 'x', ring(4, step))  8.08 us
    ppermute x6, starting transfers between devices, from_y(): return lax.ppermute(block, 'y', ring(4, -step))  7.66 us
  transfers between devices with their start and end apart: 23, of which 10 were waited for; matrix products, arithmetic and copies ran while one was open for 0% of the time, Pallas kernels for 11%

profile of v4, /device:TPU:16, one launch (start us, length us, event | category | flops | bytes accessed | tf_op | source)
XLA Modules:
  0.0 169.8 jit_solution(8212313885370185494)
XLA Ops:
  0.0 1.2 copy-done
  2.1 1.4 collective-permute-start.5
  4.2 1.5 collective-permute-start.1
  5.7 1.7 %collective-permute-start = (bf16[2,512,256]{2,1,0:T(8,128)(2,1)S(1)}, bf16[2,512,256]{2,1,0:T(8,128)(2,1)S(1)}, u32[]{:S(2)}, u32[]{:S(2)}) collective-permute-start(bf16[2,512,256]{2,1,0:T(8,128)(2,1)S(1)} %dynamic-slice_bitcast_fusion.refs_0_), channel_id=1, source_target_pairs={{0,3},{1,0},{2,1},{3,2},{4,7},{5,4},{6,5},{7,6},{8,11},{9,8},{10,9... | collective-permute-start | bytes 1572872 | tf_op jit(solution)/shard_map/ppermute | solution.py:184
  7.4 7.2 %collective-permute-start.6 = (bf16[2,512,256]{2,1,0:T(8,128)(2,1)}, bf16[2,512,256]{2,1,0:T(8,128)(2,1)}, u32[]{:S(2)}, u32[]{:S(2)}) collective-permute-start(bf16[2,512,256]{2,1,0:T(8,128)(2,1)} %dynamic-slice_bitcast_fusion.1), channel_id=1, source_target_pairs={{0,128},{128,0},{1,129},{129,1},{2,130},{130,2},{3,131},{131,3},{4... | collective-permute-start | bytes 1572872 | tf_op jit(solution)/shard_map/ppermute | solution.py:174
  14.6 1.2 collective-permute-done.5.below
  16.9 1.6 collective-permute-done.1.refs_2_
  19.6 1.4 shard_map.17
  21.0 3.0 %collective-permute-start.7 = (bf16[2,512,128]{2,1,0:T(8,128)(2,1)S(1)}, bf16[2,512,128]{2,1,0:T(8,128)(2,1)S(1)}, u32[]{:S(2)}, u32[]{:S(2)}) collective-permute-start(bf16[2,512,128]{2,1,0:T(8,128)(2,1)S(1)} %get-tuple-element.38), channel_id=1, source_target_pairs={{0,3},{1,0},{2,1},{3,2},{4,7},{5,4},{6,5},{7,6},{8,11},{9,8},{10,9... | collective-permute-start | bytes 786440 | tf_op jit(solution)/shard_map/ppermute | solution.py:189
  24.0 1.8 %collective-permute-start.9 = (bf16[2,512,128]{2,1,0:T(8,128)(2,1)S(1)}, bf16[2,512,128]{2,1,0:T(8,128)(2,1)S(1)}, u32[]{:S(2)}, u32[]{:S(2)}) collective-permute-start(bf16[2,512,128]{2,1,0:T(8,128)(2,1)S(1)} %get-tuple-element.40), channel_id=1, source_target_pairs={{0,2},{1,3},{2,0},{3,1},{4,6},{5,7},{6,4},{7,5},{8,10},{9,11},{10,... | collective-permute-start | bytes 786440 | tf_op jit(solution)/shard_map/ppermute | solution.py:189
  25.8 2.2 %collective-permute-done.6.refs_0_.refs_5_ = bf16[2,512,256]{2,1,0:T(8,128)(2,1)} collective-permute-done((bf16[2,512,256]{2,1,0:T(8,128)(2,1)}, bf16[2,512,256]{2,1,0:T(8,128)(2,1)}, u32[]{:S(2)}, u32[]{:S(2)}) %collective-permute-start.6) | collective-permute-done | bytes 524320 | tf_op jit(solution)/shard_map/ppermute | solution.py:174
  28.0 5.5 %collective-permute-done.7.refs_1_ = bf16[2,512,128]{2,1,0:T(8,128)(2,1)S(1)} collective-permute-done((bf16[2,512,128]{2,1,0:T(8,128)(2,1)S(1)}, bf16[2,512,128]{2,1,0:T(8,128)(2,1)S(1)}, u32[]{:S(2)}, u32[]{:S(2)}) %collective-permute-start.7) | collective-permute-done | bytes 262176 | tf_op jit(solution)/shard_map/ppermute | solution.py:189
  34.2 2.7 %collective-permute-done.8.refs_2_ = bf16[2,512,128]{2,1,0:T(8,128)(2,1)S(1)} collective-permute-done((bf16[2,512,128]{2,1,0:T(8,128)(2,1)S(1)}, bf16[2,512,128]{2,1,0:T(8,128)(2,1)S(1)}, u32[]{:S(2)}, u32[]{:S(2)}) %collective-permute-start.8) | collective-permute-done | bytes 262176 | tf_op jit(solution)/shard_map/ppermute | solution.py:189
  38.3 3.2 %collective-permute-start.10 = (bf16[2,512,256]{2,1,0:T(8,128)(2,1)}, bf16[2,512,256]{2,1,0:T(8,128)(2,1)S(1)}, u32[]{:S(2)}, u32[]{:S(2)}) collective-permute-start(bf16[2,512,256]{2,1,0:T(8,128)(2,1)} %collective-permute-done.6.refs_0_.refs_5_), channel_id=1, source_target_pairs={{0,3},{1,0},{2,1},{3,2},{4,7},{5,4},{6,5},{7,6},{8,11},{9,8},{10,9... | collective-permute-start | bytes 1572872 | tf_op jit(solution)/shard_map/ppermute | solution.py:184
  41.6 1.3 collective-permute-start.15
  43.7 10.2 %collective-permute-done.11.refs_2_.refs_7_ = bf16[2,512,256]{2,1,0:T(8,128)(2,1)S(1)} collective-permute-done((bf16[2,512,256]{2,1,0:T(8,128)(2,1)}, bf16[2,512,256]{2,1,0:T(8,128)(2,1)S(1)}, u32[]{:S(2)}, u32[]{:S(2)}) %collective-permute-start.11) | collective-permute-done | bytes 524320 | tf_op jit(solution)/shard_map/ppermute | solution.py:184
  54.4 1.8 %collective-permute-start.13 = (bf16[2,256,256]{2,1,0:T(8,128)(2,1)S(1)}, bf16[2,256,256]{2,1,0:T(8,128)(2,1)S(1)}, u32[]{:S(2)}, u32[]{:S(2)}) collective-permute-start(bf16[2,256,256]{2,1,0:T(8,128)(2,1)S(1)} %slice.19), channel_id=1, source_target_pairs={{0,1},{1,2},{2,3},{3,0},{4,5},{5,6},{6,7},{7,4},{8,9},{9,10},{10,1... | collective-permute-start | bytes 786440 | tf_op jit(solution)/shard_map/ppermute | solution.py:191
  56.7 1.3 collective-permute-start.12
  58.0 2.2 %collective-permute-done.2.refs_3_ = bf16[2,256,256]{2,1,0:T(8,128)(2,1)S(1)} collective-permute-done((bf16[2,256,256]{2,1,0:T(8,128)(2,1)S(1)}, bf16[2,256,256]{2,1,0:T(8,128)(2,1)S(1)}, u32[]{:S(2)}, u32[]{:S(2)}) %collective-permute-start.2) | collective-permute-done | bytes 262176 | tf_op jit(solution)/shard_map/ppermute | solution.py:190
  62.0 1.5 collective-permute-start.20
  64.6 2.4 %shard_map.19.here = bf16[2048,128]{1,0:T(8,128)(2,1)} custom-call(s32[1]{0:T(128)} %bitcast.5.x, bf16[2,512,256]{2,1,0:T(8,128)(2,1)} %collective-permute-done.6.refs_0_.refs_5_, bf16[2,512,256]{2,1,0:T(8,128)(2,1)S(1)} %collective-permute-done.10.refs_1_.refs_6_, bf16[2,512,256]{2,1,0:T(8,128)(2,1)S(1)} %collective-permute-done.11.refs_2_.refs_7_, ...), custom_call_target="tpu_custom_call" | custom-call | bytes 2097152 | tf_op jit(solution)/shard_map/pallas_call | solution.py:94
  67.8 2.1 %collective-permute-start.16 = (bf16[2048,128]{1,0:T(8,128)(2,1)}, bf16[2048,128]{1,0:T(8,128)(2,1)}, u32[]{:S(2)}, u32[]{:S(2)}) collective-permute-start(bf16[2048,128]{1,0:T(8,128)(2,1)} %shard_map.19.here), channel_id=1, source_target_pairs={{0,64},{32,96},{64,0},{96,32},{1,65},{33,97},{65,1},{97,33},{2,66}... | collective-permute-start | bytes 1572872 | tf_op jit(solution)/shard_map/ppermute | solution.py:177
  69.9 1.7 %collective-permute-start.17 = (bf16[2,512,128]{2,1,0:T(8,128)(2,1)}, bf16[2,512,128]{2,1,0:T(8,128)(2,1)S(1)}, u32[]{:S(2)}, u32[]{:S(2)}) collective-permute-start(bf16[2,512,128]{2,1,0:T(8,128)(2,1)} %copy-done.23), channel_id=1, source_target_pairs={{0,3},{1,0},{2,1},{3,2},{4,7},{5,4},{6,5},{7,6},{8,11},{9,8},{10,9... | collective-permute-start | bytes 786440 | tf_op jit(solution)/shard_map/ppermute | solution.py:189
  72.0 1.2 collective-permute-start.19
  77.5 1.3 shard_map.22.refs_10_
  79.0 3.8 %shard_map.23 = (f32[2,4,256,128]{3,2,1,0:T(8,128)S(1)}, f32[8,128]{1,0:T(8,128)S(1)}) custom-call(s32[3]{0:T(128)S(1)} %pad_add_fusion.place, bf16[2,512,256]{2,1,0:T(8,128)(2,1)S(1)} %dynamic-slice_bitcast_fusion.refs_0_, bf16[2,512,256]{2,1,0:T(8,128)(2,1)S(1)} %collective-permute-done.refs_1_, bf16[2,512,256]{2,1,0:T(8,128)(2,1)S(1)} %collective-permute-done.1.refs_2_, ...), custom_call_target="tpu_custom_call" | custom-call | flops 2147483648 | bytes 8388608 | tf_op jit(solution)/shard_map/pallas_call | solution.py:135
  82.9 1.3 shard_map.20.refs_10_
  85.0 3.8 %shard_map.25 = (f32[2,4,256,128]{3,2,1,0:T(8,128)S(1)}, f32[8,128]{1,0:T(8,128)S(1)}) custom-call(s32[3]{0:T(128)S(1)} %pad_add_fusion.place, bf16[2,512,256]{2,1,0:T(8,128)(2,1)S(1)} %dynamic-slice_bitcast_fusion.refs_0_, bf16[2,512,256]{2,1,0:T(8,128)(2,1)S(1)} %collective-permute-done.refs_1_, bf16[2,512,256]{2,1,0:T(8,128)(2,1)S(1)} %collective-permute-done.1.refs_2_, ...), custom_call_target="tpu_custom_call" | custom-call | flops 2147483648 | bytes 8388608 | tf_op jit(solution)/shard_map/pallas_call | solution.py:135
  88.8 3.8 %shard_map.24 = (f32[2,4,256,128]{3,2,1,0:T(8,128)S(1)}, f32[8,128]{1,0:T(8,128)S(1)}) custom-call(s32[3]{0:T(128)S(1)} %pad_add_fusion.place, bf16[2,512,256]{2,1,0:T(8,128)(2,1)S(1)} %dynamic-slice_bitcast_fusion.refs_0_, bf16[2,512,256]{2,1,0:T(8,128)(2,1)S(1)} %collective-permute-done.refs_1_, bf16[2,512,256]{2,1,0:T(8,128)(2,1)S(1)} %collective-permute-done.1.refs_2_, ...), custom_call_target="tpu_custom_call" | custom-call | flops 2147483648 | bytes 8388608 | tf_op jit(solution)/shard_map/pallas_call | solution.py:135
  92.7 4.2 %shard_map.26 = f32[32,264,128]{2,1,0:T(8,128)S(1)} custom-call(s32[3]{0:T(128)S(1)} %pad_add_fusion.place, bf16[2,512,256]{2,1,0:T(8,128)(2,1)S(1)} %dynamic-slice_bitcast_fusion.refs_0_, bf16[2,512,256]{2,1,0:T(8,128)(2,1)S(1)} %collective-permute-done.refs_1_, bf16[2,512,256]{2,1,0:T(8,128)(2,1)S(1)} %collective-permute-done.1.refs_2_, ...), custom_call_target="tpu_custom_call" | custom-call | flops 2147483648 | bytes 8388608 | tf_op jit(solution)/shard_map/pallas_call | solution.py:135
  97.2 70.9 %all_to_all.5 = f16[32,264,128]{2,1,0:T(8,128)(2,1)S(1)} all-to-all(f16[32,264,128]{2,1,0:T(8,128)(2,1)S(1)} %convert_element_type.6), channel_id=1, replica_groups=mesh['zh'=2,'y'=4,'core'=2,'zl'=4,'x'=4] {'zh','zl','x'}, dimensions={0} | all-to-all | bytes 4325376 | tf_op jit(solution)/shard_map/all_to_all | solution.py:211
  168.3 1.5 shard_map.27
  (83 shorter events, 17.5 us)
Async XLA Ops:
  2.1 13.7 %collective-permute-start.5 = (bf16[2,512,256]{2,1,0:T(8,128)(2,1)S(1)}, bf16[2,512,256]{2,1,0:T(8,128)(2,1)S(1)}, u32[]{:S(2)}, u32[]{:S(2)}) collective-permute-start(bf16[2,512,256]{2,1,0:T(8,128)(2,1)S(1)} %dynamic-slice_bitcast_fusion.refs_0_), channel_id=1, source_target_pairs={{0,32},{32,64},{64,96},{96,0},{1,33},{33,65},{65,97},{97,1},{2,34}... | collective-permute-start | bytes 1572872 | tf_op jit(solution)/shard_map/ppermute | solution.py:177
  3.5 13.5 %collective-permute-start.4 = (bf16[2,512,256]{2,1,0:T(8,128)(2,1)S(1)}, bf16[2,512,256]{2,1,0:T(8,128)(2,1)}, u32[]{:S(2)}, u32[]{:S(2)}) collective-permute-start(bf16[2,512,256]{2,1,0:T(8,128)(2,1)S(1)} %dynamic-slice_bitcast_fusion.refs_0_), channel_id=1, source_target_pairs={{0,96},{32,0},{64,32},{96,64},{1,97},{33,1},{65,33},{97,65},{2,98}... | collective-permute-start | bytes 1572872 | tf_op jit(solution)/shard_map/ppermute | solution.py:177
  4.2 14.3 %collective-permute-start.1 = (bf16[2,512,256]{2,1,0:T(8,128)(2,1)S(1)}, bf16[2,512,256]{2,1,0:T(8,128)(2,1)S(1)}, u32[]{:S(2)}, u32[]{:S(2)}) collective-permute-start(bf16[2,512,256]{2,1,0:T(8,128)(2,1)S(1)} %dynamic-slice_bitcast_fusion.refs_0_), channel_id=1, source_target_pairs={{0,1},{1,2},{2,3},{3,0},{4,5},{5,6},{6,7},{7,4},{8,9},{9,10},{10,1... | collective-permute-start | bytes 1572872 | tf_op jit(solution)/shard_map/ppermute | solution.py:184
  5.7 12.8 %collective-permute-start = (bf16[2,512,256]{2,1,0:T(8,128)(2,1)S(1)}, bf16[2,512,256]{2,1,0:T(8,128)(2,1)S(1)}, u32[]{:S(2)}, u32[]{:S(2)}) collective-permute-start(bf16[2,512,256]{2,1,0:T(8,128)(2,1)S(1)} %dynamic-slice_bitcast_fusion.refs_0_), channel_id=1, source_target_pairs={{0,3},{1,0},{2,1},{3,2},{4,7},{5,4},{6,5},{7,6},{8,11},{9,8},{10,9... | collective-permute-start | bytes 1572872 | tf_op jit(solution)/shard_map/ppermute | solution.py:184
  7.4 20.6 %collective-permute-start.6 = (bf16[2,512,256]{2,1,0:T(8,128)(2,1)}, bf16[2,512,256]{2,1,0:T(8,128)(2,1)}, u32[]{:S(2)}, u32[]{:S(2)}) collective-permute-start(bf16[2,512,256]{2,1,0:T(8,128)(2,1)} %dynamic-slice_bitcast_fusion.1), channel_id=1, source_target_pairs={{0,128},{128,0},{1,129},{129,1},{2,130},{130,2},{3,131},{131,3},{4... | collective-permute-start | bytes 1572872 | tf_op jit(solution)/shard_map/ppermute | solution.py:174
  21.0 39.3 %copy-start.11 = (bf16[2,512,128]{2,1,0:T(8,128)(2,1)}, bf16[2,512,128]{2,1,0:T(8,128)(2,1)S(1)}, u32[]{:S(2)}) copy-start(bf16[2,512,128]{2,1,0:T(8,128)(2,1)S(1)} %get-tuple-element.35.refs_0_) | copy-start | bytes 786436
  21.0 12.6 %collective-permute-start.7 = (bf16[2,512,128]{2,1,0:T(8,128)(2,1)S(1)}, bf16[2,512,128]{2,1,0:T(8,128)(2,1)S(1)}, u32[]{:S(2)}, u32[]{:S(2)}) collective-permute-start(bf16[2,512,128]{2,1,0:T(8,128)(2,1)S(1)} %get-tuple-element.38), channel_id=1, source_target_pairs={{0,3},{1,0},{2,1},{3,2},{4,7},{5,4},{6,5},{7,6},{8,11},{9,8},{10,9... | collective-permute-start | bytes 786440 | tf_op jit(solution)/shard_map/ppermute | solution.py:189
  24.0 12.9 %collective-permute-start.8 = (bf16[2,512,128]{2,1,0:T(8,128)(2,1)S(1)}, bf16[2,512,128]{2,1,0:T(8,128)(2,1)S(1)}, u32[]{:S(2)}, u32[]{:S(2)}) collective-permute-start(bf16[2,512,128]{2,1,0:T(8,128)(2,1)S(1)} %get-tuple-element.39), channel_id=1, source_target_pairs={{0,1},{1,2},{2,3},{3,0},{4,5},{5,6},{6,7},{7,4},{8,9},{9,10},{10,1... | collective-permute-start | bytes 786440 | tf_op jit(solution)/shard_map/ppermute | solution.py:189
  24.0 13.6 %collective-permute-start.9 = (bf16[2,512,128]{2,1,0:T(8,128)(2,1)S(1)}, bf16[2,512,128]{2,1,0:T(8,128)(2,1)S(1)}, u32[]{:S(2)}, u32[]{:S(2)}) collective-permute-start(bf16[2,512,128]{2,1,0:T(8,128)(2,1)S(1)} %get-tuple-element.40), channel_id=1, source_target_pairs={{0,2},{1,3},{2,0},{3,1},{4,6},{5,7},{6,4},{7,5},{8,10},{9,11},{10,... | collective-permute-start | bytes 786440 | tf_op jit(solution)/shard_map/ppermute | solution.py:189
  38.3 15.6 %collective-permute-start.11 = (bf16[2,512,256]{2,1,0:T(8,128)(2,1)}, bf16[2,512,256]{2,1,0:T(8,128)(2,1)S(1)}, u32[]{:S(2)}, u32[]{:S(2)}) collective-permute-start(bf16[2,512,256]{2,1,0:T(8,128)(2,1)} %collective-permute-done.6.refs_0_.refs_5_), channel_id=1, source_target_pairs={{0,1},{1,2},{2,3},{3,0},{4,5},{5,6},{6,7},{7,4},{8,9},{9,10},{10,1... | collective-permute-start | bytes 1572872 | tf_op jit(solution)/shard_map/ppermute | solution.py:184
  38.3 16.1 %collective-permute-start.10 = (bf16[2,512,256]{2,1,0:T(8,128)(2,1)}, bf16[2,512,256]{2,1,0:T(8,128)(2,1)S(1)}, u32[]{:S(2)}, u32[]{:S(2)}) collective-permute-start(bf16[2,512,256]{2,1,0:T(8,128)(2,1)} %collective-permute-done.6.refs_0_.refs_5_), channel_id=1, source_target_pairs={{0,3},{1,0},{2,1},{3,2},{4,7},{5,4},{6,5},{7,6},{8,11},{9,8},{10,9... | collective-permute-start | bytes 1572872 | tf_op jit(solution)/shard_map/ppermute | solution.py:184
  41.6 21.9 %collective-permute-start.15 = (bf16[2,512,256]{2,1,0:T(8,128)(2,1)}, bf16[2,512,256]{2,1,0:T(8,128)(2,1)S(1)}, u32[]{:S(2)}, u32[]{:S(2)}) collective-permute-start(bf16[2,512,256]{2,1,0:T(8,128)(2,1)} %collective-permute-done.6.refs_0_.refs_5_), channel_id=1, source_target_pairs={{0,32},{32,64},{64,96},{96,0},{1,33},{33,65},{65,97},{97,1},{2,34}... | collective-permute-start | bytes 1572872 | tf_op jit(solution)/shard_map/ppermute | solution.py:177
  42.8 20.6 %collective-permute-start.14 = (bf16[2,512,256]{2,1,0:T(8,128)(2,1)}, bf16[2,512,256]{2,1,0:T(8,128)(2,1)S(1)}, u32[]{:S(2)}, u32[]{:S(2)}) collective-permute-start(bf16[2,512,256]{2,1,0:T(8,128)(2,1)} %collective-permute-done.6.refs_0_.refs_5_), channel_id=1, source_target_pairs={{0,96},{32,0},{64,32},{96,64},{1,97},{33,1},{65,33},{97,65},{2,98}... | collective-permute-start | bytes 1572872 | tf_op jit(solution)/shard_map/ppermute | solution.py:177
  43.6 13.1 %collective-permute-start.3 = (bf16[2,256,256]{2,1,0:T(8,128)(2,1)S(1)}, bf16[2,256,256]{2,1,0:T(8,128)(2,1)S(1)}, u32[]{:S(2)}, u32[]{:S(2)}) collective-permute-start(bf16[2,256,256]{2,1,0:T(8,128)(2,1)S(1)} %slice.17), channel_id=1, source_target_pairs={{0,1},{1,2},{2,3},{3,0},{4,5},{5,6},{6,7},{7,4},{8,9},{9,10},{10,1... | collective-permute-start | bytes 786440 | tf_op jit(solution)/shard_map/ppermute | solution.py:191
  53.9 6.4 %collective-permute-start.2 = (bf16[2,256,256]{2,1,0:T(8,128)(2,1)S(1)}, bf16[2,256,256]{2,1,0:T(8,128)(2,1)S(1)}, u32[]{:S(2)}, u32[]{:S(2)}) collective-permute-start(bf16[2,256,256]{2,1,0:T(8,128)(2,1)S(1)} %slice.16), channel_id=1, source_target_pairs={{0,3},{1,0},{2,1},{3,2},{4,7},{5,4},{6,5},{7,6},{8,11},{9,8},{10,9... | collective-permute-start | bytes 786440 | tf_op jit(solution)/shard_map/ppermute | solution.py:190
  54.4 12.6 %copy-start.1 = (bf16[2,512,256]{2,1,0:T(8,128)(2,1)}, bf16[2,512,256]{2,1,0:T(8,128)(2,1)S(1)}, u32[]{:S(2)}) copy-start(bf16[2,512,256]{2,1,0:T(8,128)(2,1)S(1)} %collective-permute-done.10.refs_1_.refs_6_) | copy-start | bytes 1572868
  54.4 10.1 %collective-permute-start.13 = (bf16[2,256,256]{2,1,0:T(8,128)(2,1)S(1)}, bf16[2,256,256]{2,1,0:T(8,128)(2,1)S(1)}, u32[]{:S(2)}, u32[]{:S(2)}) collective-permute-start(bf16[2,256,256]{2,1,0:T(8,128)(2,1)S(1)} %slice.19), channel_id=1, source_target_pairs={{0,1},{1,2},{2,3},{3,0},{4,5},{5,6},{6,7},{7,4},{8,9},{9,10},{10,1... | collective-permute-start | bytes 786440 | tf_op jit(solution)/shard_map/ppermute | solution.py:191
  56.7 7.9 %collective-permute-start.12 = (bf16[2,256,256]{2,1,0:T(8,128)(2,1)S(1)}, bf16[2,256,256]{2,1,0:T(8,128)(2,1)S(1)}, u32[]{:S(2)}, u32[]{:S(2)}) collective-permute-start(bf16[2,256,256]{2,1,0:T(8,128)(2,1)S(1)} %slice.18), channel_id=1, source_target_pairs={{0,3},{1,0},{2,1},{3,2},{4,7},{5,4},{6,5},{7,6},{8,11},{9,8},{10,9... | collective-permute-start | bytes 786440 | tf_op jit(solution)/shard_map/ppermute | solution.py:190
  62.0 11.6 %collective-permute-start.20 = (bf16[2048,128]{1,0:T(8,128)(2,1)}, bf16[2048,128]{1,0:T(8,128)(2,1)}, u32[]{:S(2)}, u32[]{:S(2)}) collective-permute-start(bf16[2048,128]{1,0:T(8,128)(2,1)} %shard_map.21.here), channel_id=1, source_target_pairs={{0,64},{32,96},{64,0},{96,32},{1,65},{33,97},{65,1},{97,33},{2,66}... | collective-permute-start | bytes 1572872 | tf_op jit(solution)/shard_map/ppermute | solution.py:177
  64.6 2.5 %copy-start.22 = (bf16[2,512,128]{2,1,0:T(8,128)(2,1)}, bf16[2,512,128]{2,1,0:T(8,128)(2,1)S(1)}, u32[]{:S(2)}) copy-start(bf16[2,512,128]{2,1,0:T(8,128)(2,1)S(1)} %get-tuple-element.48) | copy-start | bytes 786436
  64.6 2.5 %copy-start.23 = (bf16[2,512,128]{2,1,0:T(8,128)(2,1)}, bf16[2,512,128]{2,1,0:T(8,128)(2,1)S(1)}, u32[]{:S(2)}) copy-start(bf16[2,512,128]{2,1,0:T(8,128)(2,1)S(1)} %get-tuple-element.47) | copy-start | bytes 786436
  67.8 15.1 %collective-permute-start.16 = (bf16[2048,128]{1,0:T(8,128)(2,1)}, bf16[2048,128]{1,0:T(8,128)(2,1)}, u32[]{:S(2)}, u32[]{:S(2)}) collective-permute-start(bf16[2048,128]{1,0:T(8,128)(2,1)} %shard_map.19.here), channel_id=1, source_target_pairs={{0,64},{32,96},{64,0},{96,32},{1,65},{33,97},{65,1},{97,33},{2,66}... | collective-permute-start | bytes 1572872 | tf_op jit(solution)/shard_map/ppermute | solution.py:177
  69.8 9.1 %copy-start.2 = (bf16[2,512,256]{2,1,0:T(8,128)(2,1)S(1)}, bf16[2,512,256]{2,1,0:T(8,128)(2,1)}, u32[]{:S(2)}) copy-start(bf16[2,512,256]{2,1,0:T(8,128)(2,1)} %copy-done.1) | copy-start | bytes 1572868
  69.8 9.1 %copy-start.4 = (bf16[2,256,256]{2,1,0:T(8,128)(2,1)S(1)}, bf16[2,256,256]{2,1,0:T(8,128)(2,1)}, u32[]{:S(2)}) copy-start(bf16[2,256,256]{2,1,0:T(8,128)(2,1)} %copy-done.3) | copy-start | bytes 786436
  69.8 9.1 %copy-start.6 = (bf16[2,256,256]{2,1,0:T(8,128)(2,1)S(1)}, bf16[2,256,256]{2,1,0:T(8,128)(2,1)}, u32[]{:S(2)}) copy-start(bf16[2,256,256]{2,1,0:T(8,128)(2,1)} %copy-done.5) | copy-start | bytes 786436
  69.9 9.1 %copy-start.8 = (bf16[2,256,256]{2,1,0:T(8,128)(2,1)S(1)}, bf16[2,256,256]{2,1,0:T(8,128)(2,1)}, u32[]{:S(2)}) copy-start(bf16[2,256,256]{2,1,0:T(8,128)(2,1)} %copy-done.7) | copy-start | bytes 786436
  69.9 12.9 %collective-permute-start.17 = (bf16[2,512,128]{2,1,0:T(8,128)(2,1)}, bf16[2,512,128]{2,1,0:T(8,128)(2,1)S(1)}, u32[]{:S(2)}, u32[]{:S(2)}) collective-permute-start(bf16[2,512,128]{2,1,0:T(8,128)(2,1)} %copy-done.23), channel_id=1, source_target_pairs={{0,3},{1,0},{2,1},{3,2},{4,7},{5,4},{6,5},{7,6},{8,11},{9,8},{10,9... | collective-permute-start | bytes 786440 | tf_op jit(solution)/shard_map/ppermute | solution.py:189
  71.6 11.2 %collective-permute-start.18 = (bf16[2,512,128]{2,1,0:T(8,128)(2,1)}, bf16[2,512,128]{2,1,0:T(8,128)(2,1)S(1)}, u32[]{:S(2)}, u32[]{:S(2)}) collective-permute-start(bf16[2,512,128]{2,1,0:T(8,128)(2,1)} %copy-done.22), channel_id=1, source_target_pairs={{0,1},{1,2},{2,3},{3,0},{4,5},{5,6},{6,7},{7,4},{8,9},{9,10},{10,1... | collective-permute-start | bytes 786440 | tf_op jit(solution)/shard_map/ppermute | solution.py:189
  72.0 10.9 %collective-permute-start.19 = (bf16[2,512,128]{2,1,0:T(8,128)(2,1)}, bf16[2,512,128]{2,1,0:T(8,128)(2,1)S(1)}, u32[]{:S(2)}, u32[]{:S(2)}) collective-permute-start(bf16[2,512,128]{2,1,0:T(8,128)(2,1)} %copy-done.21), channel_id=1, source_target_pairs={{0,2},{1,3},{2,0},{3,1},{4,6},{5,7},{6,4},{7,5},{8,10},{9,11},{10,... | collective-permute-start | bytes 786440 | tf_op jit(solution)/shard_map/ppermute | solution.py:189
  78.8 4.0 %copy-start.20 = (bf16[2,512,128]{2,1,0:T(8,128)(2,1)S(1)}, bf16[2,512,128]{2,1,0:T(8,128)(2,1)}, u32[]{:S(2)}) copy-start(bf16[2,512,128]{2,1,0:T(8,128)(2,1)} %copy-done.19) | copy-start | bytes 786436
  78.8 10.0 %collective-permute-start.22 = (bf16[4,2048,128]{2,1,0:T(8,128)(2,1)S(1)}, bf16[4,2048,128]{2,1,0:T(8,128)(2,1)S(1)}, u32[]{:S(2)}, u32[]{:S(2)}) collective-permute-start(bf16[4,2048,128]{2,1,0:T(8,128)(2,1)S(1)} %shard_map.22.refs_10_), channel_id=1, source_target_pairs={{0,16},{16,0},{1,17},{17,1},{2,18},{18,2},{3,19},{19,3},{4,20},{20... | collective-permute-start | bytes 6291464 | tf_op jit(solution)/shard_map/ppermute | solution.py:180
  84.2 8.5 %collective-permute-start.21 = (bf16[4,2048,128]{2,1,0:T(8,128)(2,1)S(1)}, bf16[4,2048,128]{2,1,0:T(8,128)(2,1)S(1)}, u32[]{:S(2)}, u32[]{:S(2)}) collective-permute-start(bf16[4,2048,128]{2,1,0:T(8,128)(2,1)S(1)} %shard_map.20.refs_10_), channel_id=1, source_target_pairs={{0,16},{16,0},{1,17},{17,1},{2,18},{18,2},{3,19},{19,3},{4,20},{20... | collective-permute-start | bytes 6291464 | tf_op jit(solution)/shard_map/ppermute | solution.py:180
  (15 other events, 16.1 us)

commit v5 on v4

--- a/solution.py
+++ b/solution.py
@@ -23,7 +23,7 @@
 
 def add_terms(place, *refs):
     f, y = place[0], place[1]
-    blocks, (cols, out, top) = (refs[:5], refs[5:10]), refs[10:]
+    blocks, (cols, out, top) = (refs[:4], refs[4:9]), refs[9:]
     n, c = out.shape[2:]
     first = lax.broadcasted_iota(jnp.int32, (n, 2 * c), 1) % c < c // 2
     top[...] = jnp.zeros_like(top)
@@ -102,8 +102,8 @@
 
 
 def last_kernel(place, *refs):
-    term0, top0, term1, top1, term2, top2, out, term3, top3 = refs[11:]
-    add_terms(place, *refs[:11], term3, top3)
+    term0, top0, term1, top1, term2, top2, out, term3, top3 = refs[10:]
+    add_terms(place, *refs[:10], term3, top3)
     f, core = place[0], place[2]
     n, c = term3.shape[2:]
     largest = jnp.max(jnp.maximum(jnp.maximum(top0[...], top1[...]), jnp.maximum(top2[...], top3[...])))
@@ -179,7 +179,7 @@
     def from_core(piece):
         return lax.ppermute(piece, "core", ring(2, 1))
 
-    def gathered(block, *late):
+    def gathered(block, ways, *late):
         shots = block.shape[1]
         above, below = (lax.ppermute(block, "x", ring(4, step)) for step in (-1, 1))
         near = [from_y(block, 1), from_y(block, 3)]
@@ -187,19 +187,20 @@
         cut = jax.ShapeDtypeStruct((2, shots, 2 * group), block.dtype)
         kept, *sent = small_call(near_kernel, (cut,) * 4, x[None], *near)
         moved = [lax.ppermute(part, "x", ring(4, step)) for part, step in zip(sent, (-1, 1, 2))]
-        far_a = lax.ppermute(above[:, : shots // 2], "x", ring(4, -1))
-        far_b = lax.ppermute(below[:, shots // 2 :], "x", ring(4, 1))
-        far_a, far_b = lax.optimization_barrier((far_a, far_b, kept, *late))[:2]
-        pieces = [block, above, below, far_a, far_b]
+        relayed = [lax.ppermute(above[:, : shots // ways], "x", ring(4, -1))]
+        if ways == 2:
+            relayed.append(lax.ppermute(below[:, shots // 2 :], "x", ring(4, 1)))
+        done = [*moved, *relayed]
+        pieces = [block, above, below, *lax.optimization_barrier((*relayed, kept, *late))[:ways]]
         here = jax.ShapeDtypeStruct((4 * shots, 2 * group), block.dtype)
         here = small_call(own_kernel, here, x[None], *pieces)
         far = from_y(here, 2)
         cols = jax.ShapeDtypeStruct((4, *here.shape), block.dtype)
         cols = small_call(join_kernel, cols, here, far, kept, *moved, scalars=0)
-        return pieces, cols, moved
-
-    rows0, mine0, moved0 = gathered(own, other)
-    rows1, mine1, _ = gathered(first_of(other, *moved0))
+        return pieces, cols, done
+
+    rows0, mine0, done0 = gathered(own, 1, other)
+    rows1, mine1, _ = gathered(first_of(other, *done0), 2)
     rows = (*rows0, *rows1)
 
     place = jnp.stack([f, y, core])

time: 171 us -> 171 us (level)
  blocking collectives: 70.9 us -> 63.3 us
  waiting for transfers between devices: 26.8 us -> 34.1 us
    all_to_all x1, blocking collectives: 70.9 us -> 63.3 us  [body(): got = lax.all_to_all(sent, ('zh', 'zl', 'x'), 0, 0, tiled=True)]
    ppermute x6, waiting for transfers between devices: 8.22 us -> 13.6 us  [gathered(): lax.ppermute(part, 'x', ring(4, step))]
    ppermute x6, waiting for transfers between devices: 1.97 us -> 6.73 us  [from_y(): return lax.ppermute(block, 'y', ring(4, -step))]
    ppermute x6, starting transfers between devices: 8.08 us -> 4.16 us  [gathered(): lax.ppermute(part, 'x', ring(4, step))]
    ppermute x4 -> x3, starting transfers between devices: 3.7 us -> 7.24 us  [the longest x2 7.16 us: gathered(): relayed = [lax.ppermute(above[:, :shots // ways], 'x', ring(4, -1))]]
    ppermute x4 -> x3, waiting for transfers between devices: 2.69 us -> 0.01 us  [the longest x2 0.01 us: gathered(): relayed = [lax.ppermute(above[:, :shots // ways], 'x', ring(4, -1))]]
    unnamed x48 -> x44, local copies, waits for them, and re-layouts: 11.1 us -> 12.2 us
  transfers between devices with their start and end apart: 23 -> 22, of which waited for: 10 -> 6; matrix products, arithmetic and copies ran while one was open for 0% -> 0% of each run, Pallas kernels for 11% -> 12%
where the time goes in v5:
time: 171 us; the launch traced here: 170 us
  blocking collectives  63.3 us (37%)
  waiting for transfers between devices  34.1 us (20%)
  starting transfers between devices  33.6 us (20%)
  Pallas kernels  25.3 us (15%)
  local copies, waits for them, and re-layouts  13.1 us (8%)
    all_to_all x1, blocking collectives, body(): got = lax.all_to_all(sent, ('zh', 'zl', 'x'), 0, 0, tiled=True)  63.3 us
    pallas_call x4, Pallas kernels, terms_of(): pl.pallas_call(kernel, out_shape=shapes, in_specs=[SCALAR] + [SPACE] * (l...  15.7 us
    ppermute x6, waiting for transfers between devices, gathered(): lax.ppermute(part, 'x', ring(4, step))  13.6 us
    unnamed x44, local copies, waits for them, and re-layouts  12.2 us
    ppermute x4, waiting for transfers between devices, gathered(): above, below = (lax.ppermute(block, 'x', ring(4, step)) for step in (-1, 1))  11.5 us
    pallas_call x7, Pallas kernels, small_call(): pl.pallas_call(kernel, out_shape=shapes, in_specs=[SCALAR] * scalars + [S...  9.64 us
    ppermute x6, starting transfers between devices, from_y(): return lax.ppermute(block, 'y', ring(4, -step))  7.58 us
    ppermute x1, starting transfers between devices, body(): other = lax.ppermute(other, 'zh', ring(2, 1))  7.19 us
  transfers between devices with their start and end apart: 22, of which 6 were waited for; matrix products, arithmetic and copies ran while one was open for 0% of the time, Pallas kernels for 12%

profile of v5, /device:TPU:16, one launch (start us, length us, event | category | flops | bytes accessed | tf_op | source)
XLA Modules:
  0.0 170.3 jit_solution(15691383110628745178)
XLA Ops:
  0.0 1.2 copy-done
  2.1 2.8 %collective-permute-start = (bf16[2,512,256]{2,1,0:T(8,128)(2,1)S(1)}, bf16[2,512,256]{2,1,0:T(8,128)(2,1)S(1)}, u32[]{:S(2)}, u32[]{:S(2)}) collective-permute-start(bf16[2,512,256]{2,1,0:T(8,128)(2,1)S(1)} %dynamic-slice_bitcast_fusion.refs_0_), channel_id=1, source_target_pairs={{0,3},{1,0},{2,1},{3,2},{4,7},{5,4},{6,5},{7,6},{8,11},{9,8},{10,9... | collective-permute-start | bytes 1572872 | tf_op jit(solution)/shard_map/ppermute | solution.py:184
  5.0 1.3 collective-permute-start.4
  7.0 7.2 %collective-permute-start.5 = (bf16[2,512,256]{2,1,0:T(8,128)(2,1)}, bf16[2,512,256]{2,1,0:T(8,128)(2,1)}, u32[]{:S(2)}, u32[]{:S(2)}) collective-permute-start(bf16[2,512,256]{2,1,0:T(8,128)(2,1)} %dynamic-slice_bitcast_fusion.1), channel_id=1, source_target_pairs={{0,128},{128,0},{1,129},{129,1},{2,130},{130,2},{3,131},{131,3},{4... | collective-permute-start | bytes 1572872 | tf_op jit(solution)/shard_map/ppermute | solution.py:174
  14.2 2.0 %collective-permute-done.refs_1_ = bf16[2,512,256]{2,1,0:T(8,128)(2,1)S(1)} collective-permute-done((bf16[2,512,256]{2,1,0:T(8,128)(2,1)S(1)}, bf16[2,512,256]{2,1,0:T(8,128)(2,1)S(1)}, u32[]{:S(2)}, u32[]{:S(2)}) %collective-permute-start) | collective-permute-done | bytes 524320 | tf_op jit(solution)/shard_map/ppermute | solution.py:184
  16.1 3.7 %collective-permute-start.2 = (bf16[2,512,256]{2,1,0:T(8,128)(2,1)S(1)}, bf16[2,512,256]{2,1,0:T(8,128)(2,1)S(1)}, u32[]{:S(2)}, u32[]{:S(2)}) collective-permute-start(bf16[2,512,256]{2,1,0:T(8,128)(2,1)S(1)} %collective-permute-done.refs_1_), channel_id=1, source_target_pairs={{0,3},{1,0},{2,1},{3,2},{4,7},{5,4},{6,5},{7,6},{8,11},{9,8},{10,9... | collective-permute-start | bytes 1572872 | tf_op jit(solution)/shard_map/ppermute | solution.py:190
  19.8 1.2 collective-permute-done.1.refs_2_
  21.0 1.7 %shard_map.17 = (bf16[2,512,128]{2,1,0:T(8,128)(2,1)S(1)}, bf16[2,512,128]{2,1,0:T(8,128)(2,1)S(1)}, bf16[2,512,128]{2,1,0:T(8,128)(2,1)S(1)}, bf16[2,512,128]{2,1,0:T(8,128)(2,1)S(1)}) custom-call(s32[1]{0:T(128)} %bitcast.5.x, bf16[2,512,256]{2,1,0:T(8,128)(2,1)} %collective-permute-done.3.above, bf16[2,512,256]{2,1,0:T(8,128)(2,1)} %collective-permute-done.4.below), custom_call_target="tpu_custom_call" | custom-call | bytes 1048576 | tf_op jit(solution)/shard_map/pallas_call | solution.py:94
  23.5 2.0 %collective-permute-start.7 = (bf16[2,512,128]{2,1,0:T(8,128)(2,1)S(1)}, bf16[2,512,128]{2,1,0:T(8,128)(2,1)S(1)}, u32[]{:S(2)}, u32[]{:S(2)}) collective-permute-start(bf16[2,512,128]{2,1,0:T(8,128)(2,1)S(1)} %get-tuple-element.37), channel_id=1, source_target_pairs={{0,1},{1,2},{2,3},{3,0},{4,5},{5,6},{6,7},{7,4},{8,9},{9,10},{10,1... | collective-permute-start | bytes 786440 | tf_op jit(solution)/shard_map/ppermute | solution.py:189
  25.5 2.3 %collective-permute-done.5.refs_0_.refs_4_ = bf16[2,512,256]{2,1,0:T(8,128)(2,1)} collective-permute-done((bf16[2,512,256]{2,1,0:T(8,128)(2,1)}, bf16[2,512,256]{2,1,0:T(8,128)(2,1)}, u32[]{:S(2)}, u32[]{:S(2)}) %collective-permute-start.5) | collective-permute-done | bytes 524320 | tf_op jit(solution)/shard_map/ppermute | solution.py:174
  27.8 13.5 %collective-permute-done.6.refs_1_ = bf16[2,512,128]{2,1,0:T(8,128)(2,1)S(1)} collective-permute-done((bf16[2,512,128]{2,1,0:T(8,128)(2,1)S(1)}, bf16[2,512,128]{2,1,0:T(8,128)(2,1)S(1)}, u32[]{:S(2)}, u32[]{:S(2)}) %collective-permute-start.6) | collective-permute-done | bytes 262176 | tf_op jit(solution)/shard_map/ppermute | solution.py:189
  44.5 3.5 %collective-permute-start.9 = (bf16[2,512,256]{2,1,0:T(8,128)(2,1)}, bf16[2,512,256]{2,1,0:T(8,128)(2,1)S(1)}, u32[]{:S(2)}, u32[]{:S(2)}) collective-permute-start(bf16[2,512,256]{2,1,0:T(8,128)(2,1)} %collective-permute-done.5.refs_0_.refs_4_), channel_id=1, source_target_pairs={{0,3},{1,0},{2,1},{3,2},{4,7},{5,4},{6,5},{7,6},{8,11},{9,8},{10,9... | collective-permute-start | bytes 1572872 | tf_op jit(solution)/shard_map/ppermute | solution.py:184
  48.1 1.4 collective-permute-start.14
  50.1 8.3 %collective-permute-done.10.refs_2_.refs_6_ = bf16[2,512,256]{2,1,0:T(8,128)(2,1)S(1)} collective-permute-done((bf16[2,512,256]{2,1,0:T(8,128)(2,1)}, bf16[2,512,256]{2,1,0:T(8,128)(2,1)S(1)}, u32[]{:S(2)}, u32[]{:S(2)}) %collective-permute-start.10) | collective-permute-done | bytes 524320 | tf_op jit(solution)/shard_map/ppermute | solution.py:184
  58.6 3.5 %collective-permute-start.11 = (bf16[2,256,256]{2,1,0:T(8,128)(2,1)S(1)}, bf16[2,256,256]{2,1,0:T(8,128)(2,1)S(1)}, u32[]{:S(2)}, u32[]{:S(2)}) collective-permute-start(bf16[2,256,256]{2,1,0:T(8,128)(2,1)S(1)} %slice.8), channel_id=1, source_target_pairs={{0,3},{1,0},{2,1},{3,2},{4,7},{5,4},{6,5},{7,6},{8,11},{9,8},{10,9... | collective-permute-start | bytes 786440 | tf_op jit(solution)/shard_map/ppermute | solution.py:190
  62.0 1.0 copy-done.2
  63.1 1.0 copy-done.5
  64.1 1.0 shard_map.21.here
  66.8 2.4 %shard_map.19.here = bf16[2048,128]{1,0:T(8,128)(2,1)} custom-call(s32[1]{0:T(128)} %bitcast.5.x, bf16[2,512,256]{2,1,0:T(8,128)(2,1)} %collective-permute-done.5.refs_0_.refs_4_, bf16[2,512,256]{2,1,0:T(8,128)(2,1)S(1)} %collective-permute-done.9.refs_1_.refs_5_, bf16[2,512,256]{2,1,0:T(8,128)(2,1)S(1)} %collective-permute-done.10.refs_2_.refs_6_, ...), custom_call_target="tpu_custom_call" | custom-call | bytes 2097152 | tf_op jit(solution)/shard_map/pallas_call | solution.py:94
  69.9 3.0 %collective-permute-start.15 = (bf16[2048,128]{1,0:T(8,128)(2,1)}, bf16[2048,128]{1,0:T(8,128)(2,1)}, u32[]{:S(2)}, u32[]{:S(2)}) collective-permute-start(bf16[2048,128]{1,0:T(8,128)(2,1)} %shard_map.19.here), channel_id=1, source_target_pairs={{0,64},{32,96},{64,0},{96,32},{1,65},{33,97},{65,1},{97,33},{2,66}... | collective-permute-start | bytes 1572872 | tf_op jit(solution)/shard_map/ppermute | solution.py:177
  73.5 1.4 collective-permute-start.17
  75.1 6.7 %collective-permute-done.19.far = bf16[2048,128]{1,0:T(8,128)(2,1)} collective-permute-done((bf16[2048,128]{1,0:T(8,128)(2,1)}, bf16[2048,128]{1,0:T(8,128)(2,1)}, u32[]{:S(2)}, u32[]{:S(2)}) %collective-permute-start.19) | collective-permute-done | bytes 524320 | tf_op jit(solution)/shard_map/ppermute | solution.py:177
  81.8 0.9 copy-done.10
  82.8 0.9 copy-done.12
  85.6 1.3 shard_map.22.refs_9_
  87.1 3.8 %shard_map.23 = (f32[2,4,256,128]{3,2,1,0:T(8,128)S(1)}, f32[8,128]{1,0:T(8,128)S(1)}) custom-call(s32[3]{0:T(128)S(1)} %pad_add_fusion.place, bf16[2,512,256]{2,1,0:T(8,128)(2,1)S(1)} %dynamic-slice_bitcast_fusion.refs_0_, bf16[2,512,256]{2,1,0:T(8,128)(2,1)S(1)} %collective-permute-done.refs_1_, bf16[2,512,256]{2,1,0:T(8,128)(2,1)S(1)} %copy-done.3, ...), custom_call_target="tpu_custom_call" | custom-call | flops 2147483648 | bytes 8388608 | tf_op jit(solution)/shard_map/pallas_call | solution.py:135
  91.0 1.3 shard_map.20.refs_9_
  93.1 3.8 %shard_map.25 = (f32[2,4,256,128]{3,2,1,0:T(8,128)S(1)}, f32[8,128]{1,0:T(8,128)S(1)}) custom-call(s32[3]{0:T(128)S(1)} %pad_add_fusion.place, bf16[2,512,256]{2,1,0:T(8,128)(2,1)S(1)} %dynamic-slice_bitcast_fusion.refs_0_, bf16[2,512,256]{2,1,0:T(8,128)(2,1)S(1)} %collective-permute-done.refs_1_, bf16[2,512,256]{2,1,0:T(8,128)(2,1)S(1)} %copy-done.3, ...), custom_call_target="tpu_custom_call" | custom-call | flops 2147483648 | bytes 8388608 | tf_op jit(solution)/shard_map/pallas_call | solution.py:135
  97.0 3.8 %shard_map.24 = (f32[2,4,256,128]{3,2,1,0:T(8,128)S(1)}, f32[8,128]{1,0:T(8,128)S(1)}) custom-call(s32[3]{0:T(128)S(1)} %pad_add_fusion.place, bf16[2,512,256]{2,1,0:T(8,128)(2,1)S(1)} %dynamic-slice_bitcast_fusion.refs_0_, bf16[2,512,256]{2,1,0:T(8,128)(2,1)S(1)} %collective-permute-done.refs_1_, bf16[2,512,256]{2,1,0:T(8,128)(2,1)S(1)} %copy-done.3, ...), custom_call_target="tpu_custom_call" | custom-call | flops 2147483648 | bytes 8388608 | tf_op jit(solution)/shard_map/pallas_call | solution.py:135
  100.8 4.2 %shard_map.26 = f32[32,264,128]{2,1,0:T(8,128)S(1)} custom-call(s32[3]{0:T(128)S(1)} %pad_add_fusion.place, bf16[2,512,256]{2,1,0:T(8,128)(2,1)S(1)} %dynamic-slice_bitcast_fusion.refs_0_, bf16[2,512,256]{2,1,0:T(8,128)(2,1)S(1)} %collective-permute-done.refs_1_, bf16[2,512,256]{2,1,0:T(8,128)(2,1)S(1)} %copy-done.3, bf16[2,512,256]{2,1,0:T(8,128)(2,1)S(1)} %copy-done.6, ...), custom_call_target="tpu_custom_call" | custom-call | flops 2147483648 | bytes 8388608 | tf_op jit(solution)/shard_map/pallas_call | solution.py:135
  105.3 63.3 %all_to_all.5 = f16[32,264,128]{2,1,0:T(8,128)(2,1)S(1)} all-to-all(f16[32,264,128]{2,1,0:T(8,128)(2,1)S(1)} %convert_element_type.6), channel_id=1, replica_groups=mesh['zh'=2,'y'=4,'core'=2,'zl'=4,'x'=4] {'zh','zl','x'}, dimensions={0} | all-to-all | bytes 4325376 | tf_op jit(solution)/shard_map/all_to_all | solution.py:212
  168.9 1.5 shard_map.27
  (75 shorter events, 12.7 us)
Async XLA Ops:
  0.0 1.2 copy-start
  2.1 14.0 %collective-permute-start = (bf16[2,512,256]{2,1,0:T(8,128)(2,1)S(1)}, bf16[2,512,256]{2,1,0:T(8,128)(2,1)S(1)}, u32[]{:S(2)}, u32[]{:S(2)}) collective-permute-start(bf16[2,512,256]{2,1,0:T(8,128)(2,1)S(1)} %dynamic-slice_bitcast_fusion.refs_0_), channel_id=1, source_target_pairs={{0,3},{1,0},{2,1},{3,2},{4,7},{5,4},{6,5},{7,6},{8,11},{9,8},{10,9... | collective-permute-start | bytes 1572872 | tf_op jit(solution)/shard_map/ppermute | solution.py:184
  5.0 14.9 %collective-permute-start.4 = (bf16[2,512,256]{2,1,0:T(8,128)(2,1)S(1)}, bf16[2,512,256]{2,1,0:T(8,128)(2,1)}, u32[]{:S(2)}, u32[]{:S(2)}) collective-permute-start(bf16[2,512,256]{2,1,0:T(8,128)(2,1)S(1)} %dynamic-slice_bitcast_fusion.refs_0_), channel_id=1, source_target_pairs={{0,32},{32,64},{64,96},{96,0},{1,33},{33,65},{65,97},{97,1},{2,34}... | collective-permute-start | bytes 1572872 | tf_op jit(solution)/shard_map/ppermute | solution.py:177
  6.2 13.6 %collective-permute-start.3 = (bf16[2,512,256]{2,1,0:T(8,128)(2,1)S(1)}, bf16[2,512,256]{2,1,0:T(8,128)(2,1)}, u32[]{:S(2)}, u32[]{:S(2)}) collective-permute-start(bf16[2,512,256]{2,1,0:T(8,128)(2,1)S(1)} %dynamic-slice_bitcast_fusion.refs_0_), channel_id=1, source_target_pairs={{0,96},{32,0},{64,32},{96,64},{1,97},{33,1},{65,33},{97,65},{2,98}... | collective-permute-start | bytes 1572872 | tf_op jit(solution)/shard_map/ppermute | solution.py:177
  7.0 14.0 %collective-permute-start.1 = (bf16[2,512,256]{2,1,0:T(8,128)(2,1)S(1)}, bf16[2,512,256]{2,1,0:T(8,128)(2,1)S(1)}, u32[]{:S(2)}, u32[]{:S(2)}) collective-permute-start(bf16[2,512,256]{2,1,0:T(8,128)(2,1)S(1)} %dynamic-slice_bitcast_fusion.refs_0_), channel_id=1, source_target_pairs={{0,1},{1,2},{2,3},{3,0},{4,5},{5,6},{6,7},{7,4},{8,9},{9,10},{10,1... | collective-permute-start | bytes 1572872 | tf_op jit(solution)/shard_map/ppermute | solution.py:184
  7.0 20.8 %collective-permute-start.5 = (bf16[2,512,256]{2,1,0:T(8,128)(2,1)}, bf16[2,512,256]{2,1,0:T(8,128)(2,1)}, u32[]{:S(2)}, u32[]{:S(2)}) collective-permute-start(bf16[2,512,256]{2,1,0:T(8,128)(2,1)} %dynamic-slice_bitcast_fusion.1), channel_id=1, source_target_pairs={{0,128},{128,0},{1,129},{129,1},{2,130},{130,2},{3,131},{131,3},{4... | collective-permute-start | bytes 1572872 | tf_op jit(solution)/shard_map/ppermute | solution.py:174
  16.1 27.4 %collective-permute-start.2 = (bf16[2,512,256]{2,1,0:T(8,128)(2,1)S(1)}, bf16[2,512,256]{2,1,0:T(8,128)(2,1)S(1)}, u32[]{:S(2)}, u32[]{:S(2)}) collective-permute-start(bf16[2,512,256]{2,1,0:T(8,128)(2,1)S(1)} %collective-permute-done.refs_1_), channel_id=1, source_target_pairs={{0,3},{1,0},{2,1},{3,2},{4,7},{5,4},{6,5},{7,6},{8,11},{9,8},{10,9... | collective-permute-start | bytes 1572872 | tf_op jit(solution)/shard_map/ppermute | solution.py:190
  21.0 21.8 %copy-start.1 = (bf16[2,512,256]{2,1,0:T(8,128)(2,1)}, bf16[2,512,256]{2,1,0:T(8,128)(2,1)S(1)}, u32[]{:S(2)}) copy-start(bf16[2,512,256]{2,1,0:T(8,128)(2,1)S(1)} %collective-permute-done.1.refs_2_) | copy-start | bytes 1572868
  23.5 17.9 %collective-permute-start.6 = (bf16[2,512,128]{2,1,0:T(8,128)(2,1)S(1)}, bf16[2,512,128]{2,1,0:T(8,128)(2,1)S(1)}, u32[]{:S(2)}, u32[]{:S(2)}) collective-permute-start(bf16[2,512,128]{2,1,0:T(8,128)(2,1)S(1)} %get-tuple-element.36), channel_id=1, source_target_pairs={{0,3},{1,0},{2,1},{3,2},{4,7},{5,4},{6,5},{7,6},{8,11},{9,8},{10,9... | collective-permute-start | bytes 786440 | tf_op jit(solution)/shard_map/ppermute | solution.py:189
  23.5 18.6 %collective-permute-start.7 = (bf16[2,512,128]{2,1,0:T(8,128)(2,1)S(1)}, bf16[2,512,128]{2,1,0:T(8,128)(2,1)S(1)}, u32[]{:S(2)}, u32[]{:S(2)}) collective-permute-start(bf16[2,512,128]{2,1,0:T(8,128)(2,1)S(1)} %get-tuple-element.37), channel_id=1, source_target_pairs={{0,1},{1,2},{2,3},{3,0},{4,5},{5,6},{6,7},{7,4},{8,9},{9,10},{10,1... | collective-permute-start | bytes 786440 | tf_op jit(solution)/shard_map/ppermute | solution.py:189
  25.5 17.3 %collective-permute-start.8 = (bf16[2,512,128]{2,1,0:T(8,128)(2,1)S(1)}, bf16[2,512,128]{2,1,0:T(8,128)(2,1)S(1)}, u32[]{:S(2)}, u32[]{:S(2)}) collective-permute-start(bf16[2,512,128]{2,1,0:T(8,128)(2,1)S(1)} %get-tuple-element.38), channel_id=1, source_target_pairs={{0,2},{1,3},{2,0},{3,1},{4,6},{5,7},{6,4},{7,5},{8,10},{9,11},{10,... | collective-permute-start | bytes 786440 | tf_op jit(solution)/shard_map/ppermute | solution.py:189
  44.4 14.0 %collective-permute-start.10 = (bf16[2,512,256]{2,1,0:T(8,128)(2,1)}, bf16[2,512,256]{2,1,0:T(8,128)(2,1)S(1)}, u32[]{:S(2)}, u32[]{:S(2)}) collective-permute-start(bf16[2,512,256]{2,1,0:T(8,128)(2,1)} %collective-permute-done.5.refs_0_.refs_4_), channel_id=1, source_target_pairs={{0,1},{1,2},{2,3},{3,0},{4,5},{5,6},{6,7},{7,4},{8,9},{9,10},{10,1... | collective-permute-start | bytes 1572872 | tf_op jit(solution)/shard_map/ppermute | solution.py:184
  44.5 14.0 %collective-permute-start.9 = (bf16[2,512,256]{2,1,0:T(8,128)(2,1)}, bf16[2,512,256]{2,1,0:T(8,128)(2,1)S(1)}, u32[]{:S(2)}, u32[]{:S(2)}) collective-permute-start(bf16[2,512,256]{2,1,0:T(8,128)(2,1)} %collective-permute-done.5.refs_0_.refs_4_), channel_id=1, source_target_pairs={{0,3},{1,0},{2,1},{3,2},{4,7},{5,4},{6,5},{7,6},{8,11},{9,8},{10,9... | collective-permute-start | bytes 1572872 | tf_op jit(solution)/shard_map/ppermute | solution.py:184
  48.1 17.6 %collective-permute-start.14 = (bf16[2,512,256]{2,1,0:T(8,128)(2,1)}, bf16[2,512,256]{2,1,0:T(8,128)(2,1)S(1)}, u32[]{:S(2)}, u32[]{:S(2)}) collective-permute-start(bf16[2,512,256]{2,1,0:T(8,128)(2,1)} %collective-permute-done.5.refs_0_.refs_4_), channel_id=1, source_target_pairs={{0,32},{32,64},{64,96},{96,0},{1,33},{33,65},{65,97},{97,1},{2,34}... | collective-permute-start | bytes 1572872 | tf_op jit(solution)/shard_map/ppermute | solution.py:177
  49.5 16.2 %collective-permute-start.13 = (bf16[2,512,256]{2,1,0:T(8,128)(2,1)}, bf16[2,512,256]{2,1,0:T(8,128)(2,1)S(1)}, u32[]{:S(2)}, u32[]{:S(2)}) collective-permute-start(bf16[2,512,256]{2,1,0:T(8,128)(2,1)} %collective-permute-done.5.refs_0_.refs_4_), channel_id=1, source_target_pairs={{0,96},{32,0},{64,32},{96,64},{1,97},{33,1},{65,33},{97,65},{2,98}... | collective-permute-start | bytes 1572872 | tf_op jit(solution)/shard_map/ppermute | solution.py:177
  58.4 8.4 %collective-permute-start.12 = (bf16[2,256,256]{2,1,0:T(8,128)(2,1)S(1)}, bf16[2,256,256]{2,1,0:T(8,128)(2,1)S(1)}, u32[]{:S(2)}, u32[]{:S(2)}) collective-permute-start(bf16[2,256,256]{2,1,0:T(8,128)(2,1)S(1)} %slice.9), channel_id=1, source_target_pairs={{0,1},{1,2},{2,3},{3,0},{4,5},{5,6},{6,7},{7,4},{8,9},{9,10},{10,1... | collective-permute-start | bytes 786440 | tf_op jit(solution)/shard_map/ppermute | solution.py:192
  58.6 8.2 %collective-permute-start.11 = (bf16[2,256,256]{2,1,0:T(8,128)(2,1)S(1)}, bf16[2,256,256]{2,1,0:T(8,128)(2,1)S(1)}, u32[]{:S(2)}, u32[]{:S(2)}) collective-permute-start(bf16[2,256,256]{2,1,0:T(8,128)(2,1)S(1)} %slice.8), channel_id=1, source_target_pairs={{0,3},{1,0},{2,1},{3,2},{4,7},{5,4},{6,5},{7,6},{8,11},{9,8},{10,9... | collective-permute-start | bytes 786440 | tf_op jit(solution)/shard_map/ppermute | solution.py:190
  62.0 1.0 copy-start.2
  65.1 16.7 %collective-permute-start.19 = (bf16[2048,128]{1,0:T(8,128)(2,1)}, bf16[2048,128]{1,0:T(8,128)(2,1)}, u32[]{:S(2)}, u32[]{:S(2)}) collective-permute-start(bf16[2048,128]{1,0:T(8,128)(2,1)} %shard_map.21.here), channel_id=1, source_target_pairs={{0,64},{32,96},{64,0},{96,32},{1,65},{33,97},{65,1},{97,33},{2,66}... | collective-permute-start | bytes 1572872 | tf_op jit(solution)/shard_map/ppermute | solution.py:177
  66.8 2.4 %copy-start.19 = (bf16[2,512,128]{2,1,0:T(8,128)(2,1)}, bf16[2,512,128]{2,1,0:T(8,128)(2,1)S(1)}, u32[]{:S(2)}) copy-start(bf16[2,512,128]{2,1,0:T(8,128)(2,1)S(1)} %get-tuple-element.47) | copy-start | bytes 786436
  66.8 2.4 %copy-start.20 = (bf16[2,512,128]{2,1,0:T(8,128)(2,1)}, bf16[2,512,128]{2,1,0:T(8,128)(2,1)S(1)}, u32[]{:S(2)}) copy-start(bf16[2,512,128]{2,1,0:T(8,128)(2,1)S(1)} %get-tuple-element.46) | copy-start | bytes 786436
  66.8 2.4 %copy-start.21 = (bf16[2,512,128]{2,1,0:T(8,128)(2,1)}, bf16[2,512,128]{2,1,0:T(8,128)(2,1)S(1)}, u32[]{:S(2)}) copy-start(bf16[2,512,128]{2,1,0:T(8,128)(2,1)S(1)} %get-tuple-element.45) | copy-start | bytes 786436
  69.9 21.1 %collective-permute-start.15 = (bf16[2048,128]{1,0:T(8,128)(2,1)}, bf16[2048,128]{1,0:T(8,128)(2,1)}, u32[]{:S(2)}, u32[]{:S(2)}) collective-permute-start(bf16[2048,128]{1,0:T(8,128)(2,1)} %shard_map.19.here), channel_id=1, source_target_pairs={{0,64},{32,96},{64,0},{96,32},{1,65},{33,97},{65,1},{97,33},{2,66}... | collective-permute-start | bytes 1572872 | tf_op jit(solution)/shard_map/ppermute | solution.py:177
  72.9 14.2 %copy-start.3 = (bf16[2,512,256]{2,1,0:T(8,128)(2,1)S(1)}, bf16[2,512,256]{2,1,0:T(8,128)(2,1)}, u32[]{:S(2)}) copy-start(bf16[2,512,256]{2,1,0:T(8,128)(2,1)} %copy-done.1) | copy-start | bytes 1572868
  72.9 14.2 %copy-start.6 = (bf16[2,512,256]{2,1,0:T(8,128)(2,1)S(1)}, bf16[2,512,256]{2,1,0:T(8,128)(2,1)}, u32[]{:S(2)}) copy-start(bf16[2,512,256]{2,1,0:T(8,128)(2,1)} %copy-done.4) | copy-start | bytes 1572868
  72.9 14.2 %copy-start.8 = (bf16[2,256,256]{2,1,0:T(8,128)(2,1)S(1)}, bf16[2,256,256]{2,1,0:T(8,128)(2,1)}, u32[]{:S(2)}) copy-start(bf16[2,256,256]{2,1,0:T(8,128)(2,1)} %copy-done.7) | copy-start | bytes 786436
  72.9 18.1 %collective-permute-start.16 = (bf16[2,512,128]{2,1,0:T(8,128)(2,1)}, bf16[2,512,128]{2,1,0:T(8,128)(2,1)S(1)}, u32[]{:S(2)}, u32[]{:S(2)}) collective-permute-start(bf16[2,512,128]{2,1,0:T(8,128)(2,1)} %copy-done.21), channel_id=1, source_target_pairs={{0,3},{1,0},{2,1},{3,2},{4,7},{5,4},{6,5},{7,6},{8,11},{9,8},{10,9... | collective-permute-start | bytes 786440 | tf_op jit(solution)/shard_map/ppermute | solution.py:189
  73.5 17.5 %collective-permute-start.17 = (bf16[2,512,128]{2,1,0:T(8,128)(2,1)}, bf16[2,512,128]{2,1,0:T(8,128)(2,1)S(1)}, u32[]{:S(2)}, u32[]{:S(2)}) collective-permute-start(bf16[2,512,128]{2,1,0:T(8,128)(2,1)} %copy-done.20), channel_id=1, source_target_pairs={{0,1},{1,2},{2,3},{3,0},{4,5},{5,6},{6,7},{7,4},{8,9},{9,10},{10,1... | collective-permute-start | bytes 786440 | tf_op jit(solution)/shard_map/ppermute | solution.py:189
  74.9 16.0 %collective-permute-start.18 = (bf16[2,512,128]{2,1,0:T(8,128)(2,1)}, bf16[2,512,128]{2,1,0:T(8,128)(2,1)S(1)}, u32[]{:S(2)}, u32[]{:S(2)}) collective-permute-start(bf16[2,512,128]{2,1,0:T(8,128)(2,1)} %copy-done.19), channel_id=1, source_target_pairs={{0,2},{1,3},{2,0},{3,1},{4,6},{5,7},{6,4},{7,5},{8,10},{9,11},{10,... | collective-permute-start | bytes 786440 | tf_op jit(solution)/shard_map/ppermute | solution.py:189
  87.0 4.0 %copy-start.18 = (bf16[2,512,128]{2,1,0:T(8,128)(2,1)S(1)}, bf16[2,512,128]{2,1,0:T(8,128)(2,1)}, u32[]{:S(2)}) copy-start(bf16[2,512,128]{2,1,0:T(8,128)(2,1)} %copy-done.17) | copy-start | bytes 786436
  87.0 10.0 %collective-permute-start.21 = (bf16[4,2048,128]{2,1,0:T(8,128)(2,1)S(1)}, bf16[4,2048,128]{2,1,0:T(8,128)(2,1)S(1)}, u32[]{:S(2)}, u32[]{:S(2)}) collective-permute-start(bf16[4,2048,128]{2,1,0:T(8,128)(2,1)S(1)} %shard_map.22.refs_9_), channel_id=1, source_target_pairs={{0,16},{16,0},{1,17},{17,1},{2,18},{18,2},{3,19},{19,3},{4,20},{20... | collective-permute-start | bytes 6291464 | tf_op jit(solution)/shard_map/ppermute | solution.py:180
  92.3 8.5 %collective-permute-start.20 = (bf16[4,2048,128]{2,1,0:T(8,128)(2,1)S(1)}, bf16[4,2048,128]{2,1,0:T(8,128)(2,1)S(1)}, u32[]{:S(2)}, u32[]{:S(2)}) collective-permute-start(bf16[4,2048,128]{2,1,0:T(8,128)(2,1)S(1)} %shard_map.20.refs_9_), channel_id=1, source_target_pairs={{0,16},{16,0},{1,17},{17,1},{2,18},{18,2},{3,19},{19,3},{4,20},{20... | collective-permute-start | bytes 6291464 | tf_op jit(solution)/shard_map/ppermute | solution.py:180
  (12 other events, 10.0 us)

commit v6 on v5

--- a/solution.py
+++ b/solution.py
@@ -179,10 +179,10 @@
     def from_core(piece):
         return lax.ppermute(piece, "core", ring(2, 1))
 
-    def gathered(block, ways, *late):
+    def gathered(block, ways, *late, before=()):
         shots = block.shape[1]
         above, below = (lax.ppermute(block, "x", ring(4, step)) for step in (-1, 1))
-        near = [from_y(block, 1), from_y(block, 3)]
+        near = [from_y(first_of(block, *before), step) for step in (1, 3)]
         near = lax.optimization_barrier((*near, above, below))[:2]
         cut = jax.ShapeDtypeStruct((2, shots, 2 * group), block.dtype)
         kept, *sent = small_call(near_kernel, (cut,) * 4, x[None], *near)
@@ -197,10 +197,10 @@
         far = from_y(here, 2)
         cols = jax.ShapeDtypeStruct((4, *here.shape), block.dtype)
         cols = small_call(join_kernel, cols, here, far, kept, *moved, scalars=0)
-        return pieces, cols, done
-
-    rows0, mine0, done0 = gathered(own, 1, other)
-    rows1, mine1, _ = gathered(first_of(other, *done0), 2)
+        return pieces, cols, done, here
+
+    rows0, mine0, done0, here0 = gathered(own, 1, other)
+    rows1, mine1, _, _ = gathered(first_of(other, *done0), 2, before=(here0,))
     rows = (*rows0, *rows1)
 
     place = jnp.stack([f, y, core])

time: 171 us -> 182 us (1.064); the launches traced: 170 us -> 178 us
  starting transfers between devices: 33.6 us -> 46.8 us
  waiting for transfers between devices: 34.1 us -> 27.8 us
    ppermute x6, starting transfers between devices: 7.58 us -> 19.5 us  [from_y(): return lax.ppermute(block, 'y', ring(4, -step))]
    ppermute x4, waiting for transfers between devices: 11.5 us -> 8.33 us  [gathered(): above, below = (lax.ppermute(block, 'x', ring(4, step)) for step in (-1, 1))]
    ppermute x6, waiting for transfers between devices: 6.73 us -> 3.62 us  [from_y(): return lax.ppermute(block, 'y', ring(4, -step))]
  transfers between devices with their start and end apart: 22 -> 22, of which waited for: 6 -> 7; matrix products, arithmetic and copies ran while one was open for 0% -> 0% of each run, Pallas kernels for 12% -> 11%
where the time goes in v6:
time: 182 us; the launch traced here: 178 us
  blocking collectives  64.4 us (35%)
  starting transfers between devices  46.8 us (26%)
  waiting for transfers between devices  27.8 us (15%)
  Pallas kernels  25.3 us (14%)
  local copies, waits for them, and re-layouts  13.1 us (7%)
    all_to_all x1, blocking collectives, body(): got = lax.all_to_all(sent, ('zh', 'zl', 'x'), 0, 0, tiled=True)  64.4 us
    ppermute x6, starting transfers between devices, from_y(): return lax.ppermute(block, 'y', ring(4, -step))  19.5 us
    pallas_call x4, Pallas kernels, terms_of(): pl.pallas_call(kernel, out_shape=shapes, in_specs=[SCALAR] + [SPACE] * (l...  15.7 us
    ppermute x6, waiting for transfers between devices, gathered(): lax.ppermute(part, 'x', ring(4, step))  13.6 us
    unnamed x44, local copies, waits for them, and re-layouts  12.2 us
    pallas_call x7, Pallas kernels, small_call(): pl.pallas_call(kernel, out_shape=shapes, in_specs=[SCALAR] * scalars + [S...  9.64 us
    ppermute x4, waiting for transfers between devices, gathered(): above, below = (lax.ppermute(block, 'x', ring(4, step)) for step in (-1, 1))  8.33 us
    ppermute x1, starting transfers between devices, body(): other = lax.ppermute(other, 'zh', ring(2, 1))  7.19 us
  transfers between devices with their start and end apart: 22, of which 7 were waited for; matrix products, arithmetic and copies ran while one was open for 0% of the time, Pallas kernels for 11%

profile of v6, /device:TPU:16, one launch (start us, length us, event | category | flops | bytes accessed | tf_op | source)
XLA Modules:
  0.0 178.4 jit_solution(12285491192336380738)
XLA Ops:
  0.0 1.2 copy-done
  2.1 2.8 %collective-permute-start = (bf16[2,512,256]{2,1,0:T(8,128)(2,1)S(1)}, bf16[2,512,256]{2,1,0:T(8,128)(2,1)S(1)}, u32[]{:S(2)}, u32[]{:S(2)}) collective-permute-start(bf16[2,512,256]{2,1,0:T(8,128)(2,1)S(1)} %dynamic-slice_bitcast_fusion.refs_0_), channel_id=1, source_target_pairs={{0,3},{1,0},{2,1},{3,2},{4,7},{5,4},{6,5},{7,6},{8,11},{9,8},{10,9... | collective-permute-start | bytes 1572872 | tf_op jit(solution)/shard_map/ppermute | solution.py:184
  5.0 1.3 collective-permute-start.4
  7.0 7.2 %collective-permute-start.5 = (bf16[2,512,256]{2,1,0:T(8,128)(2,1)}, bf16[2,512,256]{2,1,0:T(8,128)(2,1)}, u32[]{:S(2)}, u32[]{:S(2)}) collective-permute-start(bf16[2,512,256]{2,1,0:T(8,128)(2,1)} %dynamic-slice_bitcast_fusion.1), channel_id=1, source_target_pairs={{0,128},{128,0},{1,129},{129,1},{2,130},{130,2},{3,131},{131,3},{4... | collective-permute-start | bytes 1572872 | tf_op jit(solution)/shard_map/ppermute | solution.py:174
  14.2 2.0 %collective-permute-done.refs_1_ = bf16[2,512,256]{2,1,0:T(8,128)(2,1)S(1)} collective-permute-done((bf16[2,512,256]{2,1,0:T(8,128)(2,1)S(1)}, bf16[2,512,256]{2,1,0:T(8,128)(2,1)S(1)}, u32[]{:S(2)}, u32[]{:S(2)}) %collective-permute-start) | collective-permute-done | bytes 524320 | tf_op jit(solution)/shard_map/ppermute | solution.py:184
  16.1 3.7 %collective-permute-start.2 = (bf16[2,512,256]{2,1,0:T(8,128)(2,1)S(1)}, bf16[2,512,256]{2,1,0:T(8,128)(2,1)S(1)}, u32[]{:S(2)}, u32[]{:S(2)}) collective-permute-start(bf16[2,512,256]{2,1,0:T(8,128)(2,1)S(1)} %collective-permute-done.refs_1_), channel_id=1, source_target_pairs={{0,3},{1,0},{2,1},{3,2},{4,7},{5,4},{6,5},{7,6},{8,11},{9,8},{10,9... | collective-permute-start | bytes 1572872 | tf_op jit(solution)/shard_map/ppermute | solution.py:190
  19.8 1.2 collective-permute-done.1.refs_2_
  21.0 1.7 shard_map.17
  23.5 2.0 %collective-permute-start.7 = (bf16[2,512,128]{2,1,0:T(8,128)(2,1)S(1)}, bf16[2,512,128]{2,1,0:T(8,128)(2,1)S(1)}, u32[]{:S(2)}, u32[]{:S(2)}) collective-permute-start(bf16[2,512,128]{2,1,0:T(8,128)(2,1)S(1)} %get-tuple-element.38), channel_id=1, source_target_pairs={{0,1},{1,2},{2,3},{3,0},{4,5},{5,6},{6,7},{7,4},{8,9},{9,10},{10,1... | collective-permute-start | bytes 786440 | tf_op jit(solution)/shard_map/ppermute | solution.py:189
  25.5 2.3 %collective-permute-done.5.refs_0_.refs_4_ = bf16[2,512,256]{2,1,0:T(8,128)(2,1)} collective-permute-done((bf16[2,512,256]{2,1,0:T(8,128)(2,1)}, bf16[2,512,256]{2,1,0:T(8,128)(2,1)}, u32[]{:S(2)}, u32[]{:S(2)}) %collective-permute-start.5) | collective-permute-done | bytes 524320 | tf_op jit(solution)/shard_map/ppermute | solution.py:174
  27.8 13.5 %collective-permute-done.6.refs_1_ = bf16[2,512,128]{2,1,0:T(8,128)(2,1)S(1)} collective-permute-done((bf16[2,512,128]{2,1,0:T(8,128)(2,1)S(1)}, bf16[2,512,128]{2,1,0:T(8,128)(2,1)S(1)}, u32[]{:S(2)}, u32[]{:S(2)}) %collective-permute-start.6) | collective-permute-done | bytes 262176 | tf_op jit(solution)/shard_map/ppermute | solution.py:189
  44.5 3.5 %collective-permute-start.9 = (bf16[2,512,256]{2,1,0:T(8,128)(2,1)}, bf16[2,512,256]{2,1,0:T(8,128)(2,1)S(1)}, u32[]{:S(2)}, u32[]{:S(2)}) collective-permute-start(bf16[2,512,256]{2,1,0:T(8,128)(2,1)} %collective-permute-done.5.refs_0_.refs_4_), channel_id=1, source_target_pairs={{0,3},{1,0},{2,1},{3,2},{4,7},{5,4},{6,5},{7,6},{8,11},{9,8},{10,9... | collective-permute-start | bytes 1572872 | tf_op jit(solution)/shard_map/ppermute | solution.py:184
  48.1 1.0 copy-done.2
  49.1 1.0 copy-done.5
  50.2 1.0 shard_map.18.here
  51.2 1.4 collective-permute-start.14
  53.2 5.2 %collective-permute-done.10.refs_2_.refs_6_ = bf16[2,512,256]{2,1,0:T(8,128)(2,1)S(1)} collective-permute-done((bf16[2,512,256]{2,1,0:T(8,128)(2,1)}, bf16[2,512,256]{2,1,0:T(8,128)(2,1)S(1)}, u32[]{:S(2)}, u32[]{:S(2)}) %collective-permute-start.10) | collective-permute-done | bytes 524320 | tf_op jit(solution)/shard_map/ppermute | solution.py:184
  58.7 3.3 %collective-permute-start.11 = (bf16[2,256,256]{2,1,0:T(8,128)(2,1)S(1)}, bf16[2,256,256]{2,1,0:T(8,128)(2,1)S(1)}, u32[]{:S(2)}, u32[]{:S(2)}) collective-permute-start(bf16[2,256,256]{2,1,0:T(8,128)(2,1)S(1)} %slice.8), channel_id=1, source_target_pairs={{0,3},{1,0},{2,1},{3,2},{4,7},{5,4},{6,5},{7,6},{8,11},{9,8},{10,9... | collective-permute-start | bytes 786440 | tf_op jit(solution)/shard_map/ppermute | solution.py:190
  62.6 1.6 collective-permute-done.14.below
  64.2 2.0 %collective-permute-done.13.above = bf16[2,512,256]{2,1,0:T(8,128)(2,1)S(1)} collective-permute-done((bf16[2,512,256]{2,1,0:T(8,128)(2,1)}, bf16[2,512,256]{2,1,0:T(8,128)(2,1)S(1)}, u32[]{:S(2)}, u32[]{:S(2)}) %collective-permute-start.13) | collective-permute-done | bytes 524320 | tf_op jit(solution)/shard_map/ppermute | solution.py:177
  67.3 2.4 %shard_map.20.here = bf16[2048,128]{1,0:T(8,128)(2,1)} custom-call(s32[1]{0:T(128)} %bitcast.5.x, bf16[2,512,256]{2,1,0:T(8,128)(2,1)} %collective-permute-done.5.refs_0_.refs_4_, bf16[2,512,256]{2,1,0:T(8,128)(2,1)S(1)} %collective-permute-done.9.refs_1_.refs_5_, bf16[2,512,256]{2,1,0:T(8,128)(2,1)S(1)} %collective-permute-done.10.refs_2_.refs_6_, ...), custom_call_target="tpu_custom_call" | custom-call | bytes 2097152 | tf_op jit(solution)/shard_map/pallas_call | solution.py:94
  70.4 14.9 %collective-permute-start.15 = (bf16[2048,128]{1,0:T(8,128)(2,1)}, bf16[2048,128]{1,0:T(8,128)(2,1)}, u32[]{:S(2)}, u32[]{:S(2)}) collective-permute-start(bf16[2048,128]{1,0:T(8,128)(2,1)} %shard_map.20.here), channel_id=1, source_target_pairs={{0,64},{32,96},{64,0},{96,32},{1,65},{33,97},{65,1},{97,33},{2,66}... | collective-permute-start | bytes 1572872 | tf_op jit(solution)/shard_map/ppermute | solution.py:177
  85.3 1.7 collective-permute-start.16
  87.3 1.4 collective-permute-start.18
  92.6 1.3 shard_map.22.refs_9_
  94.1 3.8 %shard_map.23 = (f32[2,4,256,128]{3,2,1,0:T(8,128)S(1)}, f32[8,128]{1,0:T(8,128)S(1)}) custom-call(s32[3]{0:T(128)S(1)} %pad_add_fusion.place, bf16[2,512,256]{2,1,0:T(8,128)(2,1)S(1)} %dynamic-slice_bitcast_fusion.refs_0_, bf16[2,512,256]{2,1,0:T(8,128)(2,1)S(1)} %collective-permute-done.refs_1_, bf16[2,512,256]{2,1,0:T(8,128)(2,1)S(1)} %copy-done.3, ...), custom_call_target="tpu_custom_call" | custom-call | flops 2147483648 | bytes 8388608 | tf_op jit(solution)/shard_map/pallas_call | solution.py:135
  98.0 1.3 shard_map.21.refs_9_
  100.1 3.8 %shard_map.25 = (f32[2,4,256,128]{3,2,1,0:T(8,128)S(1)}, f32[8,128]{1,0:T(8,128)S(1)}) custom-call(s32[3]{0:T(128)S(1)} %pad_add_fusion.place, bf16[2,512,256]{2,1,0:T(8,128)(2,1)S(1)} %dynamic-slice_bitcast_fusion.refs_0_, bf16[2,512,256]{2,1,0:T(8,128)(2,1)S(1)} %collective-permute-done.refs_1_, bf16[2,512,256]{2,1,0:T(8,128)(2,1)S(1)} %copy-done.3, ...), custom_call_target="tpu_custom_call" | custom-call | flops 2147483648 | bytes 8388608 | tf_op jit(solution)/shard_map/pallas_call | solution.py:135
  103.9 3.8 %shard_map.24 = (f32[2,4,256,128]{3,2,1,0:T(8,128)S(1)}, f32[8,128]{1,0:T(8,128)S(1)}) custom-call(s32[3]{0:T(128)S(1)} %pad_add_fusion.place, bf16[2,512,256]{2,1,0:T(8,128)(2,1)S(1)} %dynamic-slice_bitcast_fusion.refs_0_, bf16[2,512,256]{2,1,0:T(8,128)(2,1)S(1)} %collective-permute-done.refs_1_, bf16[2,512,256]{2,1,0:T(8,128)(2,1)S(1)} %copy-done.3, ...), custom_call_target="tpu_custom_call" | custom-call | flops 2147483648 | bytes 8388608 | tf_op jit(solution)/shard_map/pallas_call | solution.py:135
  107.8 4.2 %shard_map.26 = f32[32,264,128]{2,1,0:T(8,128)S(1)} custom-call(s32[3]{0:T(128)S(1)} %pad_add_fusion.place, bf16[2,512,256]{2,1,0:T(8,128)(2,1)S(1)} %dynamic-slice_bitcast_fusion.refs_0_, bf16[2,512,256]{2,1,0:T(8,128)(2,1)S(1)} %collective-permute-done.refs_1_, bf16[2,512,256]{2,1,0:T(8,128)(2,1)S(1)} %copy-done.3, bf16[2,512,256]{2,1,0:T(8,128)(2,1)S(1)} %copy-done.6, ...), custom_call_target="tpu_custom_call" | custom-call | flops 2147483648 | bytes 8388608 | tf_op jit(solution)/shard_map/pallas_call | solution.py:135
  112.3 64.4 %all_to_all.5 = f16[32,264,128]{2,1,0:T(8,128)(2,1)S(1)} all-to-all(f16[32,264,128]{2,1,0:T(8,128)(2,1)S(1)} %convert_element_type.6), channel_id=1, replica_groups=mesh['zh'=2,'y'=4,'core'=2,'zl'=4,'x'=4] {'zh','zl','x'}, dimensions={0} | all-to-all | bytes 4325376 | tf_op jit(solution)/shard_map/all_to_all | solution.py:212
  176.9 1.5 shard_map.27
  (75 shorter events, 14.5 us)
Async XLA Ops:
  0.0 1.2 copy-start
  2.1 14.0 %collective-permute-start = (bf16[2,512,256]{2,1,0:T(8,128)(2,1)S(1)}, bf16[2,512,256]{2,1,0:T(8,128)(2,1)S(1)}, u32[]{:S(2)}, u32[]{:S(2)}) collective-permute-start(bf16[2,512,256]{2,1,0:T(8,128)(2,1)S(1)} %dynamic-slice_bitcast_fusion.refs_0_), channel_id=1, source_target_pairs={{0,3},{1,0},{2,1},{3,2},{4,7},{5,4},{6,5},{7,6},{8,11},{9,8},{10,9... | collective-permute-start | bytes 1572872 | tf_op jit(solution)/shard_map/ppermute | solution.py:184
  5.0 14.9 %collective-permute-start.4 = (bf16[2,512,256]{2,1,0:T(8,128)(2,1)S(1)}, bf16[2,512,256]{2,1,0:T(8,128)(2,1)}, u32[]{:S(2)}, u32[]{:S(2)}) collective-permute-start(bf16[2,512,256]{2,1,0:T(8,128)(2,1)S(1)} %dynamic-slice_bitcast_fusion.refs_0_), channel_id=1, source_target_pairs={{0,32},{32,64},{64,96},{96,0},{1,33},{33,65},{65,97},{97,1},{2,34}... | collective-permute-start | bytes 1572872 | tf_op jit(solution)/shard_map/ppermute | solution.py:177
  6.2 13.6 %collective-permute-start.3 = (bf16[2,512,256]{2,1,0:T(8,128)(2,1)S(1)}, bf16[2,512,256]{2,1,0:T(8,128)(2,1)}, u32[]{:S(2)}, u32[]{:S(2)}) collective-permute-start(bf16[2,512,256]{2,1,0:T(8,128)(2,1)S(1)} %dynamic-slice_bitcast_fusion.refs_0_), channel_id=1, source_target_pairs={{0,96},{32,0},{64,32},{96,64},{1,97},{33,1},{65,33},{97,65},{2,98}... | collective-permute-start | bytes 1572872 | tf_op jit(solution)/shard_map/ppermute | solution.py:177
  7.0 14.0 %collective-permute-start.1 = (bf16[2,512,256]{2,1,0:T(8,128)(2,1)S(1)}, bf16[2,512,256]{2,1,0:T(8,128)(2,1)S(1)}, u32[]{:S(2)}, u32[]{:S(2)}) collective-permute-start(bf16[2,512,256]{2,1,0:T(8,128)(2,1)S(1)} %dynamic-slice_bitcast_fusion.refs_0_), channel_id=1, source_target_pairs={{0,1},{1,2},{2,3},{3,0},{4,5},{5,6},{6,7},{7,4},{8,9},{9,10},{10,1... | collective-permute-start | bytes 1572872 | tf_op jit(solution)/shard_map/ppermute | solution.py:184
  7.0 20.8 %collective-permute-start.5 = (bf16[2,512,256]{2,1,0:T(8,128)(2,1)}, bf16[2,512,256]{2,1,0:T(8,128)(2,1)}, u32[]{:S(2)}, u32[]{:S(2)}) collective-permute-start(bf16[2,512,256]{2,1,0:T(8,128)(2,1)} %dynamic-slice_bitcast_fusion.1), channel_id=1, source_target_pairs={{0,128},{128,0},{1,129},{129,1},{2,130},{130,2},{3,131},{131,3},{4... | collective-permute-start | bytes 1572872 | tf_op jit(solution)/shard_map/ppermute | solution.py:174
  16.1 27.4 %collective-permute-start.2 = (bf16[2,512,256]{2,1,0:T(8,128)(2,1)S(1)}, bf16[2,512,256]{2,1,0:T(8,128)(2,1)S(1)}, u32[]{:S(2)}, u32[]{:S(2)}) collective-permute-start(bf16[2,512,256]{2,1,0:T(8,128)(2,1)S(1)} %collective-permute-done.refs_1_), channel_id=1, source_target_pairs={{0,3},{1,0},{2,1},{3,2},{4,7},{5,4},{6,5},{7,6},{8,11},{9,8},{10,9... | collective-permute-start | bytes 1572872 | tf_op jit(solution)/shard_map/ppermute | solution.py:190
  21.0 21.8 %copy-start.1 = (bf16[2,512,256]{2,1,0:T(8,128)(2,1)}, bf16[2,512,256]{2,1,0:T(8,128)(2,1)S(1)}, u32[]{:S(2)}) copy-start(bf16[2,512,256]{2,1,0:T(8,128)(2,1)S(1)} %collective-permute-done.1.refs_2_) | copy-start | bytes 1572868
  23.5 17.9 %collective-permute-start.6 = (bf16[2,512,128]{2,1,0:T(8,128)(2,1)S(1)}, bf16[2,512,128]{2,1,0:T(8,128)(2,1)S(1)}, u32[]{:S(2)}, u32[]{:S(2)}) collective-permute-start(bf16[2,512,128]{2,1,0:T(8,128)(2,1)S(1)} %get-tuple-element.37), channel_id=1, source_target_pairs={{0,3},{1,0},{2,1},{3,2},{4,7},{5,4},{6,5},{7,6},{8,11},{9,8},{10,9... | collective-permute-start | bytes 786440 | tf_op jit(solution)/shard_map/ppermute | solution.py:189
  23.5 18.6 %collective-permute-start.7 = (bf16[2,512,128]{2,1,0:T(8,128)(2,1)S(1)}, bf16[2,512,128]{2,1,0:T(8,128)(2,1)S(1)}, u32[]{:S(2)}, u32[]{:S(2)}) collective-permute-start(bf16[2,512,128]{2,1,0:T(8,128)(2,1)S(1)} %get-tuple-element.38), channel_id=1, source_target_pairs={{0,1},{1,2},{2,3},{3,0},{4,5},{5,6},{6,7},{7,4},{8,9},{9,10},{10,1... | collective-permute-start | bytes 786440 | tf_op jit(solution)/shard_map/ppermute | solution.py:189
  25.5 17.3 %collective-permute-start.8 = (bf16[2,512,128]{2,1,0:T(8,128)(2,1)S(1)}, bf16[2,512,128]{2,1,0:T(8,128)(2,1)S(1)}, u32[]{:S(2)}, u32[]{:S(2)}) collective-permute-start(bf16[2,512,128]{2,1,0:T(8,128)(2,1)S(1)} %get-tuple-element.39), channel_id=1, source_target_pairs={{0,2},{1,3},{2,0},{3,1},{4,6},{5,7},{6,4},{7,5},{8,10},{9,11},{10,... | collective-permute-start | bytes 786440 | tf_op jit(solution)/shard_map/ppermute | solution.py:189
  44.4 14.0 %collective-permute-start.10 = (bf16[2,512,256]{2,1,0:T(8,128)(2,1)}, bf16[2,512,256]{2,1,0:T(8,128)(2,1)S(1)}, u32[]{:S(2)}, u32[]{:S(2)}) collective-permute-start(bf16[2,512,256]{2,1,0:T(8,128)(2,1)} %collective-permute-done.5.refs_0_.refs_4_), channel_id=1, source_target_pairs={{0,1},{1,2},{2,3},{3,0},{4,5},{5,6},{6,7},{7,4},{8,9},{9,10},{10,1... | collective-permute-start | bytes 1572872 | tf_op jit(solution)/shard_map/ppermute | solution.py:184
  44.5 14.2 %collective-permute-start.9 = (bf16[2,512,256]{2,1,0:T(8,128)(2,1)}, bf16[2,512,256]{2,1,0:T(8,128)(2,1)S(1)}, u32[]{:S(2)}, u32[]{:S(2)}) collective-permute-start(bf16[2,512,256]{2,1,0:T(8,128)(2,1)} %collective-permute-done.5.refs_0_.refs_4_), channel_id=1, source_target_pairs={{0,3},{1,0},{2,1},{3,2},{4,7},{5,4},{6,5},{7,6},{8,11},{9,8},{10,9... | collective-permute-start | bytes 1572872 | tf_op jit(solution)/shard_map/ppermute | solution.py:184
  48.1 1.0 copy-start.2
  51.2 13.0 %collective-permute-start.14 = (bf16[2,512,256]{2,1,0:T(8,128)(2,1)}, bf16[2,512,256]{2,1,0:T(8,128)(2,1)S(1)}, u32[]{:S(2)}, u32[]{:S(2)}) collective-permute-start(bf16[2,512,256]{2,1,0:T(8,128)(2,1)} %collective-permute-done.5.refs_0_.refs_4_), channel_id=1, source_target_pairs={{0,32},{32,64},{64,96},{96,0},{1,33},{33,65},{65,97},{97,1},{2,34}... | collective-permute-start | bytes 1572872 | tf_op jit(solution)/shard_map/ppermute | solution.py:177
  52.6 13.6 %collective-permute-start.13 = (bf16[2,512,256]{2,1,0:T(8,128)(2,1)}, bf16[2,512,256]{2,1,0:T(8,128)(2,1)S(1)}, u32[]{:S(2)}, u32[]{:S(2)}) collective-permute-start(bf16[2,512,256]{2,1,0:T(8,128)(2,1)} %collective-permute-done.5.refs_0_.refs_4_), channel_id=1, source_target_pairs={{0,96},{32,0},{64,32},{96,64},{1,97},{33,1},{65,33},{97,65},{2,98}... | collective-permute-start | bytes 1572872 | tf_op jit(solution)/shard_map/ppermute | solution.py:177
  58.4 8.8 %collective-permute-start.12 = (bf16[2,256,256]{2,1,0:T(8,128)(2,1)S(1)}, bf16[2,256,256]{2,1,0:T(8,128)(2,1)S(1)}, u32[]{:S(2)}, u32[]{:S(2)}) collective-permute-start(bf16[2,256,256]{2,1,0:T(8,128)(2,1)S(1)} %slice.9), channel_id=1, source_target_pairs={{0,1},{1,2},{2,3},{3,0},{4,5},{5,6},{6,7},{7,4},{8,9},{9,10},{10,1... | collective-permute-start | bytes 786440 | tf_op jit(solution)/shard_map/ppermute | solution.py:192
  58.7 8.5 %collective-permute-start.11 = (bf16[2,256,256]{2,1,0:T(8,128)(2,1)S(1)}, bf16[2,256,256]{2,1,0:T(8,128)(2,1)S(1)}, u32[]{:S(2)}, u32[]{:S(2)}) collective-permute-start(bf16[2,256,256]{2,1,0:T(8,128)(2,1)S(1)} %slice.8), channel_id=1, source_target_pairs={{0,3},{1,0},{2,1},{3,2},{4,7},{5,4},{6,5},{7,6},{8,11},{9,8},{10,9... | collective-permute-start | bytes 786440 | tf_op jit(solution)/shard_map/ppermute | solution.py:190
  62.0 26.8 %collective-permute-start.19 = (bf16[2048,128]{1,0:T(8,128)(2,1)}, bf16[2048,128]{1,0:T(8,128)(2,1)}, u32[]{:S(2)}, u32[]{:S(2)}) collective-permute-start(bf16[2048,128]{1,0:T(8,128)(2,1)} %shard_map.18.here), channel_id=1, source_target_pairs={{0,64},{32,96},{64,0},{96,32},{1,65},{33,97},{65,1},{97,33},{2,66}... | collective-permute-start | bytes 1572872 | tf_op jit(solution)/shard_map/ppermute | solution.py:177
  67.2 2.4 %copy-start.17 = (bf16[2,512,128]{2,1,0:T(8,128)(2,1)}, bf16[2,512,128]{2,1,0:T(8,128)(2,1)S(1)}, u32[]{:S(2)}) copy-start(bf16[2,512,128]{2,1,0:T(8,128)(2,1)S(1)} %get-tuple-element.44.refs_0_) | copy-start | bytes 786436
  67.2 2.4 %copy-start.19 = (bf16[2,512,128]{2,1,0:T(8,128)(2,1)}, bf16[2,512,128]{2,1,0:T(8,128)(2,1)S(1)}, u32[]{:S(2)}) copy-start(bf16[2,512,128]{2,1,0:T(8,128)(2,1)S(1)} %get-tuple-element.49) | copy-start | bytes 786436
  67.2 2.4 %copy-start.20 = (bf16[2,512,128]{2,1,0:T(8,128)(2,1)}, bf16[2,512,128]{2,1,0:T(8,128)(2,1)S(1)}, u32[]{:S(2)}) copy-start(bf16[2,512,128]{2,1,0:T(8,128)(2,1)S(1)} %get-tuple-element.48) | copy-start | bytes 786436
  70.4 27.6 %collective-permute-start.15 = (bf16[2048,128]{1,0:T(8,128)(2,1)}, bf16[2048,128]{1,0:T(8,128)(2,1)}, u32[]{:S(2)}, u32[]{:S(2)}) collective-permute-start(bf16[2048,128]{1,0:T(8,128)(2,1)} %shard_map.20.here), channel_id=1, source_target_pairs={{0,64},{32,96},{64,0},{96,32},{1,65},{33,97},{65,1},{97,33},{2,66}... | collective-permute-start | bytes 1572872 | tf_op jit(solution)/shard_map/ppermute | solution.py:177
  85.2 8.8 %copy-start.3 = (bf16[2,512,256]{2,1,0:T(8,128)(2,1)S(1)}, bf16[2,512,256]{2,1,0:T(8,128)(2,1)}, u32[]{:S(2)}) copy-start(bf16[2,512,256]{2,1,0:T(8,128)(2,1)} %copy-done.1) | copy-start | bytes 1572868
  85.3 8.8 %copy-start.6 = (bf16[2,512,256]{2,1,0:T(8,128)(2,1)S(1)}, bf16[2,512,256]{2,1,0:T(8,128)(2,1)}, u32[]{:S(2)}) copy-start(bf16[2,512,256]{2,1,0:T(8,128)(2,1)} %copy-done.4) | copy-start | bytes 1572868
  85.3 8.8 %copy-start.8 = (bf16[2,256,256]{2,1,0:T(8,128)(2,1)S(1)}, bf16[2,256,256]{2,1,0:T(8,128)(2,1)}, u32[]{:S(2)}) copy-start(bf16[2,256,256]{2,1,0:T(8,128)(2,1)} %copy-done.7) | copy-start | bytes 786436
  85.3 12.6 %collective-permute-start.16 = (bf16[2,512,128]{2,1,0:T(8,128)(2,1)}, bf16[2,512,128]{2,1,0:T(8,128)(2,1)S(1)}, u32[]{:S(2)}, u32[]{:S(2)}) collective-permute-start(bf16[2,512,128]{2,1,0:T(8,128)(2,1)} %copy-done.21), channel_id=1, source_target_pairs={{0,3},{1,0},{2,1},{3,2},{4,7},{5,4},{6,5},{7,6},{8,11},{9,8},{10,9... | collective-permute-start | bytes 786440 | tf_op jit(solution)/shard_map/ppermute | solution.py:189
  86.9 11.0 %collective-permute-start.17 = (bf16[2,512,128]{2,1,0:T(8,128)(2,1)}, bf16[2,512,128]{2,1,0:T(8,128)(2,1)S(1)}, u32[]{:S(2)}, u32[]{:S(2)}) collective-permute-start(bf16[2,512,128]{2,1,0:T(8,128)(2,1)} %copy-done.20), channel_id=1, source_target_pairs={{0,1},{1,2},{2,3},{3,0},{4,5},{5,6},{6,7},{7,4},{8,9},{9,10},{10,1... | collective-permute-start | bytes 786440 | tf_op jit(solution)/shard_map/ppermute | solution.py:189
  87.3 10.6 %collective-permute-start.18 = (bf16[2,512,128]{2,1,0:T(8,128)(2,1)}, bf16[2,512,128]{2,1,0:T(8,128)(2,1)S(1)}, u32[]{:S(2)}, u32[]{:S(2)}) collective-permute-start(bf16[2,512,128]{2,1,0:T(8,128)(2,1)} %copy-done.19), channel_id=1, source_target_pairs={{0,2},{1,3},{2,0},{3,1},{4,6},{5,7},{6,4},{7,5},{8,10},{9,11},{10,... | collective-permute-start | bytes 786440 | tf_op jit(solution)/shard_map/ppermute | solution.py:189
  93.9 4.0 %copy-start.18 = (bf16[2,512,128]{2,1,0:T(8,128)(2,1)S(1)}, bf16[2,512,128]{2,1,0:T(8,128)(2,1)}, u32[]{:S(2)}) copy-start(bf16[2,512,128]{2,1,0:T(8,128)(2,1)} %copy-done.17) | copy-start | bytes 786436
  93.9 10.0 %collective-permute-start.21 = (bf16[4,2048,128]{2,1,0:T(8,128)(2,1)S(1)}, bf16[4,2048,128]{2,1,0:T(8,128)(2,1)S(1)}, u32[]{:S(2)}, u32[]{:S(2)}) collective-permute-start(bf16[4,2048,128]{2,1,0:T(8,128)(2,1)S(1)} %shard_map.22.refs_9_), channel_id=1, source_target_pairs={{0,16},{16,0},{1,17},{17,1},{2,18},{18,2},{3,19},{19,3},{4,20},{20... | collective-permute-start | bytes 6291464 | tf_op jit(solution)/shard_map/ppermute | solution.py:180
  99.3 8.5 %collective-permute-start.20 = (bf16[4,2048,128]{2,1,0:T(8,128)(2,1)S(1)}, bf16[4,2048,128]{2,1,0:T(8,128)(2,1)S(1)}, u32[]{:S(2)}, u32[]{:S(2)}) collective-permute-start(bf16[4,2048,128]{2,1,0:T(8,128)(2,1)S(1)} %shard_map.21.refs_9_), channel_id=1, source_target_pairs={{0,16},{16,0},{1,17},{17,1},{2,18},{18,2},{3,19},{19,3},{4,20},{20... | collective-permute-start | bytes 6291464 | tf_op jit(solution)/shard_map/ppermute | solution.py:180
  (12 other events, 9.9 us)

commit v7 on v4

--- a/solution.py
+++ b/solution.py
@@ -116,10 +116,19 @@
             zc, core_col = f ^ (number // 2), core ^ (number % 2)
             owner = zr * 16 + zc * 8 + yc * 2 + core_col
             out[owner, :n] = term[zr, yc] * factor
-            out[owner, n:] = power
+            out[owner, n:] = tail
         return carry
 
+    tail = jnp.where(lax.broadcasted_iota(jnp.int32, (8, c), 0) == 1, 0.0, power)
     lax.fori_loop(0, 8, step, 0)
+    on = diagonal(n, c, place[3])
+    for zc in range(2):
+        owner = zc * 24 + place[1] * 2 + core
+        value = out[owner, :n]
+        split = value * 8193.0
+        high = split - (split - value)
+        out[owner, :n] = jnp.where(on, high, value)
+        out[owner, n + 1 : n + 2] = jnp.sum(jnp.where(on, value - high, 0.0), axis=0, keepdims=True)
 
 
 def terms_of(place, rows, cols, others=None):
@@ -152,10 +161,17 @@
             total = 0.0
             for zl in range(4):
                 chunk = f * 16 + zl * 4 + x
-                total += got[chunk, :n] * jnp.exp2(got[chunk, n : n + 1] - TOP)
+                rest = jnp.where(diagonal(n, c, x), got[chunk, n + 1 : n + 2], 0.0)
+                total += (got[chunk, :n] + rest) * jnp.exp2(got[chunk, n : n + 1] - TOP)
             total *= undo
             for p in range(2):
                 out[f, p, :, x * c // 2 : (x + 1) * c // 2] = total[:, p * c // 2 : (p + 1) * c // 2]
+
+
+def diagonal(rows, cols, group):
+    i = lax.broadcasted_iota(jnp.int32, (rows, cols), 0)
+    j = lax.broadcasted_iota(jnp.int32, (rows, cols), 1)
+    return (i == group * (cols // 2) + j) & (j < cols // 2)
 
 
 def pattern(rows, cols):
@@ -202,7 +218,7 @@
     rows1, mine1, _ = gathered(first_of(other, *moved0))
     rows = (*rows0, *rows1)
 
-    place = jnp.stack([f, y, core])
+    place = jnp.stack([f, y, core, x])
     theirs0 = from_core(mine0)
     mine1, *ready = lax.optimization_barrier((mine1, *terms_of(place, rows, mine0)))
     theirs1 = from_core(mine1)

time: 171 us -> 171 us (level)
  no operation moved by 1% of the time
where the time goes in v7:
time: 171 us; the launch traced here: 170 us
  blocking collectives  70.9 us (41%)
  starting transfers between devices  34 us (20%)
  waiting for transfers between devices  26.8 us (16%)
  Pallas kernels  25.4 us (15%)
  local copies, waits for them, and re-layouts  12.1 us (7%)
    all_to_all x1, blocking collectives, body(): got = lax.all_to_all(sent, ('zh', 'zl', 'x'), 0, 0, tiled=True)  70.9 us
    pallas_call x4, Pallas kernels, terms_of(): pl.pallas_call(kernel, out_shape=shapes, in_specs=[SCALAR] + [SPACE] * (l...  15.8 us
    ppermute x4, waiting for transfers between devices, gathered(): above, below = (lax.ppermute(block, 'x', ring(4, step)) for step in (-1, 1))  11.7 us
    unnamed x48, local copies, waits for them, and re-layouts  11.1 us
    pallas_call x7, Pallas kernels, small_call(): pl.pallas_call(kernel, out_shape=shapes, in_specs=[SCALAR] * scalars + [S...  9.51 us
    ppermute x6, waiting for transfers between devices, gathered(): lax.ppermute(part, 'x', ring(4, step))  8.22 us
    ppermute x6, starting transfers between devices, gathered(): lax.ppermute(part, 'x', ring(4, step))  8.08 us
    ppermute x6, starting transfers between devices, from_y(): return lax.ppermute(block, 'y', ring(4, -step))  7.66 us
  transfers between devices with their start and end apart: 23, of which 10 were waited for; matrix products, arithmetic and copies ran while one was open for 0% of the time, Pallas kernels for 11%

profile of v7, /device:TPU:16, one launch (start us, length us, event | category | flops | bytes accessed | tf_op | source)
XLA Modules:
  0.0 170.0 jit_solution(12970429935644852533)
XLA Ops:
  0.0 1.2 copy-done
  2.1 1.4 collective-permute-start.5
  4.2 1.5 collective-permute-start.1
  5.7 1.7 %collective-permute-start = (bf16[2,512,256]{2,1,0:T(8,128)(2,1)S(1)}, bf16[2,512,256]{2,1,0:T(8,128)(2,1)S(1)}, u32[]{:S(2)}, u32[]{:S(2)}) collective-permute-start(bf16[2,512,256]{2,1,0:T(8,128)(2,1)S(1)} %dynamic-slice_bitcast_fusion.refs_0_), channel_id=1, source_target_pairs={{0,3},{1,0},{2,1},{3,2},{4,7},{5,4},{6,5},{7,6},{8,11},{9,8},{10,9... | collective-permute-start | bytes 1572872 | tf_op jit(solution)/shard_map/ppermute | solution.py:200
  7.4 7.2 %collective-permute-start.6 = (bf16[2,512,256]{2,1,0:T(8,128)(2,1)}, bf16[2,512,256]{2,1,0:T(8,128)(2,1)}, u32[]{:S(2)}, u32[]{:S(2)}) collective-permute-start(bf16[2,512,256]{2,1,0:T(8,128)(2,1)} %dynamic-slice_bitcast_fusion.1), channel_id=1, source_target_pairs={{0,128},{128,0},{1,129},{129,1},{2,130},{130,2},{3,131},{131,3},{4... | collective-permute-start | bytes 1572872 | tf_op jit(solution)/shard_map/ppermute | solution.py:190
  14.6 1.2 collective-permute-done.5.below
  16.9 1.6 collective-permute-done.1.refs_2_
  19.6 1.4 shard_map.17
  21.0 3.0 %collective-permute-start.7 = (bf16[2,512,128]{2,1,0:T(8,128)(2,1)S(1)}, bf16[2,512,128]{2,1,0:T(8,128)(2,1)S(1)}, u32[]{:S(2)}, u32[]{:S(2)}) collective-permute-start(bf16[2,512,128]{2,1,0:T(8,128)(2,1)S(1)} %get-tuple-element.38), channel_id=1, source_target_pairs={{0,3},{1,0},{2,1},{3,2},{4,7},{5,4},{6,5},{7,6},{8,11},{9,8},{10,9... | collective-permute-start | bytes 786440 | tf_op jit(solution)/shard_map/ppermute | solution.py:205
  24.0 1.8 %collective-permute-start.9 = (bf16[2,512,128]{2,1,0:T(8,128)(2,1)S(1)}, bf16[2,512,128]{2,1,0:T(8,128)(2,1)S(1)}, u32[]{:S(2)}, u32[]{:S(2)}) collective-permute-start(bf16[2,512,128]{2,1,0:T(8,128)(2,1)S(1)} %get-tuple-element.40), channel_id=1, source_target_pairs={{0,2},{1,3},{2,0},{3,1},{4,6},{5,7},{6,4},{7,5},{8,10},{9,11},{10,... | collective-permute-start | bytes 786440 | tf_op jit(solution)/shard_map/ppermute | solution.py:205
  25.8 2.2 %collective-permute-done.6.refs_0_.refs_5_ = bf16[2,512,256]{2,1,0:T(8,128)(2,1)} collective-permute-done((bf16[2,512,256]{2,1,0:T(8,128)(2,1)}, bf16[2,512,256]{2,1,0:T(8,128)(2,1)}, u32[]{:S(2)}, u32[]{:S(2)}) %collective-permute-start.6) | collective-permute-done | bytes 524320 | tf_op jit(solution)/shard_map/ppermute | solution.py:190
  28.0 5.5 %collective-permute-done.7.refs_1_ = bf16[2,512,128]{2,1,0:T(8,128)(2,1)S(1)} collective-permute-done((bf16[2,512,128]{2,1,0:T(8,128)(2,1)S(1)}, bf16[2,512,128]{2,1,0:T(8,128)(2,1)S(1)}, u32[]{:S(2)}, u32[]{:S(2)}) %collective-permute-start.7) | collective-permute-done | bytes 262176 | tf_op jit(solution)/shard_map/ppermute | solution.py:205
  34.2 2.7 %collective-permute-done.8.refs_2_ = bf16[2,512,128]{2,1,0:T(8,128)(2,1)S(1)} collective-permute-done((bf16[2,512,128]{2,1,0:T(8,128)(2,1)S(1)}, bf16[2,512,128]{2,1,0:T(8,128)(2,1)S(1)}, u32[]{:S(2)}, u32[]{:S(2)}) %collective-permute-start.8) | collective-permute-done | bytes 262176 | tf_op jit(solution)/shard_map/ppermute | solution.py:205
  38.3 3.2 %collective-permute-start.10 = (bf16[2,512,256]{2,1,0:T(8,128)(2,1)}, bf16[2,512,256]{2,1,0:T(8,128)(2,1)S(1)}, u32[]{:S(2)}, u32[]{:S(2)}) collective-permute-start(bf16[2,512,256]{2,1,0:T(8,128)(2,1)} %collective-permute-done.6.refs_0_.refs_5_), channel_id=1, source_target_pairs={{0,3},{1,0},{2,1},{3,2},{4,7},{5,4},{6,5},{7,6},{8,11},{9,8},{10,9... | collective-permute-start | bytes 1572872 | tf_op jit(solution)/shard_map/ppermute | solution.py:200
  41.6 1.3 collective-permute-start.15
  43.7 10.2 %collective-permute-done.11.refs_2_.refs_7_ = bf16[2,512,256]{2,1,0:T(8,128)(2,1)S(1)} collective-permute-done((bf16[2,512,256]{2,1,0:T(8,128)(2,1)}, bf16[2,512,256]{2,1,0:T(8,128)(2,1)S(1)}, u32[]{:S(2)}, u32[]{:S(2)}) %collective-permute-start.11) | collective-permute-done | bytes 524320 | tf_op jit(solution)/shard_map/ppermute | solution.py:200
  54.4 1.8 %collective-permute-start.13 = (bf16[2,256,256]{2,1,0:T(8,128)(2,1)S(1)}, bf16[2,256,256]{2,1,0:T(8,128)(2,1)S(1)}, u32[]{:S(2)}, u32[]{:S(2)}) collective-permute-start(bf16[2,256,256]{2,1,0:T(8,128)(2,1)S(1)} %slice.19), channel_id=1, source_target_pairs={{0,1},{1,2},{2,3},{3,0},{4,5},{5,6},{6,7},{7,4},{8,9},{9,10},{10,1... | collective-permute-start | bytes 786440 | tf_op jit(solution)/shard_map/ppermute | solution.py:207
  56.7 1.3 collective-permute-start.12
  58.0 2.2 %collective-permute-done.2.refs_3_ = bf16[2,256,256]{2,1,0:T(8,128)(2,1)S(1)} collective-permute-done((bf16[2,256,256]{2,1,0:T(8,128)(2,1)S(1)}, bf16[2,256,256]{2,1,0:T(8,128)(2,1)S(1)}, u32[]{:S(2)}, u32[]{:S(2)}) %collective-permute-start.2) | collective-permute-done | bytes 262176 | tf_op jit(solution)/shard_map/ppermute | solution.py:206
  62.0 1.5 collective-permute-start.20
  64.6 2.4 %shard_map.19.here = bf16[2048,128]{1,0:T(8,128)(2,1)} custom-call(s32[1]{0:T(128)} %bitcast.3.x, bf16[2,512,256]{2,1,0:T(8,128)(2,1)} %collective-permute-done.6.refs_0_.refs_5_, bf16[2,512,256]{2,1,0:T(8,128)(2,1)S(1)} %collective-permute-done.10.refs_1_.refs_6_, bf16[2,512,256]{2,1,0:T(8,128)(2,1)S(1)} %collective-permute-done.11.refs_2_.refs_7_, ...), custom_call_target="tpu_custom_call" | custom-call | bytes 2097152 | tf_op jit(solution)/shard_map/pallas_call | solution.py:94
  67.7 2.1 %collective-permute-start.16 = (bf16[2048,128]{1,0:T(8,128)(2,1)}, bf16[2048,128]{1,0:T(8,128)(2,1)}, u32[]{:S(2)}, u32[]{:S(2)}) collective-permute-start(bf16[2048,128]{1,0:T(8,128)(2,1)} %shard_map.19.here), channel_id=1, source_target_pairs={{0,64},{32,96},{64,0},{96,32},{1,65},{33,97},{65,1},{97,33},{2,66}... | collective-permute-start | bytes 1572872 | tf_op jit(solution)/shard_map/ppermute | solution.py:193
  69.8 1.7 %collective-permute-start.17 = (bf16[2,512,128]{2,1,0:T(8,128)(2,1)}, bf16[2,512,128]{2,1,0:T(8,128)(2,1)S(1)}, u32[]{:S(2)}, u32[]{:S(2)}) collective-permute-start(bf16[2,512,128]{2,1,0:T(8,128)(2,1)} %copy-done.23), channel_id=1, source_target_pairs={{0,3},{1,0},{2,1},{3,2},{4,7},{5,4},{6,5},{7,6},{8,11},{9,8},{10,9... | collective-permute-start | bytes 786440 | tf_op jit(solution)/shard_map/ppermute | solution.py:205
  71.9 1.2 collective-permute-start.19
  77.4 1.3 shard_map.22.refs_10_
  78.9 3.8 %shard_map.23 = (f32[2,4,256,128]{3,2,1,0:T(8,128)S(1)}, f32[8,128]{1,0:T(8,128)S(1)}) custom-call(s32[4]{0:T(128)S(1)} %pad_add_fusion.place, bf16[2,512,256]{2,1,0:T(8,128)(2,1)S(1)} %dynamic-slice_bitcast_fusion.refs_0_, bf16[2,512,256]{2,1,0:T(8,128)(2,1)S(1)} %collective-permute-done.refs_1_, bf16[2,512,256]{2,1,0:T(8,128)(2,1)S(1)} %collective-permute-done.1.refs_2_, ...), custom_call_target="tpu_custom_call" | custom-call | flops 2147483648 | bytes 8388608 | tf_op jit(solution)/shard_map/pallas_call | solution.py:144
  82.8 1.3 shard_map.20.refs_10_
  84.9 3.8 %shard_map.25 = (f32[2,4,256,128]{3,2,1,0:T(8,128)S(1)}, f32[8,128]{1,0:T(8,128)S(1)}) custom-call(s32[4]{0:T(128)S(1)} %pad_add_fusion.place, bf16[2,512,256]{2,1,0:T(8,128)(2,1)S(1)} %dynamic-slice_bitcast_fusion.refs_0_, bf16[2,512,256]{2,1,0:T(8,128)(2,1)S(1)} %collective-permute-done.refs_1_, bf16[2,512,256]{2,1,0:T(8,128)(2,1)S(1)} %collective-permute-done.1.refs_2_, ...), custom_call_target="tpu_custom_call" | custom-call | flops 2147483648 | bytes 8388608 | tf_op jit(solution)/shard_map/pallas_call | solution.py:144
  88.8 3.8 %shard_map.24 = (f32[2,4,256,128]{3,2,1,0:T(8,128)S(1)}, f32[8,128]{1,0:T(8,128)S(1)}) custom-call(s32[4]{0:T(128)S(1)} %pad_add_fusion.place, bf16[2,512,256]{2,1,0:T(8,128)(2,1)S(1)} %dynamic-slice_bitcast_fusion.refs_0_, bf16[2,512,256]{2,1,0:T(8,128)(2,1)S(1)} %collective-permute-done.refs_1_, bf16[2,512,256]{2,1,0:T(8,128)(2,1)S(1)} %collective-permute-done.1.refs_2_, ...), custom_call_target="tpu_custom_call" | custom-call | flops 2147483648 | bytes 8388608 | tf_op jit(solution)/shard_map/pallas_call | solution.py:144
  92.6 4.4 %shard_map.26 = f32[32,264,128]{2,1,0:T(8,128)S(1)} custom-call(s32[4]{0:T(128)S(1)} %pad_add_fusion.place, bf16[2,512,256]{2,1,0:T(8,128)(2,1)S(1)} %dynamic-slice_bitcast_fusion.refs_0_, bf16[2,512,256]{2,1,0:T(8,128)(2,1)S(1)} %collective-permute-done.refs_1_, bf16[2,512,256]{2,1,0:T(8,128)(2,1)S(1)} %collective-permute-done.1.refs_2_, ...), custom_call_target="tpu_custom_call" | custom-call | flops 2147483648 | bytes 8388608 | tf_op jit(solution)/shard_map/pallas_call | solution.py:144
  97.3 70.9 %all_to_all.5 = f16[32,264,128]{2,1,0:T(8,128)(2,1)S(1)} all-to-all(f16[32,264,128]{2,1,0:T(8,128)(2,1)S(1)} %convert_element_type.6), channel_id=1, replica_groups=mesh['zh'=2,'y'=4,'core'=2,'zl'=4,'x'=4] {'zh','zl','x'}, dimensions={0} | all-to-all | bytes 4325376 | tf_op jit(solution)/shard_map/all_to_all | solution.py:227
  168.4 1.6 shard_map.27
  (83 shorter events, 17.4 us)
Async XLA Ops:
  2.1 13.7 %collective-permute-start.5 = (bf16[2,512,256]{2,1,0:T(8,128)(2,1)S(1)}, bf16[2,512,256]{2,1,0:T(8,128)(2,1)S(1)}, u32[]{:S(2)}, u32[]{:S(2)}) collective-permute-start(bf16[2,512,256]{2,1,0:T(8,128)(2,1)S(1)} %dynamic-slice_bitcast_fusion.refs_0_), channel_id=1, source_target_pairs={{0,32},{32,64},{64,96},{96,0},{1,33},{33,65},{65,97},{97,1},{2,34}... | collective-permute-start | bytes 1572872 | tf_op jit(solution)/shard_map/ppermute | solution.py:193
  3.5 13.5 %collective-permute-start.4 = (bf16[2,512,256]{2,1,0:T(8,128)(2,1)S(1)}, bf16[2,512,256]{2,1,0:T(8,128)(2,1)}, u32[]{:S(2)}, u32[]{:S(2)}) collective-permute-start(bf16[2,512,256]{2,1,0:T(8,128)(2,1)S(1)} %dynamic-slice_bitcast_fusion.refs_0_), channel_id=1, source_target_pairs={{0,96},{32,0},{64,32},{96,64},{1,97},{33,1},{65,33},{97,65},{2,98}... | collective-permute-start | bytes 1572872 | tf_op jit(solution)/shard_map/ppermute | solution.py:193
  4.2 14.3 %collective-permute-start.1 = (bf16[2,512,256]{2,1,0:T(8,128)(2,1)S(1)}, bf16[2,512,256]{2,1,0:T(8,128)(2,1)S(1)}, u32[]{:S(2)}, u32[]{:S(2)}) collective-permute-start(bf16[2,512,256]{2,1,0:T(8,128)(2,1)S(1)} %dynamic-slice_bitcast_fusion.refs_0_), channel_id=1, source_target_pairs={{0,1},{1,2},{2,3},{3,0},{4,5},{5,6},{6,7},{7,4},{8,9},{9,10},{10,1... | collective-permute-start | bytes 1572872 | tf_op jit(solution)/shard_map/ppermute | solution.py:200
  5.7 12.8 %collective-permute-start = (bf16[2,512,256]{2,1,0:T(8,128)(2,1)S(1)}, bf16[2,512,256]{2,1,0:T(8,128)(2,1)S(1)}, u32[]{:S(2)}, u32[]{:S(2)}) collective-permute-start(bf16[2,512,256]{2,1,0:T(8,128)(2,1)S(1)} %dynamic-slice_bitcast_fusion.refs_0_), channel_id=1, source_target_pairs={{0,3},{1,0},{2,1},{3,2},{4,7},{5,4},{6,5},{7,6},{8,11},{9,8},{10,9... | collective-permute-start | bytes 1572872 | tf_op jit(solution)/shard_map/ppermute | solution.py:200
  7.4 20.6 %collective-permute-start.6 = (bf16[2,512,256]{2,1,0:T(8,128)(2,1)}, bf16[2,512,256]{2,1,0:T(8,128)(2,1)}, u32[]{:S(2)}, u32[]{:S(2)}) collective-permute-start(bf16[2,512,256]{2,1,0:T(8,128)(2,1)} %dynamic-slice_bitcast_fusion.1), channel_id=1, source_target_pairs={{0,128},{128,0},{1,129},{129,1},{2,130},{130,2},{3,131},{131,3},{4... | collective-permute-start | bytes 1572872 | tf_op jit(solution)/shard_map/ppermute | solution.py:190
  21.0 39.3 %copy-start.11 = (bf16[2,512,128]{2,1,0:T(8,128)(2,1)}, bf16[2,512,128]{2,1,0:T(8,128)(2,1)S(1)}, u32[]{:S(2)}) copy-start(bf16[2,512,128]{2,1,0:T(8,128)(2,1)S(1)} %get-tuple-element.35.refs_0_) | copy-start | bytes 786436
  21.0 12.6 %collective-permute-start.7 = (bf16[2,512,128]{2,1,0:T(8,128)(2,1)S(1)}, bf16[2,512,128]{2,1,0:T(8,128)(2,1)S(1)}, u32[]{:S(2)}, u32[]{:S(2)}) collective-permute-start(bf16[2,512,128]{2,1,0:T(8,128)(2,1)S(1)} %get-tuple-element.38), channel_id=1, source_target_pairs={{0,3},{1,0},{2,1},{3,2},{4,7},{5,4},{6,5},{7,6},{8,11},{9,8},{10,9... | collective-permute-start | bytes 786440 | tf_op jit(solution)/shard_map/ppermute | solution.py:205
  24.0 12.9 %collective-permute-start.8 = (bf16[2,512,128]{2,1,0:T(8,128)(2,1)S(1)}, bf16[2,512,128]{2,1,0:T(8,128)(2,1)S(1)}, u32[]{:S(2)}, u32[]{:S(2)}) collective-permute-start(bf16[2,512,128]{2,1,0:T(8,128)(2,1)S(1)} %get-tuple-element.39), channel_id=1, source_target_pairs={{0,1},{1,2},{2,3},{3,0},{4,5},{5,6},{6,7},{7,4},{8,9},{9,10},{10,1... | collective-permute-start | bytes 786440 | tf_op jit(solution)/shard_map/ppermute | solution.py:205
  24.0 13.6 %collective-permute-start.9 = (bf16[2,512,128]{2,1,0:T(8,128)(2,1)S(1)}, bf16[2,512,128]{2,1,0:T(8,128)(2,1)S(1)}, u32[]{:S(2)}, u32[]{:S(2)}) collective-permute-start(bf16[2,512,128]{2,1,0:T(8,128)(2,1)S(1)} %get-tuple-element.40), channel_id=1, source_target_pairs={{0,2},{1,3},{2,0},{3,1},{4,6},{5,7},{6,4},{7,5},{8,10},{9,11},{10,... | collective-permute-start | bytes 786440 | tf_op jit(solution)/shard_map/ppermute | solution.py:205
  38.3 15.6 %collective-permute-start.11 = (bf16[2,512,256]{2,1,0:T(8,128)(2,1)}, bf16[2,512,256]{2,1,0:T(8,128)(2,1)S(1)}, u32[]{:S(2)}, u32[]{:S(2)}) collective-permute-start(bf16[2,512,256]{2,1,0:T(8,128)(2,1)} %collective-permute-done.6.refs_0_.refs_5_), channel_id=1, source_target_pairs={{0,1},{1,2},{2,3},{3,0},{4,5},{5,6},{6,7},{7,4},{8,9},{9,10},{10,1... | collective-permute-start | bytes 1572872 | tf_op jit(solution)/shard_map/ppermute | solution.py:200
  38.3 16.1 %collective-permute-start.10 = (bf16[2,512,256]{2,1,0:T(8,128)(2,1)}, bf16[2,512,256]{2,1,0:T(8,128)(2,1)S(1)}, u32[]{:S(2)}, u32[]{:S(2)}) collective-permute-start(bf16[2,512,256]{2,1,0:T(8,128)(2,1)} %collective-permute-done.6.refs_0_.refs_5_), channel_id=1, source_target_pairs={{0,3},{1,0},{2,1},{3,2},{4,7},{5,4},{6,5},{7,6},{8,11},{9,8},{10,9... | collective-permute-start | bytes 1572872 | tf_op jit(solution)/shard_map/ppermute | solution.py:200
  41.6 21.9 %collective-permute-start.15 = (bf16[2,512,256]{2,1,0:T(8,128)(2,1)}, bf16[2,512,256]{2,1,0:T(8,128)(2,1)S(1)}, u32[]{:S(2)}, u32[]{:S(2)}) collective-permute-start(bf16[2,512,256]{2,1,0:T(8,128)(2,1)} %collective-permute-done.6.refs_0_.refs_5_), channel_id=1, source_target_pairs={{0,32},{32,64},{64,96},{96,0},{1,33},{33,65},{65,97},{97,1},{2,34}... | collective-permute-start | bytes 1572872 | tf_op jit(solution)/shard_map/ppermute | solution.py:193
  42.8 20.6 %collective-permute-start.14 = (bf16[2,512,256]{2,1,0:T(8,128)(2,1)}, bf16[2,512,256]{2,1,0:T(8,128)(2,1)S(1)}, u32[]{:S(2)}, u32[]{:S(2)}) collective-permute-start(bf16[2,512,256]{2,1,0:T(8,128)(2,1)} %collective-permute-done.6.refs_0_.refs_5_), channel_id=1, source_target_pairs={{0,96},{32,0},{64,32},{96,64},{1,97},{33,1},{65,33},{97,65},{2,98}... | collective-permute-start | bytes 1572872 | tf_op jit(solution)/shard_map/ppermute | solution.py:193
  43.6 13.1 %collective-permute-start.3 = (bf16[2,256,256]{2,1,0:T(8,128)(2,1)S(1)}, bf16[2,256,256]{2,1,0:T(8,128)(2,1)S(1)}, u32[]{:S(2)}, u32[]{:S(2)}) collective-permute-start(bf16[2,256,256]{2,1,0:T(8,128)(2,1)S(1)} %slice.17), channel_id=1, source_target_pairs={{0,1},{1,2},{2,3},{3,0},{4,5},{5,6},{6,7},{7,4},{8,9},{9,10},{10,1... | collective-permute-start | bytes 786440 | tf_op jit(solution)/shard_map/ppermute | solution.py:207
  53.9 6.4 %collective-permute-start.2 = (bf16[2,256,256]{2,1,0:T(8,128)(2,1)S(1)}, bf16[2,256,256]{2,1,0:T(8,128)(2,1)S(1)}, u32[]{:S(2)}, u32[]{:S(2)}) collective-permute-start(bf16[2,256,256]{2,1,0:T(8,128)(2,1)S(1)} %slice.16), channel_id=1, source_target_pairs={{0,3},{1,0},{2,1},{3,2},{4,7},{5,4},{6,5},{7,6},{8,11},{9,8},{10,9... | collective-permute-start | bytes 786440 | tf_op jit(solution)/shard_map/ppermute | solution.py:206
  54.4 12.6 %copy-start.1 = (bf16[2,512,256]{2,1,0:T(8,128)(2,1)}, bf16[2,512,256]{2,1,0:T(8,128)(2,1)S(1)}, u32[]{:S(2)}) copy-start(bf16[2,512,256]{2,1,0:T(8,128)(2,1)S(1)} %collective-permute-done.10.refs_1_.refs_6_) | copy-start | bytes 1572868
  54.4 10.1 %collective-permute-start.13 = (bf16[2,256,256]{2,1,0:T(8,128)(2,1)S(1)}, bf16[2,256,256]{2,1,0:T(8,128)(2,1)S(1)}, u32[]{:S(2)}, u32[]{:S(2)}) collective-permute-start(bf16[2,256,256]{2,1,0:T(8,128)(2,1)S(1)} %slice.19), channel_id=1, source_target_pairs={{0,1},{1,2},{2,3},{3,0},{4,5},{5,6},{6,7},{7,4},{8,9},{9,10},{10,1... | collective-permute-start | bytes 786440 | tf_op jit(solution)/shard_map/ppermute | solution.py:207
  56.7 7.8 %collective-permute-start.12 = (bf16[2,256,256]{2,1,0:T(8,128)(2,1)S(1)}, bf16[2,256,256]{2,1,0:T(8,128)(2,1)S(1)}, u32[]{:S(2)}, u32[]{:S(2)}) collective-permute-start(bf16[2,256,256]{2,1,0:T(8,128)(2,1)S(1)} %slice.18), channel_id=1, source_target_pairs={{0,3},{1,0},{2,1},{3,2},{4,7},{5,4},{6,5},{7,6},{8,11},{9,8},{10,9... | collective-permute-start | bytes 786440 | tf_op jit(solution)/shard_map/ppermute | solution.py:206
  62.0 11.6 %collective-permute-start.20 = (bf16[2048,128]{1,0:T(8,128)(2,1)}, bf16[2048,128]{1,0:T(8,128)(2,1)}, u32[]{:S(2)}, u32[]{:S(2)}) collective-permute-start(bf16[2048,128]{1,0:T(8,128)(2,1)} %shard_map.21.here), channel_id=1, source_target_pairs={{0,64},{32,96},{64,0},{96,32},{1,65},{33,97},{65,1},{97,33},{2,66}... | collective-permute-start | bytes 1572872 | tf_op jit(solution)/shard_map/ppermute | solution.py:193
  64.5 2.5 %copy-start.22 = (bf16[2,512,128]{2,1,0:T(8,128)(2,1)}, bf16[2,512,128]{2,1,0:T(8,128)(2,1)S(1)}, u32[]{:S(2)}) copy-start(bf16[2,512,128]{2,1,0:T(8,128)(2,1)S(1)} %get-tuple-element.48) | copy-start | bytes 786436
  64.5 2.5 %copy-start.23 = (bf16[2,512,128]{2,1,0:T(8,128)(2,1)}, bf16[2,512,128]{2,1,0:T(8,128)(2,1)S(1)}, u32[]{:S(2)}) copy-start(bf16[2,512,128]{2,1,0:T(8,128)(2,1)S(1)} %get-tuple-element.47) | copy-start | bytes 786436
  67.7 15.1 %collective-permute-start.16 = (bf16[2048,128]{1,0:T(8,128)(2,1)}, bf16[2048,128]{1,0:T(8,128)(2,1)}, u32[]{:S(2)}, u32[]{:S(2)}) collective-permute-start(bf16[2048,128]{1,0:T(8,128)(2,1)} %shard_map.19.here), channel_id=1, source_target_pairs={{0,64},{32,96},{64,0},{96,32},{1,65},{33,97},{65,1},{97,33},{2,66}... | collective-permute-start | bytes 1572872 | tf_op jit(solution)/shard_map/ppermute | solution.py:193
  69.8 9.1 %copy-start.2 = (bf16[2,512,256]{2,1,0:T(8,128)(2,1)S(1)}, bf16[2,512,256]{2,1,0:T(8,128)(2,1)}, u32[]{:S(2)}) copy-start(bf16[2,512,256]{2,1,0:T(8,128)(2,1)} %copy-done.1) | copy-start | bytes 1572868
  69.8 9.1 %copy-start.4 = (bf16[2,256,256]{2,1,0:T(8,128)(2,1)S(1)}, bf16[2,256,256]{2,1,0:T(8,128)(2,1)}, u32[]{:S(2)}) copy-start(bf16[2,256,256]{2,1,0:T(8,128)(2,1)} %copy-done.3) | copy-start | bytes 786436
  69.8 9.1 %copy-start.6 = (bf16[2,256,256]{2,1,0:T(8,128)(2,1)S(1)}, bf16[2,256,256]{2,1,0:T(8,128)(2,1)}, u32[]{:S(2)}) copy-start(bf16[2,256,256]{2,1,0:T(8,128)(2,1)} %copy-done.5) | copy-start | bytes 786436
  69.8 9.1 %copy-start.8 = (bf16[2,256,256]{2,1,0:T(8,128)(2,1)S(1)}, bf16[2,256,256]{2,1,0:T(8,128)(2,1)}, u32[]{:S(2)}) copy-start(bf16[2,256,256]{2,1,0:T(8,128)(2,1)} %copy-done.7) | copy-start | bytes 786436
  69.8 12.9 %collective-permute-start.17 = (bf16[2,512,128]{2,1,0:T(8,128)(2,1)}, bf16[2,512,128]{2,1,0:T(8,128)(2,1)S(1)}, u32[]{:S(2)}, u32[]{:S(2)}) collective-permute-start(bf16[2,512,128]{2,1,0:T(8,128)(2,1)} %copy-done.23), channel_id=1, source_target_pairs={{0,3},{1,0},{2,1},{3,2},{4,7},{5,4},{6,5},{7,6},{8,11},{9,8},{10,9... | collective-permute-start | bytes 786440 | tf_op jit(solution)/shard_map/ppermute | solution.py:205
  71.5 11.2 %collective-permute-start.18 = (bf16[2,512,128]{2,1,0:T(8,128)(2,1)}, bf16[2,512,128]{2,1,0:T(8,128)(2,1)S(1)}, u32[]{:S(2)}, u32[]{:S(2)}) collective-permute-start(bf16[2,512,128]{2,1,0:T(8,128)(2,1)} %copy-done.22), channel_id=1, source_target_pairs={{0,1},{1,2},{2,3},{3,0},{4,5},{5,6},{6,7},{7,4},{8,9},{9,10},{10,1... | collective-permute-start | bytes 786440 | tf_op jit(solution)/shard_map/ppermute | solution.py:205
  71.9 10.9 %collective-permute-start.19 = (bf16[2,512,128]{2,1,0:T(8,128)(2,1)}, bf16[2,512,128]{2,1,0:T(8,128)(2,1)S(1)}, u32[]{:S(2)}, u32[]{:S(2)}) collective-permute-start(bf16[2,512,128]{2,1,0:T(8,128)(2,1)} %copy-done.21), channel_id=1, source_target_pairs={{0,2},{1,3},{2,0},{3,1},{4,6},{5,7},{6,4},{7,5},{8,10},{9,11},{10,... | collective-permute-start | bytes 786440 | tf_op jit(solution)/shard_map/ppermute | solution.py:205
  78.8 4.0 %copy-start.20 = (bf16[2,512,128]{2,1,0:T(8,128)(2,1)S(1)}, bf16[2,512,128]{2,1,0:T(8,128)(2,1)}, u32[]{:S(2)}) copy-start(bf16[2,512,128]{2,1,0:T(8,128)(2,1)} %copy-done.19) | copy-start | bytes 786436
  78.8 10.0 %collective-permute-start.22 = (bf16[4,2048,128]{2,1,0:T(8,128)(2,1)S(1)}, bf16[4,2048,128]{2,1,0:T(8,128)(2,1)S(1)}, u32[]{:S(2)}, u32[]{:S(2)}) collective-permute-start(bf16[4,2048,128]{2,1,0:T(8,128)(2,1)S(1)} %shard_map.22.refs_10_), channel_id=1, source_target_pairs={{0,16},{16,0},{1,17},{17,1},{2,18},{18,2},{3,19},{19,3},{4,20},{20... | collective-permute-start | bytes 6291464 | tf_op jit(solution)/shard_map/ppermute | solution.py:196
  84.2 8.5 %collective-permute-start.21 = (bf16[4,2048,128]{2,1,0:T(8,128)(2,1)S(1)}, bf16[4,2048,128]{2,1,0:T(8,128)(2,1)S(1)}, u32[]{:S(2)}, u32[]{:S(2)}) collective-permute-start(bf16[4,2048,128]{2,1,0:T(8,128)(2,1)S(1)} %shard_map.20.refs_10_), channel_id=1, source_target_pairs={{0,16},{16,0},{1,17},{17,1},{2,18},{18,2},{3,19},{19,3},{4,20},{20... | collective-permute-start | bytes 6291464 | tf_op jit(solution)/shard_map/ppermute | solution.py:196
  (15 other events, 16.1 us)

commit v8 on v7

--- a/solution.py
+++ b/solution.py
@@ -29,14 +29,14 @@
     top[...] = jnp.zeros_like(top)
     for dy in (0, 2):
         for e, pieces in enumerate(blocks):
-            real = imag = 0.0
+            both = 0.0
             start = 0
             for piece in pieces:
                 here = slice(start, start + piece.shape[1])
                 start = here.stop
                 weights = jnp.concatenate([cols[dy, here], cols[dy + 1, here]], axis=1)
-                real += across(piece[0], weights)
-                imag += across(piece[1], weights)
+                both += across(jnp.concatenate([piece[0], piece[1]], axis=1), weights)
+            real, imag = both[:n], both[n:]
             turned = jnp.concatenate([pltpu.roll(imag[:, :c], c // 2, 1), pltpu.roll(imag[:, c:], c // 2, 1)], axis=1)
             term = real + jnp.where(first, turned, -turned)
             for i in range(2):

time: 171 us -> 171 us (level)
  no operation moved by 1% of the time
where the time goes in v8:
time: 171 us; the launch traced here: 170 us
  blocking collectives  70.9 us (41%)
  starting transfers between devices  34 us (20%)
  waiting for transfers between devices  26.8 us (16%)
  Pallas kernels  25 us (15%)
  local copies, waits for them, and re-layouts  12.1 us (7%)
    all_to_all x1, blocking collectives, body(): got = lax.all_to_all(sent, ('zh', 'zl', 'x'), 0, 0, tiled=True)  70.9 us
    pallas_call x4, Pallas kernels, terms_of(): pl.pallas_call(kernel, out_shape=shapes, in_specs=[SCALAR] + [SPACE] * (l...  15.5 us
    ppermute x4, waiting for transfers between devices, gathered(): above, below = (lax.ppermute(block, 'x', ring(4, step)) for step in (-1, 1))  11.7 us
    unnamed x48, local copies, waits for them, and re-layouts  11.1 us
    pallas_call x7, Pallas kernels, small_call(): pl.pallas_call(kernel, out_shape=shapes, in_specs=[SCALAR] * scalars + [S...  9.51 us
    ppermute x6, waiting for transfers between devices, gathered(): lax.ppermute(part, 'x', ring(4, step))  8.22 us
    ppermute x6, starting transfers between devices, gathered(): lax.ppermute(part, 'x', ring(4, step))  8.08 us
    ppermute x6, starting transfers between devices, from_y(): return lax.ppermute(block, 'y', ring(4, -step))  7.66 us
  transfers between devices with their start and end apart: 23, of which 10 were waited for; matrix products, arithmetic and copies ran while one was open for 0% of the time, Pallas kernels for 11%

profile of v8, /device:TPU:16, one launch (start us, length us, event | category | flops | bytes accessed | tf_op | source)
XLA Modules:
  0.0 169.7 jit_solution(4602040304598920120)
XLA Ops:
  0.0 1.2 copy-done
  2.1 1.4 collective-permute-start.5
  4.2 1.5 collective-permute-start.1
  5.7 1.7 %collective-permute-start = (bf16[2,512,256]{2,1,0:T(8,128)(2,1)S(1)}, bf16[2,512,256]{2,1,0:T(8,128)(2,1)S(1)}, u32[]{:S(2)}, u32[]{:S(2)}) collective-permute-start(bf16[2,512,256]{2,1,0:T(8,128)(2,1)S(1)} %dynamic-slice_bitcast_fusion.refs_0_), channel_id=1, source_target_pairs={{0,3},{1,0},{2,1},{3,2},{4,7},{5,4},{6,5},{7,6},{8,11},{9,8},{10,9... | collective-permute-start | bytes 1572872 | tf_op jit(solution)/shard_map/ppermute | solution.py:200
  7.4 7.2 %collective-permute-start.6 = (bf16[2,512,256]{2,1,0:T(8,128)(2,1)}, bf16[2,512,256]{2,1,0:T(8,128)(2,1)}, u32[]{:S(2)}, u32[]{:S(2)}) collective-permute-start(bf16[2,512,256]{2,1,0:T(8,128)(2,1)} %dynamic-slice_bitcast_fusion.1), channel_id=1, source_target_pairs={{0,128},{128,0},{1,129},{129,1},{2,130},{130,2},{3,131},{131,3},{4... | collective-permute-start | bytes 1572872 | tf_op jit(solution)/shard_map/ppermute | solution.py:190
  14.6 1.2 collective-permute-done.5.below
  16.9 1.6 collective-permute-done.1.refs_2_
  19.6 1.4 shard_map.17
  21.0 3.0 %collective-permute-start.7 = (bf16[2,512,128]{2,1,0:T(8,128)(2,1)S(1)}, bf16[2,512,128]{2,1,0:T(8,128)(2,1)S(1)}, u32[]{:S(2)}, u32[]{:S(2)}) collective-permute-start(bf16[2,512,128]{2,1,0:T(8,128)(2,1)S(1)} %get-tuple-element.38), channel_id=1, source_target_pairs={{0,3},{1,0},{2,1},{3,2},{4,7},{5,4},{6,5},{7,6},{8,11},{9,8},{10,9... | collective-permute-start | bytes 786440 | tf_op jit(solution)/shard_map/ppermute | solution.py:205
  24.0 1.8 %collective-permute-start.9 = (bf16[2,512,128]{2,1,0:T(8,128)(2,1)S(1)}, bf16[2,512,128]{2,1,0:T(8,128)(2,1)S(1)}, u32[]{:S(2)}, u32[]{:S(2)}) collective-permute-start(bf16[2,512,128]{2,1,0:T(8,128)(2,1)S(1)} %get-tuple-element.40), channel_id=1, source_target_pairs={{0,2},{1,3},{2,0},{3,1},{4,6},{5,7},{6,4},{7,5},{8,10},{9,11},{10,... | collective-permute-start | bytes 786440 | tf_op jit(solution)/shard_map/ppermute | solution.py:205
  25.8 2.2 %collective-permute-done.6.refs_0_.refs_5_ = bf16[2,512,256]{2,1,0:T(8,128)(2,1)} collective-permute-done((bf16[2,512,256]{2,1,0:T(8,128)(2,1)}, bf16[2,512,256]{2,1,0:T(8,128)(2,1)}, u32[]{:S(2)}, u32[]{:S(2)}) %collective-permute-start.6) | collective-permute-done | bytes 524320 | tf_op jit(solution)/shard_map/ppermute | solution.py:190
  28.0 5.5 %collective-permute-done.7.refs_1_ = bf16[2,512,128]{2,1,0:T(8,128)(2,1)S(1)} collective-permute-done((bf16[2,512,128]{2,1,0:T(8,128)(2,1)S(1)}, bf16[2,512,128]{2,1,0:T(8,128)(2,1)S(1)}, u32[]{:S(2)}, u32[]{:S(2)}) %collective-permute-start.7) | collective-permute-done | bytes 262176 | tf_op jit(solution)/shard_map/ppermute | solution.py:205
  34.2 2.7 %collective-permute-done.8.refs_2_ = bf16[2,512,128]{2,1,0:T(8,128)(2,1)S(1)} collective-permute-done((bf16[2,512,128]{2,1,0:T(8,128)(2,1)S(1)}, bf16[2,512,128]{2,1,0:T(8,128)(2,1)S(1)}, u32[]{:S(2)}, u32[]{:S(2)}) %collective-permute-start.8) | collective-permute-done | bytes 262176 | tf_op jit(solution)/shard_map/ppermute | solution.py:205
  38.3 3.2 %collective-permute-start.10 = (bf16[2,512,256]{2,1,0:T(8,128)(2,1)}, bf16[2,512,256]{2,1,0:T(8,128)(2,1)S(1)}, u32[]{:S(2)}, u32[]{:S(2)}) collective-permute-start(bf16[2,512,256]{2,1,0:T(8,128)(2,1)} %collective-permute-done.6.refs_0_.refs_5_), channel_id=1, source_target_pairs={{0,3},{1,0},{2,1},{3,2},{4,7},{5,4},{6,5},{7,6},{8,11},{9,8},{10,9... | collective-permute-start | bytes 1572872 | tf_op jit(solution)/shard_map/ppermute | solution.py:200
  41.6 1.3 collective-permute-start.15
  43.7 10.2 %collective-permute-done.11.refs_2_.refs_7_ = bf16[2,512,256]{2,1,0:T(8,128)(2,1)S(1)} collective-permute-done((bf16[2,512,256]{2,1,0:T(8,128)(2,1)}, bf16[2,512,256]{2,1,0:T(8,128)(2,1)S(1)}, u32[]{:S(2)}, u32[]{:S(2)}) %collective-permute-start.11) | collective-permute-done | bytes 524320 | tf_op jit(solution)/shard_map/ppermute | solution.py:200
  54.4 1.8 %collective-permute-start.13 = (bf16[2,256,256]{2,1,0:T(8,128)(2,1)S(1)}, bf16[2,256,256]{2,1,0:T(8,128)(2,1)S(1)}, u32[]{:S(2)}, u32[]{:S(2)}) collective-permute-start(bf16[2,256,256]{2,1,0:T(8,128)(2,1)S(1)} %slice.19), channel_id=1, source_target_pairs={{0,1},{1,2},{2,3},{3,0},{4,5},{5,6},{6,7},{7,4},{8,9},{9,10},{10,1... | collective-permute-start | bytes 786440 | tf_op jit(solution)/shard_map/ppermute | solution.py:207
  56.7 1.3 collective-permute-start.12
  58.0 2.2 %collective-permute-done.2.refs_3_ = bf16[2,256,256]{2,1,0:T(8,128)(2,1)S(1)} collective-permute-done((bf16[2,256,256]{2,1,0:T(8,128)(2,1)S(1)}, bf16[2,256,256]{2,1,0:T(8,128)(2,1)S(1)}, u32[]{:S(2)}, u32[]{:S(2)}) %collective-permute-start.2) | collective-permute-done | bytes 262176 | tf_op jit(solution)/shard_map/ppermute | solution.py:206
  62.0 1.5 collective-permute-start.20
  64.6 2.4 %shard_map.19.here = bf16[2048,128]{1,0:T(8,128)(2,1)} custom-call(s32[1]{0:T(128)} %bitcast.3.x, bf16[2,512,256]{2,1,0:T(8,128)(2,1)} %collective-permute-done.6.refs_0_.refs_5_, bf16[2,512,256]{2,1,0:T(8,128)(2,1)S(1)} %collective-permute-done.10.refs_1_.refs_6_, bf16[2,512,256]{2,1,0:T(8,128)(2,1)S(1)} %collective-permute-done.11.refs_2_.refs_7_, ...), custom_call_target="tpu_custom_call" | custom-call | bytes 2097152 | tf_op jit(solution)/shard_map/pallas_call | solution.py:94
  67.7 2.1 %collective-permute-start.16 = (bf16[2048,128]{1,0:T(8,128)(2,1)}, bf16[2048,128]{1,0:T(8,128)(2,1)}, u32[]{:S(2)}, u32[]{:S(2)}) collective-permute-start(bf16[2048,128]{1,0:T(8,128)(2,1)} %shard_map.19.here), channel_id=1, source_target_pairs={{0,64},{32,96},{64,0},{96,32},{1,65},{33,97},{65,1},{97,33},{2,66}... | collective-permute-start | bytes 1572872 | tf_op jit(solution)/shard_map/ppermute | solution.py:193
  69.8 1.7 %collective-permute-start.17 = (bf16[2,512,128]{2,1,0:T(8,128)(2,1)}, bf16[2,512,128]{2,1,0:T(8,128)(2,1)S(1)}, u32[]{:S(2)}, u32[]{:S(2)}) collective-permute-start(bf16[2,512,128]{2,1,0:T(8,128)(2,1)} %copy-done.23), channel_id=1, source_target_pairs={{0,3},{1,0},{2,1},{3,2},{4,7},{5,4},{6,5},{7,6},{8,11},{9,8},{10,9... | collective-permute-start | bytes 786440 | tf_op jit(solution)/shard_map/ppermute | solution.py:205
  71.9 1.2 collective-permute-start.19
  77.4 1.3 shard_map.22.refs_10_
  78.9 3.7 %shard_map.23 = (f32[2,4,256,128]{3,2,1,0:T(8,128)S(1)}, f32[8,128]{1,0:T(8,128)S(1)}) custom-call(s32[4]{0:T(128)S(1)} %pad_add_fusion.place, bf16[2,512,256]{2,1,0:T(8,128)(2,1)S(1)} %dynamic-slice_bitcast_fusion.refs_0_, bf16[2,512,256]{2,1,0:T(8,128)(2,1)S(1)} %collective-permute-done.refs_1_, bf16[2,512,256]{2,1,0:T(8,128)(2,1)S(1)} %collective-permute-done.1.refs_2_, ...), custom_call_target="tpu_custom_call" | custom-call | flops 2147483648 | bytes 8388608 | tf_op jit(solution)/shard_map/pallas_call | solution.py:144
  82.7 1.3 shard_map.20.refs_10_
  84.8 3.7 %shard_map.25 = (f32[2,4,256,128]{3,2,1,0:T(8,128)S(1)}, f32[8,128]{1,0:T(8,128)S(1)}) custom-call(s32[4]{0:T(128)S(1)} %pad_add_fusion.place, bf16[2,512,256]{2,1,0:T(8,128)(2,1)S(1)} %dynamic-slice_bitcast_fusion.refs_0_, bf16[2,512,256]{2,1,0:T(8,128)(2,1)S(1)} %collective-permute-done.refs_1_, bf16[2,512,256]{2,1,0:T(8,128)(2,1)S(1)} %collective-permute-done.1.refs_2_, ...), custom_call_target="tpu_custom_call" | custom-call | flops 2147483648 | bytes 8388608 | tf_op jit(solution)/shard_map/pallas_call | solution.py:144
  88.6 3.7 %shard_map.24 = (f32[2,4,256,128]{3,2,1,0:T(8,128)S(1)}, f32[8,128]{1,0:T(8,128)S(1)}) custom-call(s32[4]{0:T(128)S(1)} %pad_add_fusion.place, bf16[2,512,256]{2,1,0:T(8,128)(2,1)S(1)} %dynamic-slice_bitcast_fusion.refs_0_, bf16[2,512,256]{2,1,0:T(8,128)(2,1)S(1)} %collective-permute-done.refs_1_, bf16[2,512,256]{2,1,0:T(8,128)(2,1)S(1)} %collective-permute-done.1.refs_2_, ...), custom_call_target="tpu_custom_call" | custom-call | flops 2147483648 | bytes 8388608 | tf_op jit(solution)/shard_map/pallas_call | solution.py:144
  92.3 4.3 %shard_map.26 = f32[32,264,128]{2,1,0:T(8,128)S(1)} custom-call(s32[4]{0:T(128)S(1)} %pad_add_fusion.place, bf16[2,512,256]{2,1,0:T(8,128)(2,1)S(1)} %dynamic-slice_bitcast_fusion.refs_0_, bf16[2,512,256]{2,1,0:T(8,128)(2,1)S(1)} %collective-permute-done.refs_1_, bf16[2,512,256]{2,1,0:T(8,128)(2,1)S(1)} %collective-permute-done.1.refs_2_, ...), custom_call_target="tpu_custom_call" | custom-call | flops 2147483648 | bytes 8388608 | tf_op jit(solution)/shard_map/pallas_call | solution.py:144
  96.9 70.9 %all_to_all.5 = f16[32,264,128]{2,1,0:T(8,128)(2,1)S(1)} all-to-all(f16[32,264,128]{2,1,0:T(8,128)(2,1)S(1)} %convert_element_type.6), channel_id=1, replica_groups=mesh['zh'=2,'y'=4,'core'=2,'zl'=4,'x'=4] {'zh','zl','x'}, dimensions={0} | all-to-all | bytes 4325376 | tf_op jit(solution)/shard_map/all_to_all | solution.py:227
  168.1 1.6 shard_map.27
  (83 shorter events, 17.4 us)
Async XLA Ops:
  2.1 13.7 %collective-permute-start.5 = (bf16[2,512,256]{2,1,0:T(8,128)(2,1)S(1)}, bf16[2,512,256]{2,1,0:T(8,128)(2,1)S(1)}, u32[]{:S(2)}, u32[]{:S(2)}) collective-permute-start(bf16[2,512,256]{2,1,0:T(8,128)(2,1)S(1)} %dynamic-slice_bitcast_fusion.refs_0_), channel_id=1, source_target_pairs={{0,32},{32,64},{64,96},{96,0},{1,33},{33,65},{65,97},{97,1},{2,34}... | collective-permute-start | bytes 1572872 | tf_op jit(solution)/shard_map/ppermute | solution.py:193
  3.5 13.5 %collective-permute-start.4 = (bf16[2,512,256]{2,1,0:T(8,128)(2,1)S(1)}, bf16[2,512,256]{2,1,0:T(8,128)(2,1)}, u32[]{:S(2)}, u32[]{:S(2)}) collective-permute-start(bf16[2,512,256]{2,1,0:T(8,128)(2,1)S(1)} %dynamic-slice_bitcast_fusion.refs_0_), channel_id=1, source_target_pairs={{0,96},{32,0},{64,32},{96,64},{1,97},{33,1},{65,33},{97,65},{2,98}... | collective-permute-start | bytes 1572872 | tf_op jit(solution)/shard_map/ppermute | solution.py:193
  4.2 14.3 %collective-permute-start.1 = (bf16[2,512,256]{2,1,0:T(8,128)(2,1)S(1)}, bf16[2,512,256]{2,1,0:T(8,128)(2,1)S(1)}, u32[]{:S(2)}, u32[]{:S(2)}) collective-permute-start(bf16[2,512,256]{2,1,0:T(8,128)(2,1)S(1)} %dynamic-slice_bitcast_fusion.refs_0_), channel_id=1, source_target_pairs={{0,1},{1,2},{2,3},{3,0},{4,5},{5,6},{6,7},{7,4},{8,9},{9,10},{10,1... | collective-permute-start | bytes 1572872 | tf_op jit(solution)/shard_map/ppermute | solution.py:200
  5.7 12.8 %collective-permute-start = (bf16[2,512,256]{2,1,0:T(8,128)(2,1)S(1)}, bf16[2,512,256]{2,1,0:T(8,128)(2,1)S(1)}, u32[]{:S(2)}, u32[]{:S(2)}) collective-permute-start(bf16[2,512,256]{2,1,0:T(8,128)(2,1)S(1)} %dynamic-slice_bitcast_fusion.refs_0_), channel_id=1, source_target_pairs={{0,3},{1,0},{2,1},{3,2},{4,7},{5,4},{6,5},{7,6},{8,11},{9,8},{10,9... | collective-permute-start | bytes 1572872 | tf_op jit(solution)/shard_map/ppermute | solution.py:200
  7.4 20.6 %collective-permute-start.6 = (bf16[2,512,256]{2,1,0:T(8,128)(2,1)}, bf16[2,512,256]{2,1,0:T(8,128)(2,1)}, u32[]{:S(2)}, u32[]{:S(2)}) collective-permute-start(bf16[2,512,256]{2,1,0:T(8,128)(2,1)} %dynamic-slice_bitcast_fusion.1), channel_id=1, source_target_pairs={{0,128},{128,0},{1,129},{129,1},{2,130},{130,2},{3,131},{131,3},{4... | collective-permute-start | bytes 1572872 | tf_op jit(solution)/shard_map/ppermute | solution.py:190
  21.0 39.3 %copy-start.11 = (bf16[2,512,128]{2,1,0:T(8,128)(2,1)}, bf16[2,512,128]{2,1,0:T(8,128)(2,1)S(1)}, u32[]{:S(2)}) copy-start(bf16[2,512,128]{2,1,0:T(8,128)(2,1)S(1)} %get-tuple-element.35.refs_0_) | copy-start | bytes 786436
  21.0 12.6 %collective-permute-start.7 = (bf16[2,512,128]{2,1,0:T(8,128)(2,1)S(1)}, bf16[2,512,128]{2,1,0:T(8,128)(2,1)S(1)}, u32[]{:S(2)}, u32[]{:S(2)}) collective-permute-start(bf16[2,512,128]{2,1,0:T(8,128)(2,1)S(1)} %get-tuple-element.38), channel_id=1, source_target_pairs={{0,3},{1,0},{2,1},{3,2},{4,7},{5,4},{6,5},{7,6},{8,11},{9,8},{10,9... | collective-permute-start | bytes 786440 | tf_op jit(solution)/shard_map/ppermute | solution.py:205
  24.0 12.9 %collective-permute-start.8 = (bf16[2,512,128]{2,1,0:T(8,128)(2,1)S(1)}, bf16[2,512,128]{2,1,0:T(8,128)(2,1)S(1)}, u32[]{:S(2)}, u32[]{:S(2)}) collective-permute-start(bf16[2,512,128]{2,1,0:T(8,128)(2,1)S(1)} %get-tuple-element.39), channel_id=1, source_target_pairs={{0,1},{1,2},{2,3},{3,0},{4,5},{5,6},{6,7},{7,4},{8,9},{9,10},{10,1... | collective-permute-start | bytes 786440 | tf_op jit(solution)/shard_map/ppermute | solution.py:205
  24.0 13.6 %collective-permute-start.9 = (bf16[2,512,128]{2,1,0:T(8,128)(2,1)S(1)}, bf16[2,512,128]{2,1,0:T(8,128)(2,1)S(1)}, u32[]{:S(2)}, u32[]{:S(2)}) collective-permute-start(bf16[2,512,128]{2,1,0:T(8,128)(2,1)S(1)} %get-tuple-element.40), channel_id=1, source_target_pairs={{0,2},{1,3},{2,0},{3,1},{4,6},{5,7},{6,4},{7,5},{8,10},{9,11},{10,... | collective-permute-start | bytes 786440 | tf_op jit(solution)/shard_map/ppermute | solution.py:205
  38.3 15.6 %collective-permute-start.11 = (bf16[2,512,256]{2,1,0:T(8,128)(2,1)}, bf16[2,512,256]{2,1,0:T(8,128)(2,1)S(1)}, u32[]{:S(2)}, u32[]{:S(2)}) collective-permute-start(bf16[2,512,256]{2,1,0:T(8,128)(2,1)} %collective-permute-done.6.refs_0_.refs_5_), channel_id=1, source_target_pairs={{0,1},{1,2},{2,3},{3,0},{4,5},{5,6},{6,7},{7,4},{8,9},{9,10},{10,1... | collective-permute-start | bytes 1572872 | tf_op jit(solution)/shard_map/ppermute | solution.py:200
  38.3 16.1 %collective-permute-start.10 = (bf16[2,512,256]{2,1,0:T(8,128)(2,1)}, bf16[2,512,256]{2,1,0:T(8,128)(2,1)S(1)}, u32[]{:S(2)}, u32[]{:S(2)}) collective-permute-start(bf16[2,512,256]{2,1,0:T(8,128)(2,1)} %collective-permute-done.6.refs_0_.refs_5_), channel_id=1, source_target_pairs={{0,3},{1,0},{2,1},{3,2},{4,7},{5,4},{6,5},{7,6},{8,11},{9,8},{10,9... | collective-permute-start | bytes 1572872 | tf_op jit(solution)/shard_map/ppermute | solution.py:200
  41.6 21.9 %collective-permute-start.15 = (bf16[2,512,256]{2,1,0:T(8,128)(2,1)}, bf16[2,512,256]{2,1,0:T(8,128)(2,1)S(1)}, u32[]{:S(2)}, u32[]{:S(2)}) collective-permute-start(bf16[2,512,256]{2,1,0:T(8,128)(2,1)} %collective-permute-done.6.refs_0_.refs_5_), channel_id=1, source_target_pairs={{0,32},{32,64},{64,96},{96,0},{1,33},{33,65},{65,97},{97,1},{2,34}... | collective-permute-start | bytes 1572872 | tf_op jit(solution)/shard_map/ppermute | solution.py:193
  42.8 20.6 %collective-permute-start.14 = (bf16[2,512,256]{2,1,0:T(8,128)(2,1)}, bf16[2,512,256]{2,1,0:T(8,128)(2,1)S(1)}, u32[]{:S(2)}, u32[]{:S(2)}) collective-permute-start(bf16[2,512,256]{2,1,0:T(8,128)(2,1)} %collective-permute-done.6.refs_0_.refs_5_), channel_id=1, source_target_pairs={{0,96},{32,0},{64,32},{96,64},{1,97},{33,1},{65,33},{97,65},{2,98}... | collective-permute-start | bytes 1572872 | tf_op jit(solution)/shard_map/ppermute | solution.py:193
  43.6 13.1 %collective-permute-start.3 = (bf16[2,256,256]{2,1,0:T(8,128)(2,1)S(1)}, bf16[2,256,256]{2,1,0:T(8,128)(2,1)S(1)}, u32[]{:S(2)}, u32[]{:S(2)}) collective-permute-start(bf16[2,256,256]{2,1,0:T(8,128)(2,1)S(1)} %slice.17), channel_id=1, source_target_pairs={{0,1},{1,2},{2,3},{3,0},{4,5},{5,6},{6,7},{7,4},{8,9},{9,10},{10,1... | collective-permute-start | bytes 786440 | tf_op jit(solution)/shard_map/ppermute | solution.py:207
  53.9 6.4 %collective-permute-start.2 = (bf16[2,256,256]{2,1,0:T(8,128)(2,1)S(1)}, bf16[2,256,256]{2,1,0:T(8,128)(2,1)S(1)}, u32[]{:S(2)}, u32[]{:S(2)}) collective-permute-start(bf16[2,256,256]{2,1,0:T(8,128)(2,1)S(1)} %slice.16), channel_id=1, source_target_pairs={{0,3},{1,0},{2,1},{3,2},{4,7},{5,4},{6,5},{7,6},{8,11},{9,8},{10,9... | collective-permute-start | bytes 786440 | tf_op jit(solution)/shard_map/ppermute | solution.py:206
  54.4 12.6 %copy-start.1 = (bf16[2,512,256]{2,1,0:T(8,128)(2,1)}, bf16[2,512,256]{2,1,0:T(8,128)(2,1)S(1)}, u32[]{:S(2)}) copy-start(bf16[2,512,256]{2,1,0:T(8,128)(2,1)S(1)} %collective-permute-done.10.refs_1_.refs_6_) | copy-start | bytes 1572868
  54.4 10.1 %collective-permute-start.13 = (bf16[2,256,256]{2,1,0:T(8,128)(2,1)S(1)}, bf16[2,256,256]{2,1,0:T(8,128)(2,1)S(1)}, u32[]{:S(2)}, u32[]{:S(2)}) collective-permute-start(bf16[2,256,256]{2,1,0:T(8,128)(2,1)S(1)} %slice.19), channel_id=1, source_target_pairs={{0,1},{1,2},{2,3},{3,0},{4,5},{5,6},{6,7},{7,4},{8,9},{9,10},{10,1... | collective-permute-start | bytes 786440 | tf_op jit(solution)/shard_map/ppermute | solution.py:207
  56.7 7.8 %collective-permute-start.12 = (bf16[2,256,256]{2,1,0:T(8,128)(2,1)S(1)}, bf16[2,256,256]{2,1,0:T(8,128)(2,1)S(1)}, u32[]{:S(2)}, u32[]{:S(2)}) collective-permute-start(bf16[2,256,256]{2,1,0:T(8,128)(2,1)S(1)} %slice.18), channel_id=1, source_target_pairs={{0,3},{1,0},{2,1},{3,2},{4,7},{5,4},{6,5},{7,6},{8,11},{9,8},{10,9... | collective-permute-start | bytes 786440 | tf_op jit(solution)/shard_map/ppermute | solution.py:206
  62.0 11.6 %collective-permute-start.20 = (bf16[2048,128]{1,0:T(8,128)(2,1)}, bf16[2048,128]{1,0:T(8,128)(2,1)}, u32[]{:S(2)}, u32[]{:S(2)}) collective-permute-start(bf16[2048,128]{1,0:T(8,128)(2,1)} %shard_map.21.here), channel_id=1, source_target_pairs={{0,64},{32,96},{64,0},{96,32},{1,65},{33,97},{65,1},{97,33},{2,66}... | collective-permute-start | bytes 1572872 | tf_op jit(solution)/shard_map/ppermute | solution.py:193
  64.5 2.5 %copy-start.22 = (bf16[2,512,128]{2,1,0:T(8,128)(2,1)}, bf16[2,512,128]{2,1,0:T(8,128)(2,1)S(1)}, u32[]{:S(2)}) copy-start(bf16[2,512,128]{2,1,0:T(8,128)(2,1)S(1)} %get-tuple-element.48) | copy-start | bytes 786436
  64.5 2.5 %copy-start.23 = (bf16[2,512,128]{2,1,0:T(8,128)(2,1)}, bf16[2,512,128]{2,1,0:T(8,128)(2,1)S(1)}, u32[]{:S(2)}) copy-start(bf16[2,512,128]{2,1,0:T(8,128)(2,1)S(1)} %get-tuple-element.47) | copy-start | bytes 786436
  67.7 15.0 %collective-permute-start.16 = (bf16[2048,128]{1,0:T(8,128)(2,1)}, bf16[2048,128]{1,0:T(8,128)(2,1)}, u32[]{:S(2)}, u32[]{:S(2)}) collective-permute-start(bf16[2048,128]{1,0:T(8,128)(2,1)} %shard_map.19.here), channel_id=1, source_target_pairs={{0,64},{32,96},{64,0},{96,32},{1,65},{33,97},{65,1},{97,33},{2,66}... | collective-permute-start | bytes 1572872 | tf_op jit(solution)/shard_map/ppermute | solution.py:193
  69.8 9.1 %copy-start.2 = (bf16[2,512,256]{2,1,0:T(8,128)(2,1)S(1)}, bf16[2,512,256]{2,1,0:T(8,128)(2,1)}, u32[]{:S(2)}) copy-start(bf16[2,512,256]{2,1,0:T(8,128)(2,1)} %copy-done.1) | copy-start | bytes 1572868
  69.8 9.1 %copy-start.4 = (bf16[2,256,256]{2,1,0:T(8,128)(2,1)S(1)}, bf16[2,256,256]{2,1,0:T(8,128)(2,1)}, u32[]{:S(2)}) copy-start(bf16[2,256,256]{2,1,0:T(8,128)(2,1)} %copy-done.3) | copy-start | bytes 786436
  69.8 9.1 %copy-start.6 = (bf16[2,256,256]{2,1,0:T(8,128)(2,1)S(1)}, bf16[2,256,256]{2,1,0:T(8,128)(2,1)}, u32[]{:S(2)}) copy-start(bf16[2,256,256]{2,1,0:T(8,128)(2,1)} %copy-done.5) | copy-start | bytes 786436
  69.8 9.1 %copy-start.8 = (bf16[2,256,256]{2,1,0:T(8,128)(2,1)S(1)}, bf16[2,256,256]{2,1,0:T(8,128)(2,1)}, u32[]{:S(2)}) copy-start(bf16[2,256,256]{2,1,0:T(8,128)(2,1)} %copy-done.7) | copy-start | bytes 786436
  69.8 12.8 %collective-permute-start.17 = (bf16[2,512,128]{2,1,0:T(8,128)(2,1)}, bf16[2,512,128]{2,1,0:T(8,128)(2,1)S(1)}, u32[]{:S(2)}, u32[]{:S(2)}) collective-permute-start(bf16[2,512,128]{2,1,0:T(8,128)(2,1)} %copy-done.23), channel_id=1, source_target_pairs={{0,3},{1,0},{2,1},{3,2},{4,7},{5,4},{6,5},{7,6},{8,11},{9,8},{10,9... | collective-permute-start | bytes 786440 | tf_op jit(solution)/shard_map/ppermute | solution.py:205
  71.5 11.1 %collective-permute-start.18 = (bf16[2,512,128]{2,1,0:T(8,128)(2,1)}, bf16[2,512,128]{2,1,0:T(8,128)(2,1)S(1)}, u32[]{:S(2)}, u32[]{:S(2)}) collective-permute-start(bf16[2,512,128]{2,1,0:T(8,128)(2,1)} %copy-done.22), channel_id=1, source_target_pairs={{0,1},{1,2},{2,3},{3,0},{4,5},{5,6},{6,7},{7,4},{8,9},{9,10},{10,1... | collective-permute-start | bytes 786440 | tf_op jit(solution)/shard_map/ppermute | solution.py:205
  71.9 10.8 %collective-permute-start.19 = (bf16[2,512,128]{2,1,0:T(8,128)(2,1)}, bf16[2,512,128]{2,1,0:T(8,128)(2,1)S(1)}, u32[]{:S(2)}, u32[]{:S(2)}) collective-permute-start(bf16[2,512,128]{2,1,0:T(8,128)(2,1)} %copy-done.21), channel_id=1, source_target_pairs={{0,2},{1,3},{2,0},{3,1},{4,6},{5,7},{6,4},{7,5},{8,10},{9,11},{10,... | collective-permute-start | bytes 786440 | tf_op jit(solution)/shard_map/ppermute | solution.py:205
  78.8 3.9 %copy-start.20 = (bf16[2,512,128]{2,1,0:T(8,128)(2,1)S(1)}, bf16[2,512,128]{2,1,0:T(8,128)(2,1)}, u32[]{:S(2)}) copy-start(bf16[2,512,128]{2,1,0:T(8,128)(2,1)} %copy-done.19) | copy-start | bytes 786436
  78.8 9.8 %collective-permute-start.22 = (bf16[4,2048,128]{2,1,0:T(8,128)(2,1)S(1)}, bf16[4,2048,128]{2,1,0:T(8,128)(2,1)S(1)}, u32[]{:S(2)}, u32[]{:S(2)}) collective-permute-start(bf16[4,2048,128]{2,1,0:T(8,128)(2,1)S(1)} %shard_map.22.refs_10_), channel_id=1, source_target_pairs={{0,16},{16,0},{1,17},{17,1},{2,18},{18,2},{3,19},{19,3},{4,20},{20... | collective-permute-start | bytes 6291464 | tf_op jit(solution)/shard_map/ppermute | solution.py:196
  84.1 8.2 %collective-permute-start.21 = (bf16[4,2048,128]{2,1,0:T(8,128)(2,1)S(1)}, bf16[4,2048,128]{2,1,0:T(8,128)(2,1)S(1)}, u32[]{:S(2)}, u32[]{:S(2)}) collective-permute-start(bf16[4,2048,128]{2,1,0:T(8,128)(2,1)S(1)} %shard_map.20.refs_10_), channel_id=1, source_target_pairs={{0,16},{16,0},{1,17},{17,1},{2,18},{18,2},{3,19},{19,3},{4,20},{20... | collective-permute-start | bytes 6291464 | tf_op jit(solution)/shard_map/ppermute | solution.py:196
  (15 other events, 16.1 us)
